TPU v7x, 512 devices: a whole 4x4x16 slice. The times are simulated.
512 devices in a mesh: band: 16 (over z), fft: 16 (over x, y), pool: 2 (over core).
Axes of the slice: x: 4, y: 4, z: 16, core: 2. Of those that a mesh axis runs over, the one named last changes fastest.
Arguments:
- orbitals: float32 [32, 64, 4096], P('band', 'fft'), may hold values from -5 to 5
- kernel: float32 [64, 4096], P(None, 'fft'), may hold values from 0.05 to 2, as said below
Outputs:
- exchange_field: float32 [32, 64, 4096], P('band', 'fft')
Inputs may be any that keep to these rules, and one draw needn't show every extreme that they name: kernel is even: its value at (kx, ky, kz) equals its value at ((64 - kx) % 64, (64 - ky) % 64, (64 - kz) % 64), with 64, 64, 64 the grid sizes.
All inputs are finite; a program needn't handle non-finite values.
Results may differ from a plain program's by a relative error of at most 0.000054.
Values sent between devices are 32-bit elements; how exact they have to be, the bound alone decides.
No kernel may reach another device: no remote copies, remote signals or barrier semaphores. Data moves between devices by JAX's collectives and lax.ppermute only.
A program may use at most 64 MiB of HBM per device.

v0:
```python
import math

import jax
import jax.numpy as jnp
from jax import lax
from jax.sharding import PartitionSpec as P

NX = 64
NY = 64
NZ = 64


highest = lax.Precision.HIGHEST


def from_behind(value, axis, steps):
    count = lax.axis_size(axis)
    pairs = [(source, (source + steps) % count) for source in range(count)]
    return lax.ppermute(value, axis, pairs)


def tables(length):
    index = jnp.arange(length, dtype=jnp.int32)
    product = index[:, None] * index[None, :] % length
    angles = 2.0 * math.pi / length * product.astype(jnp.float32)
    return (jnp.cos(angles), jnp.sin(angles))


def along_axis(values, cosine, sines, pattern, inverse):
    width = values.shape[-1] // 2
    swapped = jnp.concatenate([values[..., width:], -values[..., :width]], axis=-1)
    direct = jnp.einsum(pattern, cosine, values, precision=highest)
    crossed = jnp.einsum(pattern, sines, swapped, precision=highest)
    if inverse:
        return direct - crossed
    return direct + crossed


def local(orbitals, kernel):
    bands_dev, slab_x, plane = orbitals.shape
    pool_count = lax.axis_size("pool")
    half_rows = bands_dev // pool_count
    pool_at = lax.axis_index("pool")
    grid_cells = NX * NY * NZ
    cos_x, sin_x = tables(NX)
    cos_y, sin_y = tables(NY)
    cos_z, sin_z = tables(NZ)
    real_forward = jnp.concatenate([cos_z, -sin_z], axis=1)
    real_inverse = jnp.concatenate([cos_z, -sin_z], axis=0)
    coulomb = kernel.reshape(NX, -1, NZ)
    coulomb = jnp.concatenate([coulomb, coulomb], axis=-1)[None]

    def pencil_work(pencils):
        spectra = along_axis(pencils, cos_x, sin_x, "xk,ikyz->ixyz", False) * coulomb
        spectra = along_axis(spectra, cos_x, sin_x, "xk,ikyz->ixyz", True)
        return lax.all_to_all(spectra, "fft", split_axis=1, concat_axis=2, tiled=True)

    def step_terms(partner):
        density = orbitals[:, None] * partner[None]
        pair_count = bands_dev * partner.shape[0]
        density = density.reshape(pair_count, slab_x, NY, NZ)
        spectra = jnp.matmul(density, real_forward, precision=highest)
        spectra = along_axis(spectra, cos_y, sin_y, "yk,ixkz->ixyz", False)
        returned = pencil_work(
            lax.all_to_all(spectra, "fft", split_axis=2, concat_axis=1, tiled=True)
        )
        returned = along_axis(returned, cos_y, sin_y, "yk,ixkz->ixyz", True)
        potential = jnp.matmul(returned, real_inverse, precision=highest)
        potential = potential.reshape(bands_dev, partner.shape[0], slab_x, plane) * (
            1.0 / grid_cells
        )
        mine = -jnp.sum(potential * partner[None], axis=1)
        theirs = -jnp.sum(potential * orbitals[:, None], axis=0)
        return (mine, theirs)

    def advance(slab):
        moved = from_behind(slab, "band", 1)
        return (moved, lax.dynamic_slice_in_dim(moved, pool_at * half_rows, half_rows, 0))

    cycle_length = lax.axis_size("band")
    own_half = lax.dynamic_slice_in_dim(orbitals, pool_at * half_rows, half_rows, 0)
    own_terms = step_terms(own_half)[0]

    def cycle_ordered(cycle_step, current):
        slab, chosen = advance(current[0])
        return (slab, current[1] + step_terms(chosen)[0])

    field = lax.fori_loop(1, cycle_length, cycle_ordered, (orbitals, own_terms))[1]
    return lax.psum(field, "pool")


def solution(mesh):
    return jax.shard_map(
        local,
        mesh=mesh,
        in_specs=(P("band", "fft", None), P(None, "fft")),
        out_specs=P("band", "fft", None),
        check_vma=False,
    )
```

profile of v0, /device:TPU:1, one launch (start us, length us, event | category | flops | bytes accessed | tf_op | source)
XLA Modules:
  0.0 691.0 jit_solution(1252343993322173479)
XLA Ops:
  11.2 7.7 %all-to-all-start.2 = ((f32[2,4,64,128]{3,1,0,2:T(4,128)}), f32[2,4,64,128]{3,1,0,2:T(4,128)S(1)}, u32[]{:S(2)}, u32[]{:S(2)}) async-start(f32[2,4,64,128]{3,1,0,2:T(4,128)} %copy.19), calls=%async_computation.2 | async-start | bytes 524288 | tf_op jit(solution)/shard_map/all_to_all | solution.py:65
  42.5 544.3 %while.17 = (s32[]{:T(128)}, f32[2,4,4096]{2,1,0:T(4,128)S(1)}, f32[2,4,4096]{2,1,0:T(4,128)S(1)}, f32[2,4,4096]{2,1,0:T(4,128)S(1)}, s32[]{:T(128)}, /*index=5*...) while((s32[]{:T(128)}, f32[2,4,4096]{2,1,0:T(4,128)S(1)}, ...), condition=%wide.region_1.2_spmd.clone.clone, body=%wide.region_0.1_spmd.clone.clone.sunk | while | flops 504643584 | bytes 14155945 | solution.py:88
  46.3 9.7 %collective-permute-done = f32[2,4,4096]{2,1,0:T(4,128)S(1)} collective-permute-done((f32[2,4,4096]{2,1,0:T(4,128)S(1)}, f32[2,4,4096]{2,1,0:T(4,128)S(1)}, u32[]{:S(2)}, u32[]{:S(2)}) %collective-permute-start) | collective-permute-done | bytes 131104 | tf_op jit(solution)/shard_map/while/body/eval_jaxpr/ppermute | solution.py:19
  58.0 10.8 %all_to_all.108 = f32[2,4,64,128]{3,1,0,2:T(4,128)S(1)} all-to-all(f32[2,4,64,128]{3,1,0,2:T(4,128)S(1)} %copy.40), channel_id=1, replica_groups=mesh['band'=16,'fft'=16,'pool'=2] {'fft'}, dimensions={2} | all-to-all | bytes 524288 | tf_op jit(solution)/shard_map/while/body/eval_jaxpr/all_to_all | solution.py:65
  75.7 7.3 %all-to-all-done.1 = f32[2,64,4,128]{3,2,0,1:T(4,128)S(1)} async-done(((f32[2,64,4,128]{3,2,0,1:T(4,128)}), f32[2,64,4,128]{3,2,0,1:T(4,128)S(1)}, u32[]{:S(2)}, u32[]{:S(2)}) %all-to-all-start.1) | async-done | bytes 262176 | tf_op jit(solution)/shard_map/while/body/eval_jaxpr/all_to_all | solution.py:56
  93.8 10.5 %all_to_all.108 = f32[2,4,64,128]{3,1,0,2:T(4,128)S(1)} all-to-all(f32[2,4,64,128]{3,1,0,2:T(4,128)S(1)} %copy.40), channel_id=1, replica_groups=mesh['band'=16,'fft'=16,'pool'=2] {'fft'}, dimensions={2} | all-to-all | bytes 524288 | tf_op jit(solution)/shard_map/while/body/eval_jaxpr/all_to_all | solution.py:65
  111.3 7.3 %all-to-all-done.1 = f32[2,64,4,128]{3,2,0,1:T(4,128)S(1)} async-done(((f32[2,64,4,128]{3,2,0,1:T(4,128)}), f32[2,64,4,128]{3,2,0,1:T(4,128)S(1)}, u32[]{:S(2)}, u32[]{:S(2)}) %all-to-all-start.1) | async-done | bytes 262176 | tf_op jit(solution)/shard_map/while/body/eval_jaxpr/all_to_all | solution.py:56
  129.6 10.5 %all_to_all.108 = f32[2,4,64,128]{3,1,0,2:T(4,128)S(1)} all-to-all(f32[2,4,64,128]{3,1,0,2:T(4,128)S(1)} %copy.40), channel_id=1, replica_groups=mesh['band'=16,'fft'=16,'pool'=2] {'fft'}, dimensions={2} | all-to-all | bytes 524288 | tf_op jit(solution)/shard_map/while/body/eval_jaxpr/all_to_all | solution.py:65
  165.1 10.5 %all_to_all.108 = f32[2,4,64,128]{3,1,0,2:T(4,128)S(1)} all-to-all(f32[2,4,64,128]{3,1,0,2:T(4,128)S(1)} %copy.40), channel_id=1, replica_groups=mesh['band'=16,'fft'=16,'pool'=2] {'fft'}, dimensions={2} | all-to-all | bytes 524288 | tf_op jit(solution)/shard_map/while/body/eval_jaxpr/all_to_all | solution.py:65
  182.6 7.4 %all-to-all-done.1 = f32[2,64,4,128]{3,2,0,1:T(4,128)S(1)} async-done(((f32[2,64,4,128]{3,2,0,1:T(4,128)}), f32[2,64,4,128]{3,2,0,1:T(4,128)S(1)}, u32[]{:S(2)}, u32[]{:S(2)}) %all-to-all-start.1) | async-done | bytes 262176 | tf_op jit(solution)/shard_map/while/body/eval_jaxpr/all_to_all | solution.py:56
  200.7 10.7 %all_to_all.108 = f32[2,4,64,128]{3,1,0,2:T(4,128)S(1)} all-to-all(f32[2,4,64,128]{3,1,0,2:T(4,128)S(1)} %copy.40), channel_id=1, replica_groups=mesh['band'=16,'fft'=16,'pool'=2] {'fft'}, dimensions={2} | all-to-all | bytes 524288 | tf_op jit(solution)/shard_map/while/body/eval_jaxpr/all_to_all | solution.py:65
  218.4 7.3 %all-to-all-done.1 = f32[2,64,4,128]{3,2,0,1:T(4,128)S(1)} async-done(((f32[2,64,4,128]{3,2,0,1:T(4,128)}), f32[2,64,4,128]{3,2,0,1:T(4,128)S(1)}, u32[]{:S(2)}, u32[]{:S(2)}) %all-to-all-start.1) | async-done | bytes 262176 | tf_op jit(solution)/shard_map/while/body/eval_jaxpr/all_to_all | solution.py:56
  236.4 11.4 %all_to_all.108 = f32[2,4,64,128]{3,1,0,2:T(4,128)S(1)} all-to-all(f32[2,4,64,128]{3,1,0,2:T(4,128)S(1)} %copy.40), channel_id=1, replica_groups=mesh['band'=16,'fft'=16,'pool'=2] {'fft'}, dimensions={2} | all-to-all | bytes 524288 | tf_op jit(solution)/shard_map/while/body/eval_jaxpr/all_to_all | solution.py:65
  254.8 7.3 %all-to-all-done.1 = f32[2,64,4,128]{3,2,0,1:T(4,128)S(1)} async-done(((f32[2,64,4,128]{3,2,0,1:T(4,128)}), f32[2,64,4,128]{3,2,0,1:T(4,128)S(1)}, u32[]{:S(2)}, u32[]{:S(2)}) %all-to-all-start.1) | async-done | bytes 262176 | tf_op jit(solution)/shard_map/while/body/eval_jaxpr/all_to_all | solution.py:56
  273.1 10.3 %all_to_all.108 = f32[2,4,64,128]{3,1,0,2:T(4,128)S(1)} all-to-all(f32[2,4,64,128]{3,1,0,2:T(4,128)S(1)} %copy.40), channel_id=1, replica_groups=mesh['band'=16,'fft'=16,'pool'=2] {'fft'}, dimensions={2} | all-to-all | bytes 524288 | tf_op jit(solution)/shard_map/while/body/eval_jaxpr/all_to_all | solution.py:65
  290.4 7.3 %all-to-all-done.1 = f32[2,64,4,128]{3,2,0,1:T(4,128)S(1)} async-done(((f32[2,64,4,128]{3,2,0,1:T(4,128)}), f32[2,64,4,128]{3,2,0,1:T(4,128)S(1)}, u32[]{:S(2)}, u32[]{:S(2)}) %all-to-all-start.1) | async-done | bytes 262176 | tf_op jit(solution)/shard_map/while/body/eval_jaxpr/all_to_all | solution.py:56
  308.4 10.5 %all_to_all.108 = f32[2,4,64,128]{3,1,0,2:T(4,128)S(1)} all-to-all(f32[2,4,64,128]{3,1,0,2:T(4,128)S(1)} %copy.40), channel_id=1, replica_groups=mesh['band'=16,'fft'=16,'pool'=2] {'fft'}, dimensions={2} | all-to-all | bytes 524288 | tf_op jit(solution)/shard_map/while/body/eval_jaxpr/all_to_all | solution.py:65
  325.9 7.3 %all-to-all-done.1 = f32[2,64,4,128]{3,2,0,1:T(4,128)S(1)} async-done(((f32[2,64,4,128]{3,2,0,1:T(4,128)}), f32[2,64,4,128]{3,2,0,1:T(4,128)S(1)}, u32[]{:S(2)}, u32[]{:S(2)}) %all-to-all-start.1) | async-done | bytes 262176 | tf_op jit(solution)/shard_map/while/body/eval_jaxpr/all_to_all | solution.py:56
  343.9 10.5 %all_to_all.108 = f32[2,4,64,128]{3,1,0,2:T(4,128)S(1)} all-to-all(f32[2,4,64,128]{3,1,0,2:T(4,128)S(1)} %copy.40), channel_id=1, replica_groups=mesh['band'=16,'fft'=16,'pool'=2] {'fft'}, dimensions={2} | all-to-all | bytes 524288 | tf_op jit(solution)/shard_map/while/body/eval_jaxpr/all_to_all | solution.py:65
  361.4 7.3 %all-to-all-done.1 = f32[2,64,4,128]{3,2,0,1:T(4,128)S(1)} async-done(((f32[2,64,4,128]{3,2,0,1:T(4,128)}), f32[2,64,4,128]{3,2,0,1:T(4,128)S(1)}, u32[]{:S(2)}, u32[]{:S(2)}) %all-to-all-start.1) | async-done | bytes 262176 | tf_op jit(solution)/shard_map/while/body/eval_jaxpr/all_to_all | solution.py:56
  379.5 11.4 %all_to_all.108 = f32[2,4,64,128]{3,1,0,2:T(4,128)S(1)} all-to-all(f32[2,4,64,128]{3,1,0,2:T(4,128)S(1)} %copy.40), channel_id=1, replica_groups=mesh['band'=16,'fft'=16,'pool'=2] {'fft'}, dimensions={2} | all-to-all | bytes 524288 | tf_op jit(solution)/shard_map/while/body/eval_jaxpr/all_to_all | solution.py:65
  397.8 7.7 %all-to-all-done.1 = f32[2,64,4,128]{3,2,0,1:T(4,128)S(1)} async-done(((f32[2,64,4,128]{3,2,0,1:T(4,128)}), f32[2,64,4,128]{3,2,0,1:T(4,128)S(1)}, u32[]{:S(2)}, u32[]{:S(2)}) %all-to-all-start.1) | async-done | bytes 262176 | tf_op jit(solution)/shard_map/while/body/eval_jaxpr/all_to_all | solution.py:56
  416.3 11.0 %all_to_all.108 = f32[2,4,64,128]{3,1,0,2:T(4,128)S(1)} all-to-all(f32[2,4,64,128]{3,1,0,2:T(4,128)S(1)} %copy.40), channel_id=1, replica_groups=mesh['band'=16,'fft'=16,'pool'=2] {'fft'}, dimensions={2} | all-to-all | bytes 524288 | tf_op jit(solution)/shard_map/while/body/eval_jaxpr/all_to_all | solution.py:65
  434.3 7.3 %all-to-all-done.1 = f32[2,64,4,128]{3,2,0,1:T(4,128)S(1)} async-done(((f32[2,64,4,128]{3,2,0,1:T(4,128)}), f32[2,64,4,128]{3,2,0,1:T(4,128)S(1)}, u32[]{:S(2)}, u32[]{:S(2)}) %all-to-all-start.1) | async-done | bytes 262176 | tf_op jit(solution)/shard_map/while/body/eval_jaxpr/all_to_all | solution.py:56
  452.3 10.5 %all_to_all.108 = f32[2,4,64,128]{3,1,0,2:T(4,128)S(1)} all-to-all(f32[2,4,64,128]{3,1,0,2:T(4,128)S(1)} %copy.40), channel_id=1, replica_groups=mesh['band'=16,'fft'=16,'pool'=2] {'fft'}, dimensions={2} | all-to-all | bytes 524288 | tf_op jit(solution)/shard_map/while/body/eval_jaxpr/all_to_all | solution.py:65
  469.8 7.3 %all-to-all-done.1 = f32[2,64,4,128]{3,2,0,1:T(4,128)S(1)} async-done(((f32[2,64,4,128]{3,2,0,1:T(4,128)}), f32[2,64,4,128]{3,2,0,1:T(4,128)S(1)}, u32[]{:S(2)}, u32[]{:S(2)}) %all-to-all-start.1) | async-done | bytes 262176 | tf_op jit(solution)/shard_map/while/body/eval_jaxpr/all_to_all | solution.py:56
  487.8 10.5 %all_to_all.108 = f32[2,4,64,128]{3,1,0,2:T(4,128)S(1)} all-to-all(f32[2,4,64,128]{3,1,0,2:T(4,128)S(1)} %copy.40), channel_id=1, replica_groups=mesh['band'=16,'fft'=16,'pool'=2] {'fft'}, dimensions={2} | all-to-all | bytes 524288 | tf_op jit(solution)/shard_map/while/body/eval_jaxpr/all_to_all | solution.py:65
  505.3 7.3 %all-to-all-done.1 = f32[2,64,4,128]{3,2,0,1:T(4,128)S(1)} async-done(((f32[2,64,4,128]{3,2,0,1:T(4,128)}), f32[2,64,4,128]{3,2,0,1:T(4,128)S(1)}, u32[]{:S(2)}, u32[]{:S(2)}) %all-to-all-start.1) | async-done | bytes 262176 | tf_op jit(solution)/shard_map/while/body/eval_jaxpr/all_to_all | solution.py:56
  523.7 10.2 %all_to_all.108 = f32[2,4,64,128]{3,1,0,2:T(4,128)S(1)} all-to-all(f32[2,4,64,128]{3,1,0,2:T(4,128)S(1)} %copy.40), channel_id=1, replica_groups=mesh['band'=16,'fft'=16,'pool'=2] {'fft'}, dimensions={2} | all-to-all | bytes 524288 | tf_op jit(solution)/shard_map/while/body/eval_jaxpr/all_to_all | solution.py:65
  541.0 8.0 %all-to-all-done.1 = f32[2,64,4,128]{3,2,0,1:T(4,128)S(1)} async-done(((f32[2,64,4,128]{3,2,0,1:T(4,128)}), f32[2,64,4,128]{3,2,0,1:T(4,128)S(1)}, u32[]{:S(2)}, u32[]{:S(2)}) %all-to-all-start.1) | async-done | bytes 262176 | tf_op jit(solution)/shard_map/while/body/eval_jaxpr/all_to_all | solution.py:56
  559.8 10.9 %all_to_all.108 = f32[2,4,64,128]{3,1,0,2:T(4,128)S(1)} all-to-all(f32[2,4,64,128]{3,1,0,2:T(4,128)S(1)} %copy.40), channel_id=1, replica_groups=mesh['band'=16,'fft'=16,'pool'=2] {'fft'}, dimensions={2} | all-to-all | bytes 524288 | tf_op jit(solution)/shard_map/while/body/eval_jaxpr/all_to_all | solution.py:65
  587.5 95.0 %all-reduce.2.cloned.1.call-done = f32[2,4,4096]{2,1,0:T(4,128)} async-done(((f32[2,4,4096]{2,1,0:T(4,128)}), f32[2,4,4096]{2,1,0:T(4,128)}) %all-reduce.2.cloned.1.call-update) | async-done | bytes 131088 | tf_op jit(solution)/shard_map/psum | solution.py:89
  (467 shorter events, 306.1 us)
Async XLA Ops:
  11.2 15.1 %all-to-all-start.2 = ((f32[2,4,64,128]{3,1,0,2:T(4,128)}), f32[2,4,64,128]{3,1,0,2:T(4,128)S(1)}, u32[]{:S(2)}, u32[]{:S(2)}) async-start(f32[2,4,64,128]{3,1,0,2:T(4,128)} %copy.19), calls=%async_computation.2 | async-start | bytes 524288 | tf_op jit(solution)/shard_map/all_to_all | solution.py:65
  29.7 10.9 %all-to-all-start.3 = ((f32[2,64,4,128]{3,2,0,1:T(4,128)}), f32[2,64,4,128]{3,2,0,1:T(4,128)S(1)}, u32[]{:S(2)}, u32[]{:S(2)}) async-start(f32[2,64,4,128]{3,2,0,1:T(4,128)} %copy.22), calls=%async_computation.3 | async-start | bytes 524288 | tf_op jit(solution)/shard_map/all_to_all | solution.py:56
  33.4 649.2 %all-reduce.2.cloned.1.call-start = ((), (), s32[]{:S(2)}) async-start(), calls=%async_computation.4 | async-start | bytes 262144 | tf_op jit(solution)/shard_map/psum | solution.py:89
  42.5 13.5 %collective-permute-start = (f32[2,4,4096]{2,1,0:T(4,128)S(1)}, f32[2,4,4096]{2,1,0:T(4,128)S(1)}, u32[]{:S(2)}, u32[]{:S(2)}) collective-permute-start(f32[2,4,4096]{2,1,0:T(4,128)S(1)} %get-tuple-element.366), channel_id=1, source_target_pairs={{0,32},{32,64},{64,96},{96,128},{128,160},{160,192},{192,224},{224... | collective-permute-start | bytes 393224 | tf_op jit(solution)/shard_map/while/body/eval_jaxpr/ppermute | solution.py:19
  72.2 10.8 %all-to-all-start.1 = ((f32[2,64,4,128]{3,2,0,1:T(4,128)}), f32[2,64,4,128]{3,2,0,1:T(4,128)S(1)}, u32[]{:S(2)}, u32[]{:S(2)}) async-start(f32[2,64,4,128]{3,2,0,1:T(4,128)} %copy.42), calls=%async_computation.1 | async-start | bytes 524288 | tf_op jit(solution)/shard_map/while/body/eval_jaxpr/all_to_all | solution.py:56
  84.9 6.9 %collective-permute-start = (f32[2,4,4096]{2,1,0:T(4,128)S(1)}, f32[2,4,4096]{2,1,0:T(4,128)S(1)}, u32[]{:S(2)}, u32[]{:S(2)}) collective-permute-start(f32[2,4,4096]{2,1,0:T(4,128)S(1)} %get-tuple-element.366), channel_id=1, source_target_pairs={{0,32},{32,64},{64,96},{96,128},{128,160},{160,192},{192,224},{224... | collective-permute-start | bytes 393224 | tf_op jit(solution)/shard_map/while/body/eval_jaxpr/ppermute | solution.py:19
  107.7 10.8 %all-to-all-start.1 = ((f32[2,64,4,128]{3,2,0,1:T(4,128)}), f32[2,64,4,128]{3,2,0,1:T(4,128)S(1)}, u32[]{:S(2)}, u32[]{:S(2)}) async-start(f32[2,64,4,128]{3,2,0,1:T(4,128)} %copy.42), calls=%async_computation.1 | async-start | bytes 524288 | tf_op jit(solution)/shard_map/while/body/eval_jaxpr/all_to_all | solution.py:56
  120.4 7.2 %collective-permute-start = (f32[2,4,4096]{2,1,0:T(4,128)S(1)}, f32[2,4,4096]{2,1,0:T(4,128)S(1)}, u32[]{:S(2)}, u32[]{:S(2)}) collective-permute-start(f32[2,4,4096]{2,1,0:T(4,128)S(1)} %get-tuple-element.366), channel_id=1, source_target_pairs={{0,32},{32,64},{64,96},{96,128},{128,160},{160,192},{192,224},{224... | collective-permute-start | bytes 393224 | tf_op jit(solution)/shard_map/while/body/eval_jaxpr/ppermute | solution.py:19
  143.5 10.8 %all-to-all-start.1 = ((f32[2,64,4,128]{3,2,0,1:T(4,128)}), f32[2,64,4,128]{3,2,0,1:T(4,128)S(1)}, u32[]{:S(2)}, u32[]{:S(2)}) async-start(f32[2,64,4,128]{3,2,0,1:T(4,128)} %copy.42), calls=%async_computation.1 | async-start | bytes 524288 | tf_op jit(solution)/shard_map/while/body/eval_jaxpr/all_to_all | solution.py:56
  156.2 6.9 %collective-permute-start = (f32[2,4,4096]{2,1,0:T(4,128)S(1)}, f32[2,4,4096]{2,1,0:T(4,128)S(1)}, u32[]{:S(2)}, u32[]{:S(2)}) collective-permute-start(f32[2,4,4096]{2,1,0:T(4,128)S(1)} %get-tuple-element.366), channel_id=1, source_target_pairs={{0,32},{32,64},{64,96},{96,128},{128,160},{160,192},{192,224},{224... | collective-permute-start | bytes 393224 | tf_op jit(solution)/shard_map/while/body/eval_jaxpr/ppermute | solution.py:19
  179.0 10.9 %all-to-all-start.1 = ((f32[2,64,4,128]{3,2,0,1:T(4,128)}), f32[2,64,4,128]{3,2,0,1:T(4,128)S(1)}, u32[]{:S(2)}, u32[]{:S(2)}) async-start(f32[2,64,4,128]{3,2,0,1:T(4,128)} %copy.42), calls=%async_computation.1 | async-start | bytes 524288 | tf_op jit(solution)/shard_map/while/body/eval_jaxpr/all_to_all | solution.py:56
  191.9 6.9 %collective-permute-start = (f32[2,4,4096]{2,1,0:T(4,128)S(1)}, f32[2,4,4096]{2,1,0:T(4,128)S(1)}, u32[]{:S(2)}, u32[]{:S(2)}) collective-permute-start(f32[2,4,4096]{2,1,0:T(4,128)S(1)} %get-tuple-element.366), channel_id=1, source_target_pairs={{0,32},{32,64},{64,96},{96,128},{128,160},{160,192},{192,224},{224... | collective-permute-start | bytes 393224 | tf_op jit(solution)/shard_map/while/body/eval_jaxpr/ppermute | solution.py:19
  214.8 10.8 %all-to-all-start.1 = ((f32[2,64,4,128]{3,2,0,1:T(4,128)}), f32[2,64,4,128]{3,2,0,1:T(4,128)S(1)}, u32[]{:S(2)}, u32[]{:S(2)}) async-start(f32[2,64,4,128]{3,2,0,1:T(4,128)} %copy.42), calls=%async_computation.1 | async-start | bytes 524288 | tf_op jit(solution)/shard_map/while/body/eval_jaxpr/all_to_all | solution.py:56
  227.6 6.9 %collective-permute-start = (f32[2,4,4096]{2,1,0:T(4,128)S(1)}, f32[2,4,4096]{2,1,0:T(4,128)S(1)}, u32[]{:S(2)}, u32[]{:S(2)}) collective-permute-start(f32[2,4,4096]{2,1,0:T(4,128)S(1)} %get-tuple-element.366), channel_id=1, source_target_pairs={{0,32},{32,64},{64,96},{96,128},{128,160},{160,192},{192,224},{224... | collective-permute-start | bytes 393224 | tf_op jit(solution)/shard_map/while/body/eval_jaxpr/ppermute | solution.py:19
  251.2 10.8 %all-to-all-start.1 = ((f32[2,64,4,128]{3,2,0,1:T(4,128)}), f32[2,64,4,128]{3,2,0,1:T(4,128)S(1)}, u32[]{:S(2)}, u32[]{:S(2)}) async-start(f32[2,64,4,128]{3,2,0,1:T(4,128)} %copy.42), calls=%async_computation.1 | async-start | bytes 524288 | tf_op jit(solution)/shard_map/while/body/eval_jaxpr/all_to_all | solution.py:56
  264.0 7.2 %collective-permute-start = (f32[2,4,4096]{2,1,0:T(4,128)S(1)}, f32[2,4,4096]{2,1,0:T(4,128)S(1)}, u32[]{:S(2)}, u32[]{:S(2)}) collective-permute-start(f32[2,4,4096]{2,1,0:T(4,128)S(1)} %get-tuple-element.366), channel_id=1, source_target_pairs={{0,32},{32,64},{64,96},{96,128},{128,160},{160,192},{192,224},{224... | collective-permute-start | bytes 393224 | tf_op jit(solution)/shard_map/while/body/eval_jaxpr/ppermute | solution.py:19
  286.8 10.8 %all-to-all-start.1 = ((f32[2,64,4,128]{3,2,0,1:T(4,128)}), f32[2,64,4,128]{3,2,0,1:T(4,128)S(1)}, u32[]{:S(2)}, u32[]{:S(2)}) async-start(f32[2,64,4,128]{3,2,0,1:T(4,128)} %copy.42), calls=%async_computation.1 | async-start | bytes 524288 | tf_op jit(solution)/shard_map/while/body/eval_jaxpr/all_to_all | solution.py:56
  299.6 6.9 %collective-permute-start = (f32[2,4,4096]{2,1,0:T(4,128)S(1)}, f32[2,4,4096]{2,1,0:T(4,128)S(1)}, u32[]{:S(2)}, u32[]{:S(2)}) collective-permute-start(f32[2,4,4096]{2,1,0:T(4,128)S(1)} %get-tuple-element.366), channel_id=1, source_target_pairs={{0,32},{32,64},{64,96},{96,128},{128,160},{160,192},{192,224},{224... | collective-permute-start | bytes 393224 | tf_op jit(solution)/shard_map/while/body/eval_jaxpr/ppermute | solution.py:19
  322.4 10.8 %all-to-all-start.1 = ((f32[2,64,4,128]{3,2,0,1:T(4,128)}), f32[2,64,4,128]{3,2,0,1:T(4,128)S(1)}, u32[]{:S(2)}, u32[]{:S(2)}) async-start(f32[2,64,4,128]{3,2,0,1:T(4,128)} %copy.42), calls=%async_computation.1 | async-start | bytes 524288 | tf_op jit(solution)/shard_map/while/body/eval_jaxpr/all_to_all | solution.py:56
  335.1 6.9 %collective-permute-start = (f32[2,4,4096]{2,1,0:T(4,128)S(1)}, f32[2,4,4096]{2,1,0:T(4,128)S(1)}, u32[]{:S(2)}, u32[]{:S(2)}) collective-permute-start(f32[2,4,4096]{2,1,0:T(4,128)S(1)} %get-tuple-element.366), channel_id=1, source_target_pairs={{0,32},{32,64},{64,96},{96,128},{128,160},{160,192},{192,224},{224... | collective-permute-start | bytes 393224 | tf_op jit(solution)/shard_map/while/body/eval_jaxpr/ppermute | solution.py:19
  357.9 10.8 %all-to-all-start.1 = ((f32[2,64,4,128]{3,2,0,1:T(4,128)}), f32[2,64,4,128]{3,2,0,1:T(4,128)S(1)}, u32[]{:S(2)}, u32[]{:S(2)}) async-start(f32[2,64,4,128]{3,2,0,1:T(4,128)} %copy.42), calls=%async_computation.1 | async-start | bytes 524288 | tf_op jit(solution)/shard_map/while/body/eval_jaxpr/all_to_all | solution.py:56
  370.6 6.9 %collective-permute-start = (f32[2,4,4096]{2,1,0:T(4,128)S(1)}, f32[2,4,4096]{2,1,0:T(4,128)S(1)}, u32[]{:S(2)}, u32[]{:S(2)}) collective-permute-start(f32[2,4,4096]{2,1,0:T(4,128)S(1)} %get-tuple-element.366), channel_id=1, source_target_pairs={{0,32},{32,64},{64,96},{96,128},{128,160},{160,192},{192,224},{224... | collective-permute-start | bytes 393224 | tf_op jit(solution)/shard_map/while/body/eval_jaxpr/ppermute | solution.py:19
  394.3 11.3 %all-to-all-start.1 = ((f32[2,64,4,128]{3,2,0,1:T(4,128)}), f32[2,64,4,128]{3,2,0,1:T(4,128)S(1)}, u32[]{:S(2)}, u32[]{:S(2)}) async-start(f32[2,64,4,128]{3,2,0,1:T(4,128)} %copy.42), calls=%async_computation.1 | async-start | bytes 524288 | tf_op jit(solution)/shard_map/while/body/eval_jaxpr/all_to_all | solution.py:56
  407.4 6.9 %collective-permute-start = (f32[2,4,4096]{2,1,0:T(4,128)S(1)}, f32[2,4,4096]{2,1,0:T(4,128)S(1)}, u32[]{:S(2)}, u32[]{:S(2)}) collective-permute-start(f32[2,4,4096]{2,1,0:T(4,128)S(1)} %get-tuple-element.366), channel_id=1, source_target_pairs={{0,32},{32,64},{64,96},{96,128},{128,160},{160,192},{192,224},{224... | collective-permute-start | bytes 393224 | tf_op jit(solution)/shard_map/while/body/eval_jaxpr/ppermute | solution.py:19
  430.6 11.0 %all-to-all-start.1 = ((f32[2,64,4,128]{3,2,0,1:T(4,128)}), f32[2,64,4,128]{3,2,0,1:T(4,128)S(1)}, u32[]{:S(2)}, u32[]{:S(2)}) async-start(f32[2,64,4,128]{3,2,0,1:T(4,128)} %copy.42), calls=%async_computation.1 | async-start | bytes 524288 | tf_op jit(solution)/shard_map/while/body/eval_jaxpr/all_to_all | solution.py:56
  443.5 6.9 %collective-permute-start = (f32[2,4,4096]{2,1,0:T(4,128)S(1)}, f32[2,4,4096]{2,1,0:T(4,128)S(1)}, u32[]{:S(2)}, u32[]{:S(2)}) collective-permute-start(f32[2,4,4096]{2,1,0:T(4,128)S(1)} %get-tuple-element.366), channel_id=1, source_target_pairs={{0,32},{32,64},{64,96},{96,128},{128,160},{160,192},{192,224},{224... | collective-permute-start | bytes 393224 | tf_op jit(solution)/shard_map/while/body/eval_jaxpr/ppermute | solution.py:19
  466.3 10.8 %all-to-all-start.1 = ((f32[2,64,4,128]{3,2,0,1:T(4,128)}), f32[2,64,4,128]{3,2,0,1:T(4,128)S(1)}, u32[]{:S(2)}, u32[]{:S(2)}) async-start(f32[2,64,4,128]{3,2,0,1:T(4,128)} %copy.42), calls=%async_computation.1 | async-start | bytes 524288 | tf_op jit(solution)/shard_map/while/body/eval_jaxpr/all_to_all | solution.py:56
  501.8 10.8 %all-to-all-start.1 = ((f32[2,64,4,128]{3,2,0,1:T(4,128)}), f32[2,64,4,128]{3,2,0,1:T(4,128)S(1)}, u32[]{:S(2)}, u32[]{:S(2)}) async-start(f32[2,64,4,128]{3,2,0,1:T(4,128)} %copy.42), calls=%async_computation.1 | async-start | bytes 524288 | tf_op jit(solution)/shard_map/while/body/eval_jaxpr/all_to_all | solution.py:56
  514.5 7.2 %collective-permute-start = (f32[2,4,4096]{2,1,0:T(4,128)S(1)}, f32[2,4,4096]{2,1,0:T(4,128)S(1)}, u32[]{:S(2)}, u32[]{:S(2)}) collective-permute-start(f32[2,4,4096]{2,1,0:T(4,128)S(1)} %get-tuple-element.366), channel_id=1, source_target_pairs={{0,32},{32,64},{64,96},{96,128},{128,160},{160,192},{192,224},{224... | collective-permute-start | bytes 393224 | tf_op jit(solution)/shard_map/while/body/eval_jaxpr/ppermute | solution.py:19
  537.3 11.7 %all-to-all-start.1 = ((f32[2,64,4,128]{3,2,0,1:T(4,128)}), f32[2,64,4,128]{3,2,0,1:T(4,128)S(1)}, u32[]{:S(2)}, u32[]{:S(2)}) async-start(f32[2,64,4,128]{3,2,0,1:T(4,128)} %copy.42), calls=%async_computation.1 | async-start | bytes 524288 | tf_op jit(solution)/shard_map/while/body/eval_jaxpr/all_to_all | solution.py:56
  550.9 6.9 %collective-permute-start = (f32[2,4,4096]{2,1,0:T(4,128)S(1)}, f32[2,4,4096]{2,1,0:T(4,128)S(1)}, u32[]{:S(2)}, u32[]{:S(2)}) collective-permute-start(f32[2,4,4096]{2,1,0:T(4,128)S(1)} %get-tuple-element.366), channel_id=1, source_target_pairs={{0,32},{32,64},{64,96},{96,128},{128,160},{160,192},{192,224},{224... | collective-permute-start | bytes 393224 | tf_op jit(solution)/shard_map/while/body/eval_jaxpr/ppermute | solution.py:19
  574.1 10.8 %all-to-all-start.1 = ((f32[2,64,4,128]{3,2,0,1:T(4,128)}), f32[2,64,4,128]{3,2,0,1:T(4,128)S(1)}, u32[]{:S(2)}, u32[]{:S(2)}) async-start(f32[2,64,4,128]{3,2,0,1:T(4,128)} %copy.42), calls=%async_computation.1 | async-start | bytes 524288 | tf_op jit(solution)/shard_map/while/body/eval_jaxpr/all_to_all | solution.py:56
  (4 other events, 16.2 us)
Sparse Core Ops, SparseCore 0:
  587.7 94.8 all-reduce.1
where the time goes:
time: 694 us; the launch traced here: 691 us
  waiting for transfers between devices  297 us (43%)
  blocking collectives  161 us (23%)
  starting transfers between devices  95.3 us (14%)
  matrix products  81.1 us (12%)
  local copies, waits for them, and re-layouts  29.7 us (4%)
  between operations  13.6 us (2%)
  other arithmetic  11 us (2%)
    all_to_all x15, blocking collectives, step_terms(): lax.all_to_all(spectra, 'fft', split_axis=2, concat_axis=1, tiled=True)  161 us
    all_to_all x16, waiting for transfers between devices, pencil_work(): lax.all_to_all(spectra, 'fft', split_axis=1, concat_axis=2, tiled=True)  117 us
    psum x1, waiting for transfers between devices, local(): return lax.psum(field, 'pool')  95 us
    ppermute x15, waiting for transfers between devices, from_behind(): return lax.ppermute(value, axis, pairs)  77.9 us
    all_to_all x16, starting transfers between devices, pencil_work(): lax.all_to_all(spectra, 'fft', split_axis=1, concat_axis=2, tiled=True)  56.8 us
    dot_general x64, matrix products, along_axis(): crossed = jnp.einsum(pattern, sines, swapped, precision=highest)  36.1 us
    dot_general x64, matrix products, along_axis(): direct = jnp.einsum(pattern, cosine, values, precision=highest)  33.6 us
    ppermute x15, starting transfers between devices, from_behind(): return lax.ppermute(value, axis, pairs)  30.5 us
  transfers between devices with their start and end apart: 33, of which 33 were waited for; matrix products, arithmetic and copies ran while one was open for 0% of the time, Pallas kernels for 0%

commit v1 on v0

v1 whole, which is shorter than its diff:
```python
import functools

import jax
import jax.numpy as jnp
import ml_dtypes
import numpy as np
from jax import lax
from jax.experimental import pallas as pl
from jax.experimental.pallas import tpu as pltpu
from jax.sharding import PartitionSpec as P

N = 64
CELLS = N * N * N
LANES = 2 * N
PEERS = 32
UNITS = 9
ROWS = 8 * UNITS

OFFSETS = (0, 2, -3, -4, 4)
MEETINGS = ((3, 2), (0, 1), (2, 0), (3, 0), (2, 1), (3, 1), (2, 4))
OPPOSITE = (3, 4)


def wave_parts(rows, columns):
    angle = 2.0 * np.pi / N * ((rows * columns) % N)
    return np.cos(angle), np.sin(angle)


def split_table(table):
    high = table.astype(ml_dtypes.bfloat16)
    low = (table - high.astype(np.float64)).astype(ml_dtypes.bfloat16)
    return np.stack([high, low])


def tables():
    index = np.arange(N)
    cosine, sine = wave_parts(index[:, None], index[None, :])
    turn = np.stack([np.stack([cosine, sine]), np.stack([-sine, cosine])])
    two = np.eye(2)
    along_z = np.einsum("oikz,ab->iazobk", turn, two).reshape(256, 256)
    along_y = np.einsum("oiky,ab->kaoiby", turn, two)
    along_y = along_y.reshape(32, 2, 2, 2, 2, 2, N).transpose(0, 2, 3, 1, 5, 4, 6)
    along_y = along_y.reshape(256, 256)
    along_x = np.einsum("oikx,ab->koaxib", turn, two).reshape(256, 256)
    return [split_table(t) for t in (along_z, along_y, along_x, along_x.T, along_y.T, along_z.T)]


def halves(value):
    high = value.astype(jnp.bfloat16)
    low = (value - high.astype(jnp.float32)).astype(jnp.bfloat16)
    return high, low


def dot(left, right):
    return jnp.dot(left, right, preferred_element_type=jnp.float32)


def times_table(value, table):
    high, low = halves(value)
    return dot(high, table[0]) + dot(low, table[0]) + dot(high, table[1])


def table_times(table, value):
    high, low = halves(value)
    return dot(table[0], high) + dot(table[0], low) + dot(table[1], high)


def swap(value):
    return pltpu.roll(value, N, 1)


def forward_kernel(side, b0, b1, b2, b3, b4, table_z, table_y, out):
    blocks = (b0, b1, b2, b3, b4)

    def unit(number, plane):
        if number < 14:
            left, right = MEETINGS[number // 2]
            right = blocks[right][plane]
            return blocks[left][plane] * (swap(right) if number % 2 else right)
        own = b0[plane]
        if number == 14:
            return own * own
        if number == 15:
            return own * swap(own)
        if number == 16:
            right = blocks[OPPOSITE[1]][plane]
            return blocks[OPPOSITE[0]][plane] * jnp.where(side[0] == 0, right, swap(right))
        return jnp.zeros((N, LANES), jnp.float32)

    for u in range(UNITS):
        density = jnp.concatenate(
            [
                jnp.concatenate([unit(2 * u, plane), unit(2 * u + 1, plane)], axis=1)
                for plane in range(2)
            ],
            axis=0,
        )
        rows = times_table(density, table_z)
        rows = jnp.concatenate(
            [
                rows[plane * N : plane * N + N, part * LANES : part * LANES + LANES]
                for plane in range(2)
                for part in range(2)
            ],
            axis=0,
        )
        out[:, 8 * u : 8 * u + 8, :] = table_times(table_y, rows).reshape(PEERS, 8, LANES)


def middle_kernel(spectra, coulomb, table_x, table_x_back, out):
    for u in range(UNITS):
        rows = spectra[:, 8 * u : 8 * u + 8, :].reshape(256, LANES)
        rows = table_times(table_x, rows) * coulomb[...]
        out[:, 8 * u : 8 * u + 8, :] = table_times(table_x_back, rows).reshape(PEERS, 8, LANES)


def backward_kernel(
    side, returned, b0, b1, b2, b3, b4, table_y_back, table_z_back, f0, f1, f2, f3, f4
):
    blocks = (b0, b1, b2, b3, b4)
    fields = (f0, f1, f2, f3, f4)
    started = set()

    def add(place, plane, value):
        if (place, plane) in started:
            fields[place][plane] += value
        else:
            started.add((place, plane))
            fields[place][plane] = value

    def collect(number, plane, potential):
        if number < 14:
            left, right = MEETINGS[number // 2]
            if number % 2:
                add(left, plane, potential * swap(blocks[right][plane]))
                add(right, plane, swap(potential * blocks[left][plane]))
            else:
                add(left, plane, potential * blocks[right][plane])
                add(right, plane, potential * blocks[left][plane])
        elif number == 14:
            add(0, plane, potential * b0[plane])
        elif number == 15:
            add(0, plane, potential * swap(b0[plane]))
        elif number == 16:
            left, right = OPPOSITE
            partner = blocks[right][plane]
            add(left, plane, potential * jnp.where(side[0] == 0, partner, swap(partner)))
            given = potential * blocks[left][plane]
            add(right, plane, jnp.where(side[0] == 0, given, swap(given)))

    for u in range(UNITS):
        rows = returned[:, 8 * u : 8 * u + 8, :].reshape(256, LANES)
        rows = table_times(table_y_back, rows)
        rows = jnp.concatenate(
            [
                jnp.concatenate(
                    [
                        rows[plane * LANES + part * N : plane * LANES + part * N + N]
                        for part in range(2)
                    ],
                    axis=1,
                )
                for plane in range(2)
            ],
            axis=0,
        )
        rows = times_table(rows, table_z_back)
        for plane in range(2):
            for half in range(2):
                collect(
                    2 * u + half,
                    plane,
                    rows[plane * N : plane * N + N, half * LANES : half * LANES + LANES],
                )


VMEM = pl.BlockSpec(memory_space=pltpu.VMEM)
SMEM = pl.BlockSpec(memory_space=pltpu.SMEM)
PARAMS = pltpu.CompilerParams(vmem_limit_bytes=32 * 1024 * 1024)
CHUNKS = jax.ShapeDtypeStruct((PEERS, ROWS, LANES), jnp.float32)
BLOCK = jax.ShapeDtypeStruct((2, N, LANES), jnp.float32)


def forward(side, blocks, table_z, table_y):
    return pl.pallas_call(
        forward_kernel,
        out_shape=CHUNKS,
        in_specs=[SMEM] + [VMEM] * 7,
        out_specs=VMEM,
        compiler_params=PARAMS,
    )(side, *blocks, table_z, table_y)


def middle(spectra, coulomb, table_x, table_x_back):
    return pl.pallas_call(
        middle_kernel,
        out_shape=CHUNKS,
        in_specs=[VMEM] * 4,
        out_specs=VMEM,
        compiler_params=PARAMS,
    )(spectra, coulomb, table_x, table_x_back)


def backward(side, returned, blocks, table_y_back, table_z_back):
    return pl.pallas_call(
        backward_kernel,
        out_shape=[BLOCK] * 5,
        in_specs=[SMEM] + [VMEM] * 8,
        out_specs=[VMEM] * 5,
        compiler_params=PARAMS,
    )(side, returned, *blocks, table_y_back, table_z_back)


def along_band(value, steps):
    count = lax.axis_size("band")
    pairs = [(source, (source + steps) % count) for source in range(count)]
    return lax.ppermute(value, "band", pairs)


def spread_kernel(kernel, pool_at):
    mine = lax.dynamic_slice_in_dim(kernel, pool_at * LANES, LANES, 1)
    mine = mine.reshape(N, 1, 2, 1, N) * (-1.0 / CELLS)
    return jnp.broadcast_to(mine, (N, 2, 2, 2, N)).reshape(256, LANES)


def exchange(value):
    return lax.all_to_all(value, ("fft", "pool"), split_axis=0, concat_axis=0, tiled=True)


def local(orbitals, kernel):
    pool_at = lax.axis_index("pool")
    side = (lax.axis_index("band") // 8).astype(jnp.int32).reshape(1)
    table_z, table_y, table_x, table_x_back, table_y_back, table_z_back = [
        jnp.asarray(t) for t in tables()
    ]
    own = lax.dynamic_slice_in_dim(orbitals, 2 * pool_at, 2, 1)
    own = own.reshape(2, 2, N, N).transpose(1, 2, 0, 3).reshape(2, N, LANES)
    blocks = [along_band(own, -s) if s else own for s in OFFSETS]
    coulomb = spread_kernel(kernel, pool_at)
    spectra = exchange(forward(side, blocks, table_z, table_y))
    returned = exchange(middle(spectra, coulomb, table_x, table_x_back))
    fields = backward(side, returned, blocks, table_y_back, table_z_back)
    total = functools.reduce(
        jnp.add, [along_band(f, s) if s else f for s, f in zip(OFFSETS, fields)]
    )
    both = lax.all_gather(total, "pool", tiled=True)
    return both.reshape(4, N, 2, N).transpose(2, 0, 1, 3).reshape(2, 4, N * N)


def solution(mesh):
    return jax.shard_map(
        local,
        mesh=mesh,
        in_specs=(P("band", "fft", None), P(None, "fft")),
        out_specs=P("band", "fft", None),
        check_vma=False,
    )
```

time: 694 us -> 124 us (0.18)
  waiting for transfers between devices: 297 us -> 27.9 us
  blocking collectives: 161 us -> 27.6 us
  matrix products: 81.1 us -> 0 us
  starting transfers between devices: 95.3 us -> 52.3 us
  local copies, waits for them, and re-layouts: 29.7 us -> 4.58 us
  between operations: 13.6 us -> 0.23 us
  other arithmetic: 11 us -> 0.03 us
  Pallas kernels: 0 us -> 10.7 us
    all_to_all x15 -> x1, blocking collectives: 161 us -> 22.8 us  [exchange(): lax.all_to_all(value, ('fft', 'pool'), split_axis=0, concat_axis=0, tiled...]
    all_to_all x17 -> x1, waiting for transfers between devices: 124 us -> 18 us  [exchange(): lax.all_to_all(value, ('fft', 'pool'), split_axis=0, concat_axis=0, tiled...]
    psum x1 -> x0, waiting for transfers between devices: 95 us -> none  [local(): return lax.psum(field, 'pool')]
    dot_general x160 -> x0, matrix products: 81.1 us -> none  [the longest x64 36.1 us: along_axis(): crossed = jnp.einsum(pattern, sines, swapped, precision=highest)]
    ppermute x15 -> x8, waiting for transfers between devices: 77.9 us -> 9.92 us  [along_band(): return lax.ppermute(value, 'band', pairs)]
    all_to_all x17 -> x1, starting transfers between devices: 64.5 us -> 9.41 us  [exchange(): lax.all_to_all(value, ('fft', 'pool'), split_axis=0, concat_axis=0, tiled...]
    sub x16 -> x0, local copies, waits for them, and re-layouts: 13.9 us -> none  [along_axis(): return direct - crossed]
    ppermute x15 -> x8, starting transfers between devices: 30.5 us -> 42.9 us  [along_band(): return lax.ppermute(value, 'band', pairs)]
  transfers between devices with their start and end apart: 33 -> 9, of which waited for: 33 -> 4; matrix products, arithmetic and copies ran while one was open for 0% -> 0% of each run, Pallas kernels for 0% -> 0%
where the time goes in v1:
time: 124 us; the launch traced here: 123 us
  starting transfers between devices  52.3 us (42%)
  waiting for transfers between devices  27.9 us (22%)
  blocking collectives  27.6 us (22%)
  Pallas kernels  10.7 us (9%)
  local copies, waits for them, and re-layouts  4.58 us (4%)
    ppermute x8, starting transfers between devices, along_band(): return lax.ppermute(value, 'band', pairs)  42.9 us
    all_to_all x1, blocking collectives, exchange(): lax.all_to_all(value, ('fft', 'pool'), split_axis=0, concat_axis=0, tiled...  22.8 us
    all_to_all x1, waiting for transfers between devices, exchange(): lax.all_to_all(value, ('fft', 'pool'), split_axis=0, concat_axis=0, tiled...  18 us
    ppermute x8, waiting for transfers between devices, along_band(): return lax.ppermute(value, 'band', pairs)  9.92 us
    all_to_all x1, starting transfers between devices, exchange(): lax.all_to_all(value, ('fft', 'pool'), split_axis=0, concat_axis=0, tiled...  9.41 us
    all_gather x1, blocking collectives, local(): both = lax.all_gather(total, 'pool', tiled=True)  4.77 us
    pallas_call x1, Pallas kernels, forward(): pl.pallas_call(forward_kernel, out_shape=CHUNKS, in_specs=[SMEM] + [VMEM]...  4.64 us
    pallas_call x1, Pallas kernels, middle(): pl.pallas_call(middle_kernel, out_shape=CHUNKS, in_specs=[VMEM] * 4, out_...  3.32 us
  transfers between devices with their start and end apart: 9, of which 4 were waited for; matrix products, arithmetic and copies ran while one was open for 0% of the time, Pallas kernels for 0%

profile of v1, /device:TPU:1, one launch (start us, length us, event | category | flops | bytes accessed | tf_op | source)
XLA Modules:
  0.0 123.3 jit_solution(7378725933511462943)
XLA Ops:
  0.0 0.9 copy-done
  0.9 0.1 reshape.29
  1.1 0.1 copy.12
  1.2 0.1 reshape.30.b0
  1.3 12.4 %collective-permute-start = (f32[2,64,128]{2,1,0:T(8,128)S(1)}, f32[2,64,128]{2,1,0:T(8,128)S(1)}, u32[]{:S(2)}, u32[]{:S(2)}) collective-permute-start(f32[2,64,128]{2,1,0:T(8,128)S(1)} %reshape.30.b0), channel_id=1, source_target_pairs={{0,448},{32,480},{64,0},{96,32},{128,64},{160,96},{192,128},{224,1... | collective-permute-start | bytes 196616 | tf_op jit(solution)/shard_map/ppermute | solution.py:217
  13.7 1.9 %collective-permute-start.1 = (f32[2,64,128]{2,1,0:T(8,128)S(1)}, f32[2,64,128]{2,1,0:T(8,128)S(1)}, u32[]{:S(2)}, u32[]{:S(2)}) collective-permute-start(f32[2,64,128]{2,1,0:T(8,128)S(1)} %reshape.30.b0), channel_id=1, source_target_pairs={{0,96},{32,128},{64,160},{96,192},{128,224},{160,256},{192,288},{2... | collective-permute-start | bytes 196616 | tf_op jit(solution)/shard_map/ppermute | solution.py:217
  15.6 3.5 %collective-permute-start.2 = (f32[2,64,128]{2,1,0:T(8,128)S(1)}, f32[2,64,128]{2,1,0:T(8,128)S(1)}, u32[]{:S(2)}, u32[]{:S(2)}) collective-permute-start(f32[2,64,128]{2,1,0:T(8,128)S(1)} %reshape.30.b0), channel_id=1, source_target_pairs={{0,128},{32,160},{64,192},{96,224},{128,256},{160,288},{192,320},{... | collective-permute-start | bytes 196616 | tf_op jit(solution)/shard_map/ppermute | solution.py:217
  19.2 5.7 %collective-permute-start.3 = (f32[2,64,128]{2,1,0:T(8,128)S(1)}, f32[2,64,128]{2,1,0:T(8,128)S(1)}, u32[]{:S(2)}, u32[]{:S(2)}) collective-permute-start(f32[2,64,128]{2,1,0:T(8,128)S(1)} %reshape.30.b0), channel_id=1, source_target_pairs={{0,384},{32,416},{64,448},{96,480},{128,0},{160,32},{192,64},{224,... | collective-permute-start | bytes 196616 | tf_op jit(solution)/shard_map/ppermute | solution.py:217
  24.9 0.0 collective-permute-done.1.b2
  24.9 3.5 %collective-permute-done.3.b4 = f32[2,64,128]{2,1,0:T(8,128)S(1)} collective-permute-done((f32[2,64,128]{2,1,0:T(8,128)S(1)}, f32[2,64,128]{2,1,0:T(8,128)S(1)}, u32[]{:S(2)}, u32[]{:S(2)}) %collective-permute-start.3) | collective-permute-done | bytes 65568 | tf_op jit(solution)/shard_map/ppermute | solution.py:217
  28.4 0.9 copy-done.5
  29.4 0.9 copy-done.6
  30.3 4.6 %shard_map.82 = f32[32,72,128]{2,1,0:T(8,128)} custom-call(s32[1]{0:T(128)} %bitcast.side, f32[2,64,128]{2,1,0:T(8,128)S(1)} %reshape.30.b0, f32[2,64,128]{2,1,0:T(8,128)S(1)} %collective-permute-done.b1, f32[2,64,128]{2,1,0:T(8,128)S(1)} %collective-permute-done.1.b2, f32[2,64,128]{2,1,0:T(8,128)S(1)} %collective-permute-done.2.b3, ...), custom_call_target="tpu_custom_call" | custom-call | tf_op jit(solution)/shard_map/pallas_call | solution.py:185
  35.0 9.4 %all-to-all-start = ((f32[32,72,128]{2,1,0:T(8,128)}), f32[32,72,128]{2,1,0:T(8,128)S(1)}, u32[]{:S(2)}, u32[]{:S(2)}) async-start(f32[32,72,128]{2,1,0:T(8,128)} %shard_map.82), calls=%async_computation | async-start | bytes 2359296 | tf_op jit(solution)/shard_map/all_to_all | solution.py:227
  44.4 0.1 mul.20
  44.5 0.1 broadcast_in_dim.2
  44.6 0.2 reshape.31.coulomb
  44.8 18.0 %all-to-all-done.spectra = f32[32,72,128]{2,1,0:T(8,128)S(1)} async-done(((f32[32,72,128]{2,1,0:T(8,128)}), f32[32,72,128]{2,1,0:T(8,128)S(1)}, u32[]{:S(2)}, u32[]{:S(2)}) %all-to-all-start) | async-done | bytes 1179680 | tf_op jit(solution)/shard_map/all_to_all | solution.py:227
  62.8 3.3 %shard_map.83 = f32[32,72,128]{2,1,0:T(8,128)S(1)} custom-call(f32[32,72,128]{2,1,0:T(8,128)S(1)} %all-to-all-done.spectra, f32[256,128]{1,0:T(8,128)S(1)} %reshape.31.coulomb, bf16[2,256,256]{2,1,0:T(8,128)(2,1)S(1)} %copy-done.3, bf16[2,256,256]{2,1,0:T(8,128)(2,1)S(1)} %copy-done.4), custom_call_target="tpu_custom_call" | custom-call | tf_op jit(solution)/shard_map/pallas_call | solution.py:195
  66.1 0.0 copy-start.1
  66.1 0.0 copy-start.2
  66.1 22.8 %all_to_all.10.returned = f32[32,72,128]{2,1,0:T(8,128)S(1)} all-to-all(f32[32,72,128]{2,1,0:T(8,128)S(1)} %shard_map.83), channel_id=1, replica_groups=mesh['band'=16,'fft'=16,'pool'=2] {'fft','pool'}, dimensions={0} | all-to-all | bytes 2359296 | tf_op jit(solution)/shard_map/all_to_all | solution.py:227
  88.9 2.7 %shard_map.84 = (f32[2,64,128]{2,1,0:T(8,128)S(1)}, f32[2,64,128]{2,1,0:T(8,128)S(1)}, f32[2,64,128]{2,1,0:T(8,128)S(1)}, f32[2,64,128]{2,1,0:T(8,128)S(1)}, f32[2,64,128]{2,1,0:T(8,128)S(1)}) custom-call(s32[1]{0:T(128)} %bitcast.side, f32[32,72,128]{2,1,0:T(8,128)S(1)} %all_to_all.10.returned, f32[2,64,128]{2,1,0:T(8,128)S(1)} %reshape.30.b0, ...), custom_call_target="tpu_custom_call" | custom-call | tf_op jit(solution)/shard_map/pallas_call | solution.py:205
  91.6 7.2 %collective-permute-start.4 = (f32[2,64,128]{2,1,0:T(8,128)S(1)}, f32[2,64,128]{2,1,0:T(8,128)S(1)}, u32[]{:S(2)}, u32[]{:S(2)}) collective-permute-start(f32[2,64,128]{2,1,0:T(8,128)S(1)} %get-tuple-element.11), channel_id=1, source_target_pairs={{0,64},{32,96},{64,128},{96,160},{128,192},{160,224},{192,256},{22... | collective-permute-start | bytes 196616 | tf_op jit(solution)/shard_map/ppermute | solution.py:217
  98.8 3.1 %collective-permute-start.5 = (f32[2,64,128]{2,1,0:T(8,128)S(1)}, f32[2,64,128]{2,1,0:T(8,128)S(1)}, u32[]{:S(2)}, u32[]{:S(2)}) collective-permute-start(f32[2,64,128]{2,1,0:T(8,128)S(1)} %get-tuple-element.12), channel_id=1, source_target_pairs={{0,416},{32,448},{64,480},{96,0},{128,32},{160,64},{192,96},{224,1... | collective-permute-start | bytes 196616 | tf_op jit(solution)/shard_map/ppermute | solution.py:217
  101.9 5.8 %collective-permute-start.6 = (f32[2,64,128]{2,1,0:T(8,128)S(1)}, f32[2,64,128]{2,1,0:T(8,128)S(1)}, u32[]{:S(2)}, u32[]{:S(2)}) collective-permute-start(f32[2,64,128]{2,1,0:T(8,128)S(1)} %get-tuple-element.13), channel_id=1, source_target_pairs={{0,384},{32,416},{64,448},{96,480},{128,0},{160,32},{192,64},{224,... | collective-permute-start | bytes 196616 | tf_op jit(solution)/shard_map/ppermute | solution.py:217
  107.7 3.4 %collective-permute-start.7 = (f32[2,64,128]{2,1,0:T(8,128)S(1)}, f32[2,64,128]{2,1,0:T(8,128)S(1)}, u32[]{:S(2)}, u32[]{:S(2)}) collective-permute-start(f32[2,64,128]{2,1,0:T(8,128)S(1)} %get-tuple-element.14), channel_id=1, source_target_pairs={{0,128},{32,160},{64,192},{96,224},{128,256},{160,288},{192,320},{... | collective-permute-start | bytes 196616 | tf_op jit(solution)/shard_map/ppermute | solution.py:217
  111.1 5.4 %collective-permute-done.6 = f32[2,64,128]{2,1,0:T(8,128)S(1)} collective-permute-done((f32[2,64,128]{2,1,0:T(8,128)S(1)}, f32[2,64,128]{2,1,0:T(8,128)S(1)}, u32[]{:S(2)}, u32[]{:S(2)}) %collective-permute-start.6) | collective-permute-done | bytes 65568 | tf_op jit(solution)/shard_map/ppermute | solution.py:217
  116.6 0.9 collective-permute-done.7
  117.5 4.8 %all_gather.3 = f32[4,64,128]{2,1,0:T(8,128)S(1)} all-gather(f32[2,64,128]{2,1,0:T(8,128)S(1)} %add_add_fusion), channel_id=1, replica_groups=mesh['band'=16,'fft'=16,'pool'=2] {'pool'}, dimensions={0}, use_global_device_ids=true | all-gather | bytes 196608 | tf_op jit(solution)/shard_map/all_gather | solution.py:246
  122.3 0.2 reshape.32
  122.5 0.8 reshape.33
  (19 shorter events, 0.1 us)
Async XLA Ops:
  0.0 0.9 copy-start
  1.3 23.5 %collective-permute-start = (f32[2,64,128]{2,1,0:T(8,128)S(1)}, f32[2,64,128]{2,1,0:T(8,128)S(1)}, u32[]{:S(2)}, u32[]{:S(2)}) collective-permute-start(f32[2,64,128]{2,1,0:T(8,128)S(1)} %reshape.30.b0), channel_id=1, source_target_pairs={{0,448},{32,480},{64,0},{96,32},{128,64},{160,96},{192,128},{224,1... | collective-permute-start | bytes 196616 | tf_op jit(solution)/shard_map/ppermute | solution.py:217
  13.7 11.2 %collective-permute-start.1 = (f32[2,64,128]{2,1,0:T(8,128)S(1)}, f32[2,64,128]{2,1,0:T(8,128)S(1)}, u32[]{:S(2)}, u32[]{:S(2)}) collective-permute-start(f32[2,64,128]{2,1,0:T(8,128)S(1)} %reshape.30.b0), channel_id=1, source_target_pairs={{0,96},{32,128},{64,160},{96,192},{128,224},{160,256},{192,288},{2... | collective-permute-start | bytes 196616 | tf_op jit(solution)/shard_map/ppermute | solution.py:217
  15.6 9.2 %collective-permute-start.2 = (f32[2,64,128]{2,1,0:T(8,128)S(1)}, f32[2,64,128]{2,1,0:T(8,128)S(1)}, u32[]{:S(2)}, u32[]{:S(2)}) collective-permute-start(f32[2,64,128]{2,1,0:T(8,128)S(1)} %reshape.30.b0), channel_id=1, source_target_pairs={{0,128},{32,160},{64,192},{96,224},{128,256},{160,288},{192,320},{... | collective-permute-start | bytes 196616 | tf_op jit(solution)/shard_map/ppermute | solution.py:217
  19.2 9.3 %collective-permute-start.3 = (f32[2,64,128]{2,1,0:T(8,128)S(1)}, f32[2,64,128]{2,1,0:T(8,128)S(1)}, u32[]{:S(2)}, u32[]{:S(2)}) collective-permute-start(f32[2,64,128]{2,1,0:T(8,128)S(1)} %reshape.30.b0), channel_id=1, source_target_pairs={{0,384},{32,416},{64,448},{96,480},{128,0},{160,32},{192,64},{224,... | collective-permute-start | bytes 196616 | tf_op jit(solution)/shard_map/ppermute | solution.py:217
  28.4 1.0 copy-start.5
  29.4 0.9 copy-start.6
  35.0 9.4 %copy-start.7 = (f32[64,256]{1,0:T(8,128)S(1)}, f32[64,256]{1,0:T(8,128)}, u32[]{:S(2)}) copy-start(f32[64,256]{1,0:T(8,128)} %param.9) | copy-start | bytes 196612
  35.0 27.8 %copy-start.3 = (bf16[2,256,256]{2,1,0:T(8,128)(2,1)S(1)}, bf16[2,256,256]{2,1,0:T(8,128)(2,1)}, u32[]{:S(2)}) copy-start(bf16[2,256,256]{2,1,0:T(8,128)(2,1)} %constant.51.clone.table_x) | copy-start | bytes 786436
  35.0 27.8 %copy-start.4 = (bf16[2,256,256]{2,1,0:T(8,128)(2,1)S(1)}, bf16[2,256,256]{2,1,0:T(8,128)(2,1)}, u32[]{:S(2)}) copy-start(bf16[2,256,256]{2,1,0:T(8,128)(2,1)} %constant.52.clone.table_x_back) | copy-start | bytes 786436
  35.0 27.8 %all-to-all-start = ((f32[32,72,128]{2,1,0:T(8,128)}), f32[32,72,128]{2,1,0:T(8,128)S(1)}, u32[]{:S(2)}, u32[]{:S(2)}) async-start(f32[32,72,128]{2,1,0:T(8,128)} %shard_map.82), calls=%async_computation | async-start | bytes 2359296 | tf_op jit(solution)/shard_map/all_to_all | solution.py:227
  66.1 22.8 %copy-start.1 = (bf16[2,256,256]{2,1,0:T(8,128)(2,1)S(1)}, bf16[2,256,256]{2,1,0:T(8,128)(2,1)}, u32[]{:S(2)}) copy-start(bf16[2,256,256]{2,1,0:T(8,128)(2,1)} %constant.53.clone.table_y_back) | copy-start | bytes 786436
  66.1 22.8 %copy-start.2 = (bf16[2,256,256]{2,1,0:T(8,128)(2,1)S(1)}, bf16[2,256,256]{2,1,0:T(8,128)(2,1)}, u32[]{:S(2)}) copy-start(bf16[2,256,256]{2,1,0:T(8,128)(2,1)} %constant.54.clone.table_z_back) | copy-start | bytes 786436
  91.6 19.5 %collective-permute-start.4 = (f32[2,64,128]{2,1,0:T(8,128)S(1)}, f32[2,64,128]{2,1,0:T(8,128)S(1)}, u32[]{:S(2)}, u32[]{:S(2)}) collective-permute-start(f32[2,64,128]{2,1,0:T(8,128)S(1)} %get-tuple-element.11), channel_id=1, source_target_pairs={{0,64},{32,96},{64,128},{96,160},{128,192},{160,224},{192,256},{22... | collective-permute-start | bytes 196616 | tf_op jit(solution)/shard_map/ppermute | solution.py:217
  98.8 12.3 %collective-permute-start.5 = (f32[2,64,128]{2,1,0:T(8,128)S(1)}, f32[2,64,128]{2,1,0:T(8,128)S(1)}, u32[]{:S(2)}, u32[]{:S(2)}) collective-permute-start(f32[2,64,128]{2,1,0:T(8,128)S(1)} %get-tuple-element.12), channel_id=1, source_target_pairs={{0,416},{32,448},{64,480},{96,0},{128,32},{160,64},{192,96},{224,1... | collective-permute-start | bytes 196616 | tf_op jit(solution)/shard_map/ppermute | solution.py:217
  101.9 14.7 %collective-permute-start.6 = (f32[2,64,128]{2,1,0:T(8,128)S(1)}, f32[2,64,128]{2,1,0:T(8,128)S(1)}, u32[]{:S(2)}, u32[]{:S(2)}) collective-permute-start(f32[2,64,128]{2,1,0:T(8,128)S(1)} %get-tuple-element.13), channel_id=1, source_target_pairs={{0,384},{32,416},{64,448},{96,480},{128,0},{160,32},{192,64},{224,... | collective-permute-start | bytes 196616 | tf_op jit(solution)/shard_map/ppermute | solution.py:217
  107.7 9.8 %collective-permute-start.7 = (f32[2,64,128]{2,1,0:T(8,128)S(1)}, f32[2,64,128]{2,1,0:T(8,128)S(1)}, u32[]{:S(2)}, u32[]{:S(2)}) collective-permute-start(f32[2,64,128]{2,1,0:T(8,128)S(1)} %get-tuple-element.14), channel_id=1, source_target_pairs={{0,128},{32,160},{64,192},{96,224},{128,256},{160,288},{192,320},{... | collective-permute-start | bytes 196616 | tf_op jit(solution)/shard_map/ppermute | solution.py:217

commit v2 on v1

v2 whole, which is shorter than its diff:
```python
import jax
import jax.numpy as jnp
import ml_dtypes
import numpy as np
from jax import lax
from jax.experimental import pallas as pl
from jax.experimental.pallas import tpu as pltpu
from jax.sharding import PartitionSpec as P

N = 64
CELLS = N * N * N
LANES = 2 * N
PEERS = 32
UNITS = 9
ROWS = 8 * UNITS

NEAR = (2, -3)
FAR = (4, -4)
MEETINGS = ((4, 2), (0, 1), (2, 0), (4, 0), (2, 1), (4, 1), (2, 3))
OPPOSITE = (4, 3)


def wave_parts(rows, columns):
    angle = 2.0 * np.pi / N * ((rows * columns) % N)
    return np.cos(angle), np.sin(angle)


def split_table(table):
    high = table.astype(ml_dtypes.bfloat16)
    low = (table - high.astype(np.float64)).astype(ml_dtypes.bfloat16)
    return np.stack([high, low])


def tables():
    index = np.arange(N)
    cosine, sine = wave_parts(index[:, None], index[None, :])
    turn = np.stack([np.stack([cosine, sine]), np.stack([-sine, cosine])])
    two = np.eye(2)
    along_z = np.einsum("oikz,ab->iazobk", turn, two).reshape(256, 256)
    along_y = np.einsum("oiky,ab->kaoiby", turn, two)
    along_y = along_y.reshape(32, 2, 2, 2, 2, 2, N).transpose(0, 2, 3, 1, 5, 4, 6)
    along_y = along_y.reshape(256, 256)
    along_x = np.einsum("oikx,ab->oakxib", turn, two).reshape(256, 256)
    return [split_table(t) for t in (along_z, along_y, along_x, along_x.T, along_y.T, along_z.T)]


def halves(value):
    high = value.astype(jnp.bfloat16)
    low = (value - high.astype(jnp.float32)).astype(jnp.bfloat16)
    return high, low


def dot(left, right):
    return jnp.dot(left, right, preferred_element_type=jnp.float32)


def times_table(value, table):
    high, low = halves(value)
    return dot(high, table[0]) + dot(low, table[0]) + dot(high, table[1])


def table_times(table, value):
    high, low = halves(value)
    return dot(table[0], high) + dot(table[0], low) + dot(table[1], high)


def swap(value):
    return pltpu.roll(value, N, 1)


def block_reader(own, near, far):
    half = 2 * lax.axis_index("pool")

    def read(place, plane):
        if place == 0:
            return own[half + plane]
        return (near, far)[(place - 1) // 2][(place - 1) % 2 * 4 + half + plane]

    return read


def first_side():
    return lax.axis_index("band") < 8


def forward_kernel(own, near, far, table_z_far, table_y_far, out, table_z, table_y, arrived):
    copies = [
        pltpu.make_async_copy(source, target, arrived.at[at])
        for at, (source, target) in enumerate(((table_z_far, table_z), (table_y_far, table_y)))
    ]
    for copy in copies:
        copy.start()
    read = block_reader(own, near, far)

    def unit(number, plane):
        if number < 14:
            left, right = MEETINGS[number // 2]
            right = read(right, plane)
            return read(left, plane) * (swap(right) if number % 2 else right)
        if number == 14:
            return read(0, plane) * read(0, plane)
        if number == 15:
            return read(0, plane) * swap(read(0, plane))
        if number == 16:
            left, right = OPPOSITE
            right = read(right, plane)
            return read(left, plane) * jnp.where(first_side(), right, swap(right))
        return jnp.zeros((N, LANES), jnp.float32)

    for copy in copies:
        copy.wait()
    for u in range(UNITS):
        density = jnp.concatenate(
            [
                jnp.concatenate([unit(2 * u, plane), unit(2 * u + 1, plane)], axis=1)
                for plane in range(2)
            ],
            axis=0,
        )
        rows = times_table(density, table_z)
        rows = jnp.concatenate(
            [
                rows[plane * N : plane * N + N, part * LANES : part * LANES + LANES]
                for plane in range(2)
                for part in range(2)
            ],
            axis=0,
        )
        out[:, 8 * u : 8 * u + 8, :] = table_times(table_y, rows).reshape(PEERS, 8, LANES)


def middle_kernel(spectra, kernel, table_x, table_x_back, out):
    at = pl.multiple_of(lax.axis_index("pool") * LANES, LANES)
    mine = kernel[:, pl.ds(at, LANES)] * (-1.0 / CELLS)
    turned = swap(mine)
    low = lax.broadcasted_iota(jnp.int32, (N, LANES), 1) < N
    even, odd = jnp.where(low, mine, turned), jnp.where(low, turned, mine)
    coulomb = jnp.concatenate([even, odd, even, odd], axis=0)
    for u in range(UNITS):
        rows = spectra[:, 8 * u : 8 * u + 8, :].reshape(256, LANES)
        rows = table_times(table_x, rows) * coulomb
        out[:, 8 * u : 8 * u + 8, :] = table_times(table_x_back, rows).reshape(PEERS, 8, LANES)


def backward_kernel(
    returned, own, near, far, table_y_back, table_z_back, own_field, near_fields, far_fields
):
    read = block_reader(own, near, far)
    started = set()

    def add(place, plane, value):
        if place == 0:
            field, at = own_field, (plane,)
        else:
            field, at = (near_fields, far_fields)[(place - 1) // 2], ((place - 1) % 2, plane)
        if (place, plane) in started:
            field[at] += value
        else:
            started.add((place, plane))
            field[at] = value

    def collect(number, plane, potential):
        if number < 14:
            left, right = MEETINGS[number // 2]
            if number % 2:
                add(left, plane, potential * swap(read(right, plane)))
                add(right, plane, swap(potential * read(left, plane)))
            else:
                add(left, plane, potential * read(right, plane))
                add(right, plane, potential * read(left, plane))
        elif number == 14:
            add(0, plane, potential * read(0, plane))
        elif number == 15:
            add(0, plane, potential * swap(read(0, plane)))
        elif number == 16:
            left, right = OPPOSITE
            partner = read(right, plane)
            add(left, plane, potential * jnp.where(first_side(), partner, swap(partner)))
            given = potential * read(left, plane)
            add(right, plane, jnp.where(first_side(), given, swap(given)))

    for u in range(UNITS):
        rows = returned[:, 8 * u : 8 * u + 8, :].reshape(256, LANES)
        rows = table_times(table_y_back, rows)
        rows = jnp.concatenate(
            [
                jnp.concatenate(
                    [
                        rows[plane * LANES + part * N : plane * LANES + part * N + N]
                        for part in range(2)
                    ],
                    axis=1,
                )
                for plane in range(2)
            ],
            axis=0,
        )
        rows = times_table(rows, table_z_back)
        for plane in range(2):
            for half in range(2):
                collect(
                    2 * u + half,
                    plane,
                    rows[plane * N : plane * N + N, half * LANES : half * LANES + LANES],
                )


VMEM = pl.BlockSpec(memory_space=pltpu.VMEM)
ANY = pl.BlockSpec(memory_space=pl.ANY)
PARAMS = pltpu.CompilerParams(vmem_limit_bytes=32 * 1024 * 1024)
CHUNKS = jax.ShapeDtypeStruct((PEERS, ROWS, LANES), jnp.float32)
FIELD = jax.ShapeDtypeStruct((2, N, LANES), jnp.float32)
FIELDS = jax.ShapeDtypeStruct((2, 2, N, LANES), jnp.float32)
TABLE = pltpu.VMEM((2, 256, 256), jnp.bfloat16)


def forward(own, near, far, table_z, table_y):
    return pl.pallas_call(
        forward_kernel,
        out_shape=CHUNKS,
        in_specs=[VMEM] * 3 + [ANY] * 2,
        out_specs=VMEM,
        scratch_shapes=[TABLE, TABLE, pltpu.SemaphoreType.DMA((2,))],
        compiler_params=PARAMS,
    )(own, near, far, table_z, table_y)


def middle(spectra, kernel, table_x, table_x_back):
    return pl.pallas_call(
        middle_kernel,
        out_shape=CHUNKS,
        in_specs=[VMEM] * 4,
        out_specs=VMEM,
        compiler_params=PARAMS,
    )(spectra, kernel, table_x, table_x_back)


def backward(returned, own, near, far, table_y_back, table_z_back):
    return pl.pallas_call(
        backward_kernel,
        out_shape=[FIELD, FIELDS, FIELDS],
        in_specs=[VMEM] * 6,
        out_specs=[VMEM] * 3,
        compiler_params=PARAMS,
    )(returned, own, near, far, table_y_back, table_z_back)


def along_band(value, steps):
    count = lax.axis_size("band")
    pairs = [
        (2 * source + core, 2 * ((source + steps[core]) % count) + core)
        for source in range(count)
        for core in range(2)
    ]
    return lax.ppermute(value, ("band", "pool"), pairs)


def both_cores(value):
    return lax.all_gather(value, "pool", tiled=True)


def exchange(value):
    return lax.all_to_all(value, ("fft", "pool"), split_axis=0, concat_axis=0, tiled=True)


def send_home(fields, steps, pool_at):
    halves_of = both_cores(fields).reshape(2, 2, 2, N, LANES)
    mine = lax.dynamic_index_in_dim(halves_of, pool_at, 1, keepdims=False)
    return along_band(mine.reshape(4, N, LANES), steps)


def local(orbitals, kernel):
    pool_at = lax.axis_index("pool")
    table_z, table_y, table_x, table_x_back, table_y_back, table_z_back = [
        jnp.asarray(t) for t in tables()
    ]
    own = orbitals.reshape(2, 4, N, N).transpose(1, 2, 0, 3).reshape(4, N, LANES)
    near = both_cores(along_band(own, [-s for s in NEAR]))
    far = both_cores(along_band(own, [-s for s in FAR]))
    spectra = exchange(forward(own, near, far, table_z, table_y))
    returned = exchange(middle(spectra, kernel, table_x, table_x_back))
    own_field, near_fields, far_fields = backward(
        returned, own, near, far, table_y_back, table_z_back
    )
    total = send_home(near_fields, NEAR, pool_at) + send_home(far_fields, FAR, pool_at)
    placed = jnp.where(
        (jnp.arange(2) == pool_at).reshape(2, 1, 1, 1), own_field[None], 0.0
    ).reshape(4, N, LANES)
    both = both_cores(total + placed).reshape(2, 4, N, LANES)
    field = both[0] + both[1]
    return field.reshape(4, N, 2, N).transpose(2, 0, 1, 3).reshape(2, 4, N * N)


def solution(mesh):
    return jax.shard_map(
        local,
        mesh=mesh,
        in_specs=(P("band", "fft", None), P(None, "fft")),
        out_specs=P("band", "fft", None),
        check_vma=False,
    )
```

time: 124 us -> 111 us (0.90)
  starting transfers between devices: 52.3 us -> 28.4 us
  blocking collectives: 27.6 us -> 43 us
  waiting for transfers between devices: 27.9 us -> 25 us
  local copies, waits for them, and re-layouts: 4.58 us -> 2.74 us
    ppermute x8 -> x4, starting transfers between devices: 42.9 us -> 24.3 us  [along_band(): return lax.ppermute(value, ('band', 'pool'), pairs)]
    all_gather x1 -> x5, blocking collectives: 4.77 us -> 17.2 us  [both_cores(): return lax.all_gather(value, 'pool', tiled=True)]
    all_to_all x1, starting transfers between devices: 9.41 us -> 4.12 us  [exchange(): lax.all_to_all(value, ('fft', 'pool'), split_axis=0, concat_axis=0, tiled...]
    ppermute x8 -> x4, waiting for transfers between devices: 9.92 us -> 6.51 us  [along_band(): return lax.ppermute(value, ('band', 'pool'), pairs)]
    all_to_all x1, blocking collectives: 22.8 us -> 25.8 us  [exchange(): lax.all_to_all(value, ('fft', 'pool'), split_axis=0, concat_axis=0, tiled...]
    unnamed x16 -> x14, local copies, waits for them, and re-layouts: 2.83 us -> 0.03 us
  transfers between devices with their start and end apart: 9 -> 5, of which waited for: 4 -> 4; matrix products, arithmetic and copies ran while one was open for 0% -> 0% of each run, Pallas kernels for 0% -> 0%
where the time goes in v2:
time: 111 us; the launch traced here: 110 us
  blocking collectives  43 us (39%)
  starting transfers between devices  28.4 us (26%)
  waiting for transfers between devices  25 us (23%)
  Pallas kernels  10.6 us (10%)
  local copies, waits for them, and re-layouts  2.74 us (2%)
    all_to_all x1, blocking collectives, exchange(): lax.all_to_all(value, ('fft', 'pool'), split_axis=0, concat_axis=0, tiled...  25.8 us
    ppermute x4, starting transfers between devices, along_band(): return lax.ppermute(value, ('band', 'pool'), pairs)  24.3 us
    all_to_all x1, waiting for transfers between devices, exchange(): lax.all_to_all(value, ('fft', 'pool'), split_axis=0, concat_axis=0, tiled...  18.4 us
    all_gather x5, blocking collectives, both_cores(): return lax.all_gather(value, 'pool', tiled=True)  17.2 us
    ppermute x4, waiting for transfers between devices, along_band(): return lax.ppermute(value, ('band', 'pool'), pairs)  6.51 us
    pallas_call x1, Pallas kernels, middle(): pl.pallas_call(middle_kernel, out_shape=CHUNKS, in_specs=[VMEM] * 4, out_...  4.35 us
    all_to_all x1, starting transfers between devices, exchange(): lax.all_to_all(value, ('fft', 'pool'), split_axis=0, concat_axis=0, tiled...  4.12 us
    pallas_call x1, Pallas kernels, forward(): pl.pallas_call(forward_kernel, out_shape=CHUNKS, in_specs=[VMEM] * 3 + [A...  3.62 us
  transfers between devices with their start and end apart: 5, of which 4 were waited for; matrix products, arithmetic and copies ran while one was open for 0% of the time, Pallas kernels for 0%

profile of v2, /device:TPU:1, one launch (start us, length us, event | category | flops | bytes accessed | tf_op | source)
XLA Modules:
  0.0 110.0 jit_solution(17109560914490626471)
XLA Ops:
  0.0 1.1 %reshape.41 = f32[2,4,64,64]{3,2,1,0:T(8,128)S(1)} reshape(f32[2,4,4096]{2,1,0:T(4,128)} %param.8) | data formatting | bytes 262144 | tf_op jit(solution)/shard_map/reshape | solution.py:277
  1.1 0.2 copy.16
  1.4 0.2 reshape.42.own
  1.5 7.1 %collective-permute-start = (f32[4,64,128]{2,1,0:T(8,128)S(1)}, f32[4,64,128]{2,1,0:T(8,128)S(1)}, u32[]{:S(2)}, u32[]{:S(2)}) collective-permute-start(f32[4,64,128]{2,1,0:T(8,128)S(1)} %reshape.42.own), channel_id=1, source_target_pairs={{0,448},{1,97},{32,480},{33,129},{64,0},{65,161},{96,32},{97,193},... | collective-permute-start | bytes 393224 | tf_op jit(solution)/shard_map/ppermute | solution.py:255
  8.6 8.8 %collective-permute-start.1 = (f32[4,64,128]{2,1,0:T(8,128)S(1)}, f32[4,64,128]{2,1,0:T(8,128)S(1)}, u32[]{:S(2)}, u32[]{:S(2)}) collective-permute-start(f32[4,64,128]{2,1,0:T(8,128)S(1)} %reshape.42.own), channel_id=1, source_target_pairs={{0,384},{1,129},{32,416},{33,161},{64,448},{65,193},{96,480},{97,2... | collective-permute-start | bytes 393224 | tf_op jit(solution)/shard_map/ppermute | solution.py:255
  17.4 0.0 collective-permute-done
  17.5 4.5 %all_gather.15.near = f32[8,64,128]{2,1,0:T(8,128)S(1)} all-gather(f32[4,64,128]{2,1,0:T(8,128)S(1)} %collective-permute-done), channel_id=1, replica_groups=mesh['band'=16,'fft'=16,'pool'=2] {'pool'}, dimensions={0}, use_global_device_ids=true | all-gather | bytes 393216 | tf_op jit(solution)/shard_map/all_gather | solution.py:259
  22.0 1.7 %collective-permute-done.1 = f32[4,64,128]{2,1,0:T(8,128)S(1)} collective-permute-done((f32[4,64,128]{2,1,0:T(8,128)S(1)}, f32[4,64,128]{2,1,0:T(8,128)S(1)}, u32[]{:S(2)}, u32[]{:S(2)}) %collective-permute-start.1) | collective-permute-done | bytes 131104 | tf_op jit(solution)/shard_map/ppermute | solution.py:255
  23.6 5.6 %all_gather.16.far = f32[8,64,128]{2,1,0:T(8,128)S(1)} all-gather(f32[4,64,128]{2,1,0:T(8,128)S(1)} %collective-permute-done.1), channel_id=1, replica_groups=mesh['band'=16,'fft'=16,'pool'=2] {'pool'}, dimensions={0}, use_global_device_ids=true | all-gather | bytes 393216 | tf_op jit(solution)/shard_map/all_gather | solution.py:259
  29.2 3.6 %shard_map.82 = f32[32,72,128]{2,1,0:T(8,128)S(1)} custom-call(f32[4,64,128]{2,1,0:T(8,128)S(1)} %reshape.42.own, f32[8,64,128]{2,1,0:T(8,128)S(1)} %all_gather.15.near, f32[8,64,128]{2,1,0:T(8,128)S(1)} %all_gather.16.far, bf16[2,256,256]{2,1,0:T(8,128)(2,1)S(1)} %copy-done.4, bf16[2,256,256]{2,1,0:T(8,128)(2,1)S(1)} %copy-done.5), custom_call_target="tpu_custom_call" | custom-call | tf_op jit(solution)/shard_map/pallas_call | solution.py:218
  32.8 0.0 copy-start.2
  32.9 0.0 copy-start.3
  32.9 0.0 copy-start.6
  32.9 25.8 %all_to_all.10.spectra = f32[32,72,128]{2,1,0:T(8,128)S(1)} all-to-all(f32[32,72,128]{2,1,0:T(8,128)S(1)} %shard_map.82), channel_id=1, replica_groups=mesh['band'=16,'fft'=16,'pool'=2] {'fft','pool'}, dimensions={0} | all-to-all | bytes 2359296 | tf_op jit(solution)/shard_map/all_to_all | solution.py:263
  58.7 0.0 copy-done.3
  58.7 4.4 %shard_map.83 = f32[32,72,128]{2,1,0:T(8,128)} custom-call(f32[32,72,128]{2,1,0:T(8,128)S(1)} %all_to_all.10.spectra, f32[64,256]{1,0:T(8,128)S(1)} %copy-done.6, bf16[2,256,256]{2,1,0:T(8,128)(2,1)S(1)} %copy-done.2, bf16[2,256,256]{2,1,0:T(8,128)(2,1)S(1)} %copy-done.3), custom_call_target="tpu_custom_call" | custom-call | tf_op jit(solution)/shard_map/pallas_call | solution.py:229
  63.1 4.1 %all-to-all-start.1 = ((f32[32,72,128]{2,1,0:T(8,128)}), f32[32,72,128]{2,1,0:T(8,128)S(1)}, u32[]{:S(2)}, u32[]{:S(2)}) async-start(f32[32,72,128]{2,1,0:T(8,128)} %shard_map.83), calls=%async_computation.1 | async-start | bytes 2359296 | tf_op jit(solution)/shard_map/all_to_all | solution.py:263
  67.2 18.4 %all-to-all-done.1.returned = f32[32,72,128]{2,1,0:T(8,128)S(1)} async-done(((f32[32,72,128]{2,1,0:T(8,128)}), f32[32,72,128]{2,1,0:T(8,128)S(1)}, u32[]{:S(2)}, u32[]{:S(2)}) %all-to-all-start.1) | async-done | bytes 1179680 | tf_op jit(solution)/shard_map/all_to_all | solution.py:263
  85.6 0.0 copy-done
  85.7 2.7 %shard_map.84 = (f32[2,64,128]{2,1,0:T(8,128)S(1)}, f32[2,2,64,128]{3,2,1,0:T(8,128)S(1)}, f32[2,2,64,128]{3,2,1,0:T(8,128)S(1)}) custom-call(f32[32,72,128]{2,1,0:T(8,128)S(1)} %all-to-all-done.1.returned, f32[4,64,128]{2,1,0:T(8,128)S(1)} %reshape.42.own, f32[8,64,128]{2,1,0:T(8,128)S(1)} %all_gather.15.near, f32[8,64,128]{2,1,0:T(8,128)S(1)} %all_gather.16.far, ...), custom_call_target="tpu_custom_call" | custom-call | tf_op jit(solution)/shard_map/pallas_call | solution.py:239
  88.3 2.0 %all_gather.18 = f32[4,2,64,128]{3,2,1,0:T(8,128)S(1)} all-gather(f32[2,2,64,128]{3,2,1,0:T(8,128)S(1)} %get-tuple-element.9), channel_id=1, replica_groups=mesh['band'=16,'fft'=16,'pool'=2] {'pool'}, dimensions={0}, use_global_device_ids=true | all-gather | bytes 393216 | tf_op jit(solution)/shard_map/all_gather | solution.py:259
  90.3 5.6 %collective-permute-start.3 = (f32[4,64,128]{2,1,0:T(8,128)S(1)}, f32[4,64,128]{2,1,0:T(8,128)S(1)}, u32[]{:S(2)}, u32[]{:S(2)}) collective-permute-start(f32[4,64,128]{2,1,0:T(8,128)S(1)} %bitcast.18), channel_id=1, source_target_pairs={{0,128},{1,385},{32,160},{33,417},{64,192},{65,449},{96,224},{97,4... | collective-permute-start | bytes 393224 | tf_op jit(solution)/shard_map/ppermute | solution.py:255
  96.0 2.0 %all_gather.17 = f32[4,2,64,128]{3,2,1,0:T(8,128)S(1)} all-gather(f32[2,2,64,128]{3,2,1,0:T(8,128)S(1)} %get-tuple-element.8), channel_id=1, replica_groups=mesh['band'=16,'fft'=16,'pool'=2] {'pool'}, dimensions={0}, use_global_device_ids=true | all-gather | bytes 393216 | tf_op jit(solution)/shard_map/all_gather | solution.py:259
  98.0 2.8 %collective-permute-start.2 = (f32[4,64,128]{2,1,0:T(8,128)S(1)}, f32[4,64,128]{2,1,0:T(8,128)S(1)}, u32[]{:S(2)}, u32[]{:S(2)}) collective-permute-start(f32[4,64,128]{2,1,0:T(8,128)S(1)} %bitcast.19), channel_id=1, source_target_pairs={{0,64},{1,417},{32,96},{33,449},{64,128},{65,481},{96,160},{97,1},... | collective-permute-start | bytes 393224 | tf_op jit(solution)/shard_map/ppermute | solution.py:255
  100.8 0.1 broadcast_in_dim.27
  100.9 0.1 broadcast_in_dim.28
  100.9 0.9 collective-permute-done.3
  101.8 4.0 %collective-permute-done.2 = f32[4,64,128]{2,1,0:T(8,128)S(1)} collective-permute-done((f32[4,64,128]{2,1,0:T(8,128)S(1)}, f32[4,64,128]{2,1,0:T(8,128)S(1)}, u32[]{:S(2)}, u32[]{:S(2)}) %collective-permute-start.2) | collective-permute-done | bytes 131104 | tf_op jit(solution)/shard_map/ppermute | solution.py:255
  105.8 0.1 fusion
  105.9 3.1 %all_gather.19 = f32[8,64,128]{2,1,0:T(8,128)S(1)} all-gather(f32[4,64,128]{2,1,0:T(8,128)S(1)} %fusion), channel_id=1, replica_groups=mesh['band'=16,'fft'=16,'pool'=2] {'pool'}, dimensions={0}, use_global_device_ids=true | all-gather | bytes 393216 | tf_op jit(solution)/shard_map/all_gather | solution.py:259
  109.0 0.2 add.22
  109.2 0.8 reshape.47
  (14 shorter events, 0.1 us)
Async XLA Ops:
  0.0 29.2 %copy-start.4 = (bf16[2,256,256]{2,1,0:T(8,128)(2,1)S(1)}, bf16[2,256,256]{2,1,0:T(8,128)(2,1)}, u32[]{:S(2)}) copy-start(bf16[2,256,256]{2,1,0:T(8,128)(2,1)} %constant.26.clone.table_z_far) | copy-start | bytes 786436
  0.0 29.2 %copy-start.5 = (bf16[2,256,256]{2,1,0:T(8,128)(2,1)S(1)}, bf16[2,256,256]{2,1,0:T(8,128)(2,1)}, u32[]{:S(2)}) copy-start(bf16[2,256,256]{2,1,0:T(8,128)(2,1)} %constant.27.clone.table_y_far) | copy-start | bytes 786436
  1.5 15.9 %collective-permute-start = (f32[4,64,128]{2,1,0:T(8,128)S(1)}, f32[4,64,128]{2,1,0:T(8,128)S(1)}, u32[]{:S(2)}, u32[]{:S(2)}) collective-permute-start(f32[4,64,128]{2,1,0:T(8,128)S(1)} %reshape.42.own), channel_id=1, source_target_pairs={{0,448},{1,97},{32,480},{33,129},{64,0},{65,161},{96,32},{97,193},... | collective-permute-start | bytes 393224 | tf_op jit(solution)/shard_map/ppermute | solution.py:255
  8.6 15.0 %collective-permute-start.1 = (f32[4,64,128]{2,1,0:T(8,128)S(1)}, f32[4,64,128]{2,1,0:T(8,128)S(1)}, u32[]{:S(2)}, u32[]{:S(2)}) collective-permute-start(f32[4,64,128]{2,1,0:T(8,128)S(1)} %reshape.42.own), channel_id=1, source_target_pairs={{0,384},{1,129},{32,416},{33,161},{64,448},{65,193},{96,480},{97,2... | collective-permute-start | bytes 393224 | tf_op jit(solution)/shard_map/ppermute | solution.py:255
  32.8 25.9 %copy-start.2 = (bf16[2,256,256]{2,1,0:T(8,128)(2,1)S(1)}, bf16[2,256,256]{2,1,0:T(8,128)(2,1)}, u32[]{:S(2)}) copy-start(bf16[2,256,256]{2,1,0:T(8,128)(2,1)} %constant.28.clone.table_x) | copy-start | bytes 786436
  32.9 25.9 %copy-start.3 = (bf16[2,256,256]{2,1,0:T(8,128)(2,1)S(1)}, bf16[2,256,256]{2,1,0:T(8,128)(2,1)}, u32[]{:S(2)}) copy-start(bf16[2,256,256]{2,1,0:T(8,128)(2,1)} %constant.29.clone.table_x_back) | copy-start | bytes 786436
  32.9 25.8 %copy-start.6 = (f32[64,256]{1,0:T(8,128)S(1)}, f32[64,256]{1,0:T(8,128)}, u32[]{:S(2)}) copy-start(f32[64,256]{1,0:T(8,128)} %kernel.1) | copy-start | bytes 196612
  63.1 22.6 %copy-start = (bf16[2,256,256]{2,1,0:T(8,128)(2,1)S(1)}, bf16[2,256,256]{2,1,0:T(8,128)(2,1)}, u32[]{:S(2)}) copy-start(bf16[2,256,256]{2,1,0:T(8,128)(2,1)} %constant.30.clone.table_y_back) | copy-start | bytes 786436
  63.1 22.6 %copy-start.1 = (bf16[2,256,256]{2,1,0:T(8,128)(2,1)S(1)}, bf16[2,256,256]{2,1,0:T(8,128)(2,1)}, u32[]{:S(2)}) copy-start(bf16[2,256,256]{2,1,0:T(8,128)(2,1)} %constant.31.clone.table_z_back) | copy-start | bytes 786436
  63.1 22.6 %all-to-all-start.1 = ((f32[32,72,128]{2,1,0:T(8,128)}), f32[32,72,128]{2,1,0:T(8,128)S(1)}, u32[]{:S(2)}, u32[]{:S(2)}) async-start(f32[32,72,128]{2,1,0:T(8,128)} %shard_map.83), calls=%async_computation.1 | async-start | bytes 2359296 | tf_op jit(solution)/shard_map/all_to_all | solution.py:263
  90.3 11.5 %collective-permute-start.3 = (f32[4,64,128]{2,1,0:T(8,128)S(1)}, f32[4,64,128]{2,1,0:T(8,128)S(1)}, u32[]{:S(2)}, u32[]{:S(2)}) collective-permute-start(f32[4,64,128]{2,1,0:T(8,128)S(1)} %bitcast.18), channel_id=1, source_target_pairs={{0,128},{1,385},{32,160},{33,417},{64,192},{65,449},{96,224},{97,4... | collective-permute-start | bytes 393224 | tf_op jit(solution)/shard_map/ppermute | solution.py:255
  98.0 7.8 %collective-permute-start.2 = (f32[4,64,128]{2,1,0:T(8,128)S(1)}, f32[4,64,128]{2,1,0:T(8,128)S(1)}, u32[]{:S(2)}, u32[]{:S(2)}) collective-permute-start(f32[4,64,128]{2,1,0:T(8,128)S(1)} %bitcast.19), channel_id=1, source_target_pairs={{0,64},{1,417},{32,96},{33,449},{64,128},{65,481},{96,160},{97,1},... | collective-permute-start | bytes 393224 | tf_op jit(solution)/shard_map/ppermute | solution.py:255

commit v3 on v2

v3 whole, which is shorter than its diff:
```python
import jax
import jax.numpy as jnp
import ml_dtypes
import numpy as np
from jax import lax
from jax.experimental import pallas as pl
from jax.experimental.pallas import tpu as pltpu
from jax.sharding import PartitionSpec as P

N = 64
HALF = N // 2
CELLS = N * N * N
LANES = 2 * N
PEERS = 16
UNITS = 4
ROWS = 32 * UNITS + 16

NEAR = (2, -3)
FAR = (4, -4)
MEETINGS = (((0, 1), (0, 2)), ((1, 4), (2, 3)), ((2, 4), (0, 4)), ((1, 2), None))
SQUARES = (0, 0)
OPPOSITE = (4, 3)


def wave_parts(rows, columns):
    angle = 2.0 * np.pi / N * ((rows * columns) % N)
    return np.cos(angle), np.sin(angle)


def split_table(table):
    high = table.astype(ml_dtypes.bfloat16)
    low = (table - high.astype(np.float64)).astype(ml_dtypes.bfloat16)
    return np.stack([high, low])


def tables():
    index = np.arange(N)
    cosine, sine = wave_parts(index[:, None], index[None, :])
    turn = np.stack([np.stack([cosine, sine]), np.stack([-sine, cosine])])
    two = np.eye(2)
    along_z = np.einsum("oikz,ab->iazobk", turn, two).reshape(256, 256)
    along_y = np.einsum("oiky,ab->kaoiby", turn, two)
    along_y = along_y.reshape(PEERS, 2, 2, 2, 2, 2, 2, HALF, 2)
    along_y = along_y.transpose(0, 1, 3, 4, 2, 6, 5, 8, 7).reshape(256, 256)
    along_x = np.einsum("oikx,ab->oakxib", turn, two).reshape(256, 256)
    return [split_table(t) for t in (along_z, along_y, along_x, along_x.T, along_y.T, along_z.T)]


def halves(value):
    high = value.astype(jnp.bfloat16)
    low = (value - high.astype(jnp.float32)).astype(jnp.bfloat16)
    return high, low


def dot(left, right):
    return jnp.dot(left, right, preferred_element_type=jnp.float32)


def times_table(value, table):
    high, low = halves(value)
    return dot(high, table[0]) + dot(low, table[0]) + dot(high, table[1])


def table_times(table, value):
    high, low = halves(value)
    return dot(table[0], high) + dot(table[0], low) + dot(table[1], high)


def swap(value):
    return pltpu.roll(value, N, 1)


def low_lanes(rows):
    return lax.broadcasted_iota(jnp.int32, (rows, LANES), 1) < N


def pick(first, second):
    return jnp.where(lax.axis_index("pool") == 0, first, second)


def places(unit, half):
    first, second = MEETINGS[unit]
    if second is None:
        second = OPPOSITE if half else SQUARES
    return pick(first[0], second[0]), pick(first[1], second[1])


def crossed_there():
    return (lax.axis_index("pool") == 0) | (lax.axis_index("band") >= 8)


def turned(unit, half, value):
    if not half:
        return value
    if MEETINGS[unit][1] is not None:
        return swap(value)
    return jnp.where(crossed_there(), swap(value), value)


def forward_kernel(own, near, far, table_z_far, table_y_far, out, blocks, table_z, table_y, arrived):
    copies = [
        pltpu.make_async_copy(source, target, arrived.at[at])
        for at, (source, target) in enumerate(((table_z_far, table_z), (table_y_far, table_y)))
    ]
    for copy in copies:
        copy.start()
    low = low_lanes(HALF)
    for place, (source, base) in enumerate(((own, 0), (near, 0), (near, 256), (far, 0), (far, 256))):
        for plane in range(4):
            first = source[pl.ds(base + plane, HALF, stride=4), :]
            second = source[pl.ds(base + 128 + plane, HALF, stride=4), :]
            blocks[4 * place + plane, :HALF] = jnp.where(low, first, swap(second))
            blocks[4 * place + plane, HALF:] = jnp.where(low, swap(first), second)

    def density(unit, half, plane):
        left, right = places(unit, half)
        return blocks[4 * left + plane] * turned(unit, half, blocks[4 * right + plane])

    def last_density(half, plane_low):
        if half:
            return jnp.zeros((N, LANES), jnp.float32)
        at, behind = blocks[plane_low], blocks[2 + plane_low]
        return 0.5 * jnp.where(low_lanes(N), at * swap(at), behind * swap(behind))

    def spectrum(halves_of):
        rows = jnp.concatenate(
            [jnp.concatenate([halves_of(0, at), halves_of(1, at)], axis=1) for at in range(2)], axis=0
        )
        rows = times_table(rows, table_z)
        rows = jnp.concatenate(
            [
                rows[at * N : at * N + N, part * LANES : part * LANES + LANES]
                for at in range(2)
                for part in range(2)
            ],
            axis=0,
        )
        return table_times(table_y, rows).reshape(PEERS, 16, LANES)

    for copy in copies:
        copy.wait()
    for u in range(UNITS):
        for high in range(2):
            rows = spectrum(lambda half, at: density(u, half, 2 * high + at))
            at = 32 * u + 8 * high
            out[:, at : at + 8, :] = rows[:, :8]
            out[:, at + 16 : at + 24, :] = rows[:, 8:]
    out[:, 32 * UNITS :, :] = spectrum(last_density)


def middle_kernel(spectra, kernel, table_x, table_x_back, out):
    low = low_lanes(N)
    first, second = (kernel[:, at : at + LANES] * (-1.0 / CELLS) for at in (0, LANES))

    def twice(value):
        other = swap(value)
        return jnp.where(low, value, other), jnp.where(low, other, value)

    def rows_of(pair):
        return jnp.concatenate([*pair, *pair], axis=0)

    def apply(rows, coulomb):
        rows = table_times(table_x, rows.reshape(256, LANES)) * coulomb
        return table_times(table_x_back, rows).reshape(PEERS, 16, LANES)

    coulombs = rows_of(twice(first)), rows_of(twice(second))
    for u in range(UNITS):
        for high in range(2):
            at = 32 * u + 16 * high
            out[:, at : at + 16, :] = apply(spectra[:, at : at + 16, :], coulombs[high])

    def exchanged(one, two):
        wide = lax.broadcasted_iota(jnp.int32, one.shape, 2) < N
        one_other, two_other = pltpu.roll(one, N, 2), pltpu.roll(two, N, 2)
        return jnp.where(wide, one, two_other), jnp.where(wide, one_other, two)

    at = 32 * UNITS
    rows = jnp.concatenate(
        exchanged(spectra[:, at : at + 8, :], spectra[:, at + 8 : at + 16, :]), axis=1
    )
    rows = apply(
        rows, rows_of((jnp.where(low, first, swap(second)), jnp.where(low, swap(first), second)))
    )
    one, two = exchanged(rows[:, :8], rows[:, 8:])
    out[:, at : at + 8, :] = one
    out[:, at + 8 : at + 16, :] = two


def backward_kernel(
    returned, blocks, table_y_back, table_z_back, own_field, near_fields, far_fields, fields
):
    fields[...] = jnp.zeros_like(fields)

    def collect(unit, half, plane, potential):
        left, right = places(unit, half)
        partner = turned(unit, half, blocks[4 * right + plane])
        fields[4 * left + plane] += potential * partner
        given = turned(unit, half, potential * blocks[4 * left + plane])
        if unit == UNITS - 1 and not half:
            given = given * pick(1.0, 0.0)
        fields[4 * right + plane] += given

    def potentials(rows):
        rows = table_times(table_y_back, rows.reshape(256, LANES))
        rows = jnp.concatenate(
            [
                jnp.concatenate(
                    [rows[at * LANES + part * N : at * LANES + part * N + N] for part in range(2)],
                    axis=1,
                )
                for at in range(2)
            ],
            axis=0,
        )
        return times_table(rows, table_z_back)

    for u in range(UNITS):
        for high in range(2):
            at = 32 * u + 8 * high
            rows = potentials(
                jnp.concatenate([returned[:, at : at + 8, :], returned[:, at + 16 : at + 24, :]], axis=1)
            )
            for at in range(2):
                for half in range(2):
                    collect(
                        u,
                        half,
                        2 * high + at,
                        rows[at * N : at * N + N, half * LANES : half * LANES + LANES],
                    )
    rows = potentials(returned[:, 32 * UNITS :, :])
    low = low_lanes(N)
    for at in range(2):
        potential = rows[at * N : at * N + N, :LANES]
        other = swap(potential)
        fields[at] += jnp.where(low, potential, other) * swap(blocks[at])
        fields[2 + at] += jnp.where(low, other, potential) * swap(blocks[2 + at])
    own_field[...] = fields[0:4]
    near_fields[...] = fields[4:12]
    far_fields[...] = fields[12:20]


def final_kernel(both, out):
    low = low_lanes(HALF)
    for plane in range(4):
        even, odd = (
            both[plane, at : at + HALF] + both[4 + plane, at : at + HALF] for at in (0, HALF)
        )
        out[pl.ds(plane, HALF, stride=4), :] = jnp.where(low, even, swap(odd))
        out[pl.ds(128 + plane, HALF, stride=4), :] = jnp.where(low, swap(even), odd)


VMEM = pl.BlockSpec(memory_space=pltpu.VMEM)
ANY = pl.BlockSpec(memory_space=pl.ANY)
PARAMS = pltpu.CompilerParams(vmem_limit_bytes=32 * 1024 * 1024)
CHUNKS = jax.ShapeDtypeStruct((PEERS, ROWS, LANES), jnp.float32)
TABLE = pltpu.VMEM((2, 256, 256), jnp.bfloat16)


def planes(count):
    return jax.ShapeDtypeStruct((count, N, LANES), jnp.float32)


def forward(own, near, far, table_z, table_y):
    return pl.pallas_call(
        forward_kernel,
        out_shape=[CHUNKS, planes(20)],
        in_specs=[VMEM] * 3 + [ANY] * 2,
        out_specs=[VMEM] * 2,
        scratch_shapes=[TABLE, TABLE, pltpu.SemaphoreType.DMA((2,))],
        compiler_params=PARAMS,
    )(own, near, far, table_z, table_y)


def middle(spectra, kernel, table_x, table_x_back):
    return pl.pallas_call(
        middle_kernel,
        out_shape=CHUNKS,
        in_specs=[VMEM] * 4,
        out_specs=VMEM,
        compiler_params=PARAMS,
    )(spectra, kernel, table_x, table_x_back)


def backward(returned, blocks, table_y_back, table_z_back):
    return pl.pallas_call(
        backward_kernel,
        out_shape=[planes(4), planes(8), planes(8)],
        in_specs=[VMEM] * 4,
        out_specs=[VMEM] * 3,
        scratch_shapes=[pltpu.VMEM((20, N, LANES), jnp.float32)],
        compiler_params=PARAMS,
    )(returned, blocks, table_y_back, table_z_back)


def final(both):
    return pl.pallas_call(
        final_kernel,
        out_shape=jax.ShapeDtypeStruct((256, LANES), jnp.float32),
        in_specs=[VMEM],
        out_specs=VMEM,
        compiler_params=PARAMS,
    )(both)


def along_band(value, steps):
    count = lax.axis_size("band")
    pairs = [
        (2 * source + core, 2 * ((source + steps[core]) % count) + core)
        for source in range(count)
        for core in range(2)
    ]
    return lax.ppermute(value, ("band", "pool"), pairs)


def both_cores(value):
    return lax.all_gather(value, "pool", tiled=True)


def exchange(value):
    return lax.all_to_all(value, "fft", split_axis=0, concat_axis=0, tiled=True)


def send_home(fields, steps, pool_at):
    shares = both_cores(fields).reshape(2, 2, 4, N, LANES)
    mine = lax.dynamic_index_in_dim(shares, pool_at, 1, keepdims=False)
    return along_band(mine[0] + mine[1], steps)


def local(orbitals, kernel):
    pool_at = lax.axis_index("pool")
    table_z, table_y, table_x, table_x_back, table_y_back, table_z_back = [
        jnp.asarray(t) for t in tables()
    ]
    own = orbitals.reshape(2, 4, HALF, LANES).transpose(0, 2, 1, 3).reshape(256, LANES)
    near = both_cores(along_band(own, [-s for s in NEAR]))
    far = both_cores(along_band(own, [-s for s in FAR]))
    spectra, blocks = forward(own, near, far, table_z, table_y)
    returned = exchange(middle(exchange(spectra), kernel, table_x, table_x_back))
    own_field, near_fields, far_fields = backward(returned, blocks, table_y_back, table_z_back)
    arrived = send_home(near_fields, NEAR, pool_at) + send_home(far_fields, FAR, pool_at)
    field = final(both_cores(arrived + own_field))
    return field.reshape(2, HALF, 4, LANES).transpose(0, 2, 1, 3).reshape(2, 4, N * N)


def solution(mesh):
    return jax.shard_map(
        local,
        mesh=mesh,
        in_specs=(P("band", "fft", None), P(None, "fft")),
        out_specs=P("band", "fft", None),
        check_vma=False,
    )
```

time: 111 us -> 113 us (1.018)
  waiting for transfers between devices: 25 us -> 21.6 us
  blocking collectives: 43 us -> 45.9 us
  starting transfers between devices: 28.4 us -> 29.9 us
  Pallas kernels: 10.6 us -> 11.9 us
    all_gather x5, blocking collectives: 17.2 us -> 22.1 us  [both_cores(): return lax.all_gather(value, 'pool', tiled=True)]
    unnamed x14 -> x16, local copies, waits for them, and re-layouts: 0.03 us -> 2.83 us
    reshape x4 -> x0, local copies, waits for them, and re-layouts: 2.32 us -> none  [the longest x3 1.53 us: local(): orbitals.reshape(2, 4, N, N).transpose(1, 2, 0, 3).reshape(4, N, LANES)]
    all_to_all x1, blocking collectives: 25.8 us -> 23.8 us  [exchange(): return lax.all_to_all(value, 'fft', split_axis=0, concat_axis=0, tiled=True)]
    all_to_all x1, waiting for transfers between devices: 18.4 us -> 16.5 us  [exchange(): return lax.all_to_all(value, 'fft', split_axis=0, concat_axis=0, tiled=True)]
    ppermute x4, starting transfers between devices: 24.3 us -> 26.1 us  [along_band(): return lax.ppermute(value, ('band', 'pool'), pairs)]
    ppermute x4, waiting for transfers between devices: 6.51 us -> 5.09 us  [along_band(): return lax.ppermute(value, ('band', 'pool'), pairs)]
    pallas_call x2 -> x3, Pallas kernels: 6.29 us -> 7.48 us  [the longest x1 3.85 us: forward(): pl.pallas_call(forward_kernel, out_shape=[CHUNKS, planes(20)], in_specs=[...]
  transfers between devices with their start and end apart: 5 -> 5, of which waited for: 4 -> 3; matrix products, arithmetic and copies ran while one was open for 0% -> 0% of each run, Pallas kernels for 0% -> 0%
where the time goes in v3:
time: 113 us; the launch traced here: 112 us
  blocking collectives  45.9 us (41%)
  starting transfers between devices  29.9 us (26%)
  waiting for transfers between devices  21.6 us (19%)
  Pallas kernels  11.9 us (11%)
  local copies, waits for them, and re-layouts  2.83 us (3%)
    ppermute x4, starting transfers between devices, along_band(): return lax.ppermute(value, ('band', 'pool'), pairs)  26.1 us
    all_to_all x1, blocking collectives, exchange(): return lax.all_to_all(value, 'fft', split_axis=0, concat_axis=0, tiled=True)  23.8 us
    all_gather x5, blocking collectives, both_cores(): return lax.all_gather(value, 'pool', tiled=True)  22.1 us
    all_to_all x1, waiting for transfers between devices, exchange(): return lax.all_to_all(value, 'fft', split_axis=0, concat_axis=0, tiled=True)  16.5 us
    ppermute x4, waiting for transfers between devices, along_band(): return lax.ppermute(value, ('band', 'pool'), pairs)  5.09 us
    pallas_call x1, Pallas kernels, middle(): pl.pallas_call(middle_kernel, out_shape=CHUNKS, in_specs=[VMEM] * 4, out_...  4.43 us
    pallas_call x1, Pallas kernels, forward(): pl.pallas_call(forward_kernel, out_shape=[CHUNKS, planes(20)], in_specs=[...  3.85 us
    all_to_all x1, starting transfers between devices, exchange(): return lax.all_to_all(value, 'fft', split_axis=0, concat_axis=0, tiled=True)  3.83 us
  transfers between devices with their start and end apart: 5, of which 3 were waited for; matrix products, arithmetic and copies ran while one was open for 0% of the time, Pallas kernels for 0%

profile of v3, /device:TPU:1, one launch (start us, length us, event | category | flops | bytes accessed | tf_op | source)
XLA Modules:
  0.0 112.4 jit_solution(7726180390592186805)
XLA Ops:
  0.0 7.1 %collective-permute-start = (f32[256,128]{1,0:T(8,128)}, f32[256,128]{1,0:T(8,128)S(1)}, u32[]{:S(2)}, u32[]{:S(2)}) collective-permute-start(f32[256,128]{1,0:T(8,128)} %bitcast.16), channel_id=1, source_target_pairs={{0,448},{1,97},{32,480},{33,129},{64,0},{65,161},{96,32},{97,193},... | collective-permute-start | bytes 393224 | tf_op jit(solution)/shard_map/ppermute | solution.py:313
  7.1 8.8 %collective-permute-start.1 = (f32[256,128]{1,0:T(8,128)}, f32[256,128]{1,0:T(8,128)S(1)}, u32[]{:S(2)}, u32[]{:S(2)}) collective-permute-start(f32[256,128]{1,0:T(8,128)} %bitcast.17), channel_id=1, source_target_pairs={{0,384},{1,129},{32,416},{33,161},{64,448},{65,193},{96,480},{97,2... | collective-permute-start | bytes 393224 | tf_op jit(solution)/shard_map/ppermute | solution.py:313
  15.9 0.0 collective-permute-done
  15.9 4.5 %all_gather.15.near = f32[512,128]{1,0:T(8,128)S(1)} all-gather(f32[256,128]{1,0:T(8,128)S(1)} %collective-permute-done), channel_id=1, replica_groups=mesh['band'=16,'fft'=16,'pool'=2] {'pool'}, dimensions={0}, use_global_device_ids=true | all-gather | bytes 393216 | tf_op jit(solution)/shard_map/all_gather | solution.py:317
  20.5 1.9 %collective-permute-done.1 = f32[256,128]{1,0:T(8,128)S(1)} collective-permute-done((f32[256,128]{1,0:T(8,128)}, f32[256,128]{1,0:T(8,128)S(1)}, u32[]{:S(2)}, u32[]{:S(2)}) %collective-permute-start.1) | collective-permute-done | bytes 131104 | tf_op jit(solution)/shard_map/ppermute | solution.py:313
  22.3 5.6 %all_gather.16.far = f32[512,128]{1,0:T(8,128)S(1)} all-gather(f32[256,128]{1,0:T(8,128)S(1)} %collective-permute-done.1), channel_id=1, replica_groups=mesh['band'=16,'fft'=16,'pool'=2] {'pool'}, dimensions={0}, use_global_device_ids=true | all-gather | bytes 393216 | tf_op jit(solution)/shard_map/all_gather | solution.py:317
  27.9 0.0 copy-start.4
  27.9 0.9 copy-done.4
  28.8 0.9 copy-done.5
  29.8 0.9 copy-done.6
  30.7 3.8 %shard_map.82 = (f32[16,144,128]{2,1,0:T(8,128)S(1)}, f32[20,64,128]{2,1,0:T(8,128)S(1)}) custom-call(f32[256,128]{1,0:T(8,128)S(1)} %bitcast.18, f32[512,128]{1,0:T(8,128)S(1)} %all_gather.15.near, f32[512,128]{1,0:T(8,128)S(1)} %all_gather.16.far, bf16[2,256,256]{2,1,0:T(8,128)(2,1)S(1)} %copy-done.4, bf16[2,256,256]{2,1,0:T(8,128)(2,1)S(1)} %copy-done.5), custom_call_target="tpu_custom_call" | custom-call | tf_op jit(solution)/shard_map/pallas_call | solution.py:265
  34.6 0.0 copy-start.2
  34.6 0.0 copy-start.3
  34.6 0.0 copy-start.7
  34.6 23.8 %all_to_all.10.spectra = f32[16,144,128]{2,1,0:T(8,128)S(1)} all-to-all(f32[16,144,128]{2,1,0:T(8,128)S(1)} %get-tuple-element.10), channel_id=1, replica_groups=mesh['band'=16,'fft'=16,'pool'=2] {'fft'}, dimensions={0} | all-to-all | bytes 2359296 | tf_op jit(solution)/shard_map/all_to_all | solution.py:321
  58.4 0.0 copy-done.2
  58.4 0.0 copy-done.3
  58.4 0.0 copy-done.7
  58.4 4.4 %shard_map.83 = f32[16,144,128]{2,1,0:T(8,128)} custom-call(f32[16,144,128]{2,1,0:T(8,128)S(1)} %all_to_all.10.spectra, f32[64,256]{1,0:T(8,128)S(1)} %copy-done.7, bf16[2,256,256]{2,1,0:T(8,128)(2,1)S(1)} %copy-done.2, bf16[2,256,256]{2,1,0:T(8,128)(2,1)S(1)} %copy-done.3), custom_call_target="tpu_custom_call" | custom-call | tf_op jit(solution)/shard_map/pallas_call | solution.py:276
  62.8 3.8 %all-to-all-start.1 = ((f32[16,144,128]{2,1,0:T(8,128)}), f32[16,144,128]{2,1,0:T(8,128)S(1)}, u32[]{:S(2)}, u32[]{:S(2)}) async-start(f32[16,144,128]{2,1,0:T(8,128)} %shard_map.83), calls=%async_computation.1 | async-start | bytes 2359296 | tf_op jit(solution)/shard_map/all_to_all | solution.py:321
  66.7 16.5 %all-to-all-done.1.returned = f32[16,144,128]{2,1,0:T(8,128)S(1)} async-done(((f32[16,144,128]{2,1,0:T(8,128)}), f32[16,144,128]{2,1,0:T(8,128)S(1)}, u32[]{:S(2)}, u32[]{:S(2)}) %all-to-all-start.1) | async-done | bytes 1179680 | tf_op jit(solution)/shard_map/all_to_all | solution.py:321
  83.2 0.0 copy-done
  83.2 0.0 copy-done.1
  83.2 2.9 %shard_map.84 = (f32[4,64,128]{2,1,0:T(8,128)S(1)}, f32[8,64,128]{2,1,0:T(8,128)S(1)}, f32[8,64,128]{2,1,0:T(8,128)S(1)}) custom-call(f32[16,144,128]{2,1,0:T(8,128)S(1)} %all-to-all-done.1.returned, f32[20,64,128]{2,1,0:T(8,128)S(1)} %get-tuple-element.11.blocks, bf16[2,256,256]{2,1,0:T(8,128)(2,1)S(1)} %copy-done, bf16[2,256,256]{2,1,0:T(8,128)(2,1)S(1)} %copy-done.1), custom_call_target="tpu_custom_call" | custom-call | tf_op jit(solution)/shard_map/pallas_call | solution.py:286
  86.0 5.2 %all_gather.18 = f32[16,64,128]{2,1,0:T(8,128)S(1)} all-gather(f32[8,64,128]{2,1,0:T(8,128)S(1)} %get-tuple-element.13), channel_id=1, replica_groups=mesh['band'=16,'fft'=16,'pool'=2] {'pool'}, dimensions={0}, use_global_device_ids=true | all-gather | bytes 786432 | tf_op jit(solution)/shard_map/all_gather | solution.py:317
  91.3 5.6 %collective-permute-start.3 = (f32[4,64,128]{2,1,0:T(8,128)S(1)}, f32[4,64,128]{2,1,0:T(8,128)S(1)}, u32[]{:S(2)}, u32[]{:S(2)}) collective-permute-start(f32[4,64,128]{2,1,0:T(8,128)S(1)} %fusion), channel_id=1, source_target_pairs={{0,128},{1,385},{32,160},{33,417},{64,192},{65,449},{96,224},{97,4... | collective-permute-start | bytes 393224 | tf_op jit(solution)/shard_map/ppermute | solution.py:313
  96.9 2.2 %all_gather.17 = f32[16,64,128]{2,1,0:T(8,128)S(1)} all-gather(f32[8,64,128]{2,1,0:T(8,128)S(1)} %get-tuple-element.12), channel_id=1, replica_groups=mesh['band'=16,'fft'=16,'pool'=2] {'pool'}, dimensions={0}, use_global_device_ids=true | all-gather | bytes 786432 | tf_op jit(solution)/shard_map/all_gather | solution.py:317
  99.1 4.6 %collective-permute-start.2 = (f32[4,64,128]{2,1,0:T(8,128)S(1)}, f32[4,64,128]{2,1,0:T(8,128)S(1)}, u32[]{:S(2)}, u32[]{:S(2)}) collective-permute-start(f32[4,64,128]{2,1,0:T(8,128)S(1)} %fusion.1), channel_id=1, source_target_pairs={{0,64},{1,417},{32,96},{33,449},{64,128},{65,481},{96,160},{97,1},... | collective-permute-start | bytes 393224 | tf_op jit(solution)/shard_map/ppermute | solution.py:313
  103.7 0.0 collective-permute-done.3
  103.7 3.2 %collective-permute-done.2 = f32[4,64,128]{2,1,0:T(8,128)S(1)} collective-permute-done((f32[4,64,128]{2,1,0:T(8,128)S(1)}, f32[4,64,128]{2,1,0:T(8,128)S(1)}, u32[]{:S(2)}, u32[]{:S(2)}) %collective-permute-start.2) | collective-permute-done | bytes 131104 | tf_op jit(solution)/shard_map/ppermute | solution.py:313
  107.0 4.7 %all_gather.19.both = f32[8,64,128]{2,1,0:T(8,128)S(1)} all-gather(f32[4,64,128]{2,1,0:T(8,128)S(1)} %add_add_fusion), channel_id=1, replica_groups=mesh['band'=16,'fft'=16,'pool'=2] {'pool'}, dimensions={0}, use_global_device_ids=true | all-gather | bytes 393216 | tf_op jit(solution)/shard_map/all_gather | solution.py:317
  111.6 0.8 shard_map.85
  (7 shorter events, 0.1 us)
Async XLA Ops:
  0.0 15.9 %collective-permute-start = (f32[256,128]{1,0:T(8,128)}, f32[256,128]{1,0:T(8,128)S(1)}, u32[]{:S(2)}, u32[]{:S(2)}) collective-permute-start(f32[256,128]{1,0:T(8,128)} %bitcast.16), channel_id=1, source_target_pairs={{0,448},{1,97},{32,480},{33,129},{64,0},{65,161},{96,32},{97,193},... | collective-permute-start | bytes 393224 | tf_op jit(solution)/shard_map/ppermute | solution.py:313
  7.1 15.2 %collective-permute-start.1 = (f32[256,128]{1,0:T(8,128)}, f32[256,128]{1,0:T(8,128)S(1)}, u32[]{:S(2)}, u32[]{:S(2)}) collective-permute-start(f32[256,128]{1,0:T(8,128)} %bitcast.17), channel_id=1, source_target_pairs={{0,384},{1,129},{32,416},{33,161},{64,448},{65,193},{96,480},{97,2... | collective-permute-start | bytes 393224 | tf_op jit(solution)/shard_map/ppermute | solution.py:313
  27.9 0.9 copy-start.4
  28.8 0.9 copy-start.5
  29.8 0.9 copy-start.6
  34.6 23.8 %copy-start.2 = (bf16[2,256,256]{2,1,0:T(8,128)(2,1)S(1)}, bf16[2,256,256]{2,1,0:T(8,128)(2,1)}, u32[]{:S(2)}) copy-start(bf16[2,256,256]{2,1,0:T(8,128)(2,1)} %constant.26.clone.table_x) | copy-start | bytes 786436
  34.6 23.8 %copy-start.3 = (bf16[2,256,256]{2,1,0:T(8,128)(2,1)S(1)}, bf16[2,256,256]{2,1,0:T(8,128)(2,1)}, u32[]{:S(2)}) copy-start(bf16[2,256,256]{2,1,0:T(8,128)(2,1)} %constant.27.clone.table_x_back) | copy-start | bytes 786436
  34.6 23.8 %copy-start.7 = (f32[64,256]{1,0:T(8,128)S(1)}, f32[64,256]{1,0:T(8,128)}, u32[]{:S(2)}) copy-start(f32[64,256]{1,0:T(8,128)} %kernel.1) | copy-start | bytes 196612
  62.8 20.3 %copy-start = (bf16[2,256,256]{2,1,0:T(8,128)(2,1)S(1)}, bf16[2,256,256]{2,1,0:T(8,128)(2,1)}, u32[]{:S(2)}) copy-start(bf16[2,256,256]{2,1,0:T(8,128)(2,1)} %constant.28.clone.table_y_back) | copy-start | bytes 786436
  62.8 20.3 %copy-start.1 = (bf16[2,256,256]{2,1,0:T(8,128)(2,1)S(1)}, bf16[2,256,256]{2,1,0:T(8,128)(2,1)}, u32[]{:S(2)}) copy-start(bf16[2,256,256]{2,1,0:T(8,128)(2,1)} %constant.29.clone.table_z_back) | copy-start | bytes 786436
  62.8 20.3 %all-to-all-start.1 = ((f32[16,144,128]{2,1,0:T(8,128)}), f32[16,144,128]{2,1,0:T(8,128)S(1)}, u32[]{:S(2)}, u32[]{:S(2)}) async-start(f32[16,144,128]{2,1,0:T(8,128)} %shard_map.83), calls=%async_computation.1 | async-start | bytes 2359296 | tf_op jit(solution)/shard_map/all_to_all | solution.py:321
  91.3 12.4 %collective-permute-start.3 = (f32[4,64,128]{2,1,0:T(8,128)S(1)}, f32[4,64,128]{2,1,0:T(8,128)S(1)}, u32[]{:S(2)}, u32[]{:S(2)}) collective-permute-start(f32[4,64,128]{2,1,0:T(8,128)S(1)} %fusion), channel_id=1, source_target_pairs={{0,128},{1,385},{32,160},{33,417},{64,192},{65,449},{96,224},{97,4... | collective-permute-start | bytes 393224 | tf_op jit(solution)/shard_map/ppermute | solution.py:313
  99.1 7.8 %collective-permute-start.2 = (f32[4,64,128]{2,1,0:T(8,128)S(1)}, f32[4,64,128]{2,1,0:T(8,128)S(1)}, u32[]{:S(2)}, u32[]{:S(2)}) collective-permute-start(f32[4,64,128]{2,1,0:T(8,128)S(1)} %fusion.1), channel_id=1, source_target_pairs={{0,64},{1,417},{32,96},{33,449},{64,128},{65,481},{96,160},{97,1},... | collective-permute-start | bytes 393224 | tf_op jit(solution)/shard_map/ppermute | solution.py:313

commit v4 on v3

--- a/solution.py
+++ b/solution.py
@@ -97,55 +97,61 @@
     return jnp.where(crossed_there(), swap(value), value)
 
 
-def forward_kernel(own, near, far, table_z_far, table_y_far, out, blocks, table_z, table_y, arrived):
-    copies = [
-        pltpu.make_async_copy(source, target, arrived.at[at])
-        for at, (source, target) in enumerate(((table_z_far, table_z), (table_y_far, table_y)))
-    ]
-    for copy in copies:
-        copy.start()
+def unfold(source, base, blocks, place):
     low = low_lanes(HALF)
-    for place, (source, base) in enumerate(((own, 0), (near, 0), (near, 256), (far, 0), (far, 256))):
-        for plane in range(4):
-            first = source[pl.ds(base + plane, HALF, stride=4), :]
-            second = source[pl.ds(base + 128 + plane, HALF, stride=4), :]
-            blocks[4 * place + plane, :HALF] = jnp.where(low, first, swap(second))
-            blocks[4 * place + plane, HALF:] = jnp.where(low, swap(first), second)
-
-    def density(unit, half, plane):
-        left, right = places(unit, half)
-        return blocks[4 * left + plane] * turned(unit, half, blocks[4 * right + plane])
-
-    def last_density(half, plane_low):
+    for plane in range(4):
+        first = source[pl.ds(base + plane, HALF, stride=4), :]
+        second = source[pl.ds(base + 128 + plane, HALF, stride=4), :]
+        blocks[4 * place + plane, :HALF] = jnp.where(low, first, swap(second))
+        blocks[4 * place + plane, HALF:] = jnp.where(low, swap(first), second)
+
+
+def spectrum(halves_of, table_z, table_y):
+    rows = jnp.concatenate(
+        [jnp.concatenate([halves_of(0, at), halves_of(1, at)], axis=1) for at in range(2)], axis=0
+    )
+    rows = times_table(rows, table_z)
+    rows = jnp.concatenate(
+        [
+            rows[at * N : at * N + N, part * LANES : part * LANES + LANES]
+            for at in range(2)
+            for part in range(2)
+        ],
+        axis=0,
+    )
+    return table_times(table_y, rows).reshape(PEERS, 16, LANES)
+
+
+def first_kernel(own, table_z, table_y, blocks, last):
+    unfold(own, 0, blocks, 0)
+
+    def density(half, plane_low):
         if half:
             return jnp.zeros((N, LANES), jnp.float32)
         at, behind = blocks[plane_low], blocks[2 + plane_low]
         return 0.5 * jnp.where(low_lanes(N), at * swap(at), behind * swap(behind))
 
-    def spectrum(halves_of):
-        rows = jnp.concatenate(
-            [jnp.concatenate([halves_of(0, at), halves_of(1, at)], axis=1) for at in range(2)], axis=0
-        )
-        rows = times_table(rows, table_z)
-        rows = jnp.concatenate(
-            [
-                rows[at * N : at * N + N, part * LANES : part * LANES + LANES]
-                for at in range(2)
-                for part in range(2)
-            ],
-            axis=0,
-        )
-        return table_times(table_y, rows).reshape(PEERS, 16, LANES)
-
-    for copy in copies:
-        copy.wait()
+    last[...] = spectrum(density, table_z, table_y)
+
+
+def forward_kernel(own_blocks, last, near, far, table_z, table_y, out, blocks):
+    blocks[:4] = own_blocks[...]
+    unfold(near, 0, blocks, 1)
+    unfold(near, 256, blocks, 2)
+    unfold(far, 0, blocks, 3)
+    unfold(far, 256, blocks, 4)
+    out[:, 32 * UNITS :, :] = last[...]
+
+    def density(unit, half, plane):
+        left, right = places(unit, half)
+        return blocks[4 * left + plane] * turned(unit, half, blocks[4 * right + plane])
+
     for u in range(UNITS):
         for high in range(2):
-            rows = spectrum(lambda half, at: density(u, half, 2 * high + at))
+            rows = spectrum(lambda half, at: density(u, half, 2 * high + at), table_z, table_y)
             at = 32 * u + 8 * high
             out[:, at : at + 8, :] = rows[:, :8]
             out[:, at + 16 : at + 24, :] = rows[:, 8:]
-    out[:, 32 * UNITS :, :] = spectrum(last_density)
 
 
 def middle_kernel(spectra, kernel, table_x, table_x_back, out):
@@ -240,6 +246,12 @@
     far_fields[...] = fields[12:20]
 
 
+def share_kernel(shares, field):
+    at = 4 * lax.axis_index("pool")
+    for plane in range(4):
+        field[plane] = shares[at + plane] + shares[8 + at + plane]
+
+
 def final_kernel(both, out):
     low = low_lanes(HALF)
     for plane in range(4):
@@ -251,25 +263,34 @@
 
 
 VMEM = pl.BlockSpec(memory_space=pltpu.VMEM)
-ANY = pl.BlockSpec(memory_space=pl.ANY)
 PARAMS = pltpu.CompilerParams(vmem_limit_bytes=32 * 1024 * 1024)
 CHUNKS = jax.ShapeDtypeStruct((PEERS, ROWS, LANES), jnp.float32)
-TABLE = pltpu.VMEM((2, 256, 256), jnp.bfloat16)
+LAST = jax.ShapeDtypeStruct((PEERS, 16, LANES), jnp.float32)
 
 
 def planes(count):
     return jax.ShapeDtypeStruct((count, N, LANES), jnp.float32)
 
 
-def forward(own, near, far, table_z, table_y):
+def first(own, table_z, table_y):
+    return pl.pallas_call(
+        first_kernel,
+        out_shape=[planes(4), LAST],
+        in_specs=[VMEM] * 3,
+        out_specs=[VMEM] * 2,
+        compiler_params=PARAMS,
+        cost_estimate=pl.CostEstimate(flops=10**8, bytes_accessed=10**6, transcendentals=0),
+    )(own, table_z, table_y)
+
+
+def forward(own_blocks, last, near, far, table_z, table_y):
     return pl.pallas_call(
         forward_kernel,
         out_shape=[CHUNKS, planes(20)],
-        in_specs=[VMEM] * 3 + [ANY] * 2,
+        in_specs=[VMEM] * 6,
         out_specs=[VMEM] * 2,
-        scratch_shapes=[TABLE, TABLE, pltpu.SemaphoreType.DMA((2,))],
-        compiler_params=PARAMS,
-    )(own, near, far, table_z, table_y)
+        compiler_params=PARAMS,
+    )(own_blocks, last, near, far, table_z, table_y)
 
 
 def middle(spectra, kernel, table_x, table_x_back):
@@ -291,6 +312,16 @@
         scratch_shapes=[pltpu.VMEM((20, N, LANES), jnp.float32)],
         compiler_params=PARAMS,
     )(returned, blocks, table_y_back, table_z_back)
+
+
+def share(fields):
+    return pl.pallas_call(
+        share_kernel,
+        out_shape=planes(4),
+        in_specs=[VMEM],
+        out_specs=VMEM,
+        compiler_params=PARAMS,
+    )(both_cores(fields))
 
 
 def final(both):
@@ -321,25 +352,20 @@
     return lax.all_to_all(value, "fft", split_axis=0, concat_axis=0, tiled=True)
 
 
-def send_home(fields, steps, pool_at):
-    shares = both_cores(fields).reshape(2, 2, 4, N, LANES)
-    mine = lax.dynamic_index_in_dim(shares, pool_at, 1, keepdims=False)
-    return along_band(mine[0] + mine[1], steps)
-
-
 def local(orbitals, kernel):
-    pool_at = lax.axis_index("pool")
     table_z, table_y, table_x, table_x_back, table_y_back, table_z_back = [
         jnp.asarray(t) for t in tables()
     ]
     own = orbitals.reshape(2, 4, HALF, LANES).transpose(0, 2, 1, 3).reshape(256, LANES)
+    far = both_cores(along_band(own, [-s for s in FAR]))
     near = both_cores(along_band(own, [-s for s in NEAR]))
-    far = both_cores(along_band(own, [-s for s in FAR]))
-    spectra, blocks = forward(own, near, far, table_z, table_y)
+    own_blocks, last = first(own, table_z, table_y)
+    spectra, blocks = forward(own_blocks, last, near, far, table_z, table_y)
     returned = exchange(middle(exchange(spectra), kernel, table_x, table_x_back))
     own_field, near_fields, far_fields = backward(returned, blocks, table_y_back, table_z_back)
-    arrived = send_home(near_fields, NEAR, pool_at) + send_home(far_fields, FAR, pool_at)
-    field = final(both_cores(arrived + own_field))
+    far_field = along_band(share(far_fields), FAR)
+    near_field = along_band(share(near_fields), NEAR)
+    field = final(both_cores(far_field + near_field + own_field))
     return field.reshape(2, HALF, 4, LANES).transpose(0, 2, 1, 3).reshape(2, 4, N * N)
 
 

time: 113 us -> 108 us (0.956)
  waiting for transfers between devices: 21.6 us -> 6.93 us
  blocking collectives: 45.9 us -> 59.6 us
  starting transfers between devices: 29.9 us -> 27.3 us
    all_to_all x1 -> x2, blocking collectives: 23.8 us -> 43.8 us  [exchange(): return lax.all_to_all(value, 'fft', split_axis=0, concat_axis=0, tiled=True)]
    all_to_all x1 -> x0, waiting for transfers between devices: 16.5 us -> none  [exchange(): return lax.all_to_all(value, 'fft', split_axis=0, concat_axis=0, tiled=True)]
    all_gather x5, blocking collectives: 22.1 us -> 15.8 us  [both_cores(): return lax.all_gather(value, 'pool', tiled=True)]
    all_to_all x1 -> x0, starting transfers between devices: 3.83 us -> none  [exchange(): return lax.all_to_all(value, 'fft', split_axis=0, concat_axis=0, tiled=True)]
    ppermute x4, waiting for transfers between devices: 5.09 us -> 6.93 us  [along_band(): return lax.ppermute(value, ('band', 'pool'), pairs)]
    ppermute x4, starting transfers between devices: 26.1 us -> 27.3 us  [along_band(): return lax.ppermute(value, ('band', 'pool'), pairs)]
    unnamed x16 -> x18, local copies, waits for them, and re-layouts: 2.83 us -> 2.84 us
  transfers between devices with their start and end apart: 5 -> 4, of which waited for: 3 -> 1; matrix products, arithmetic and copies ran while one was open for 0% -> 0% of each run, Pallas kernels for 0% -> 1%
where the time goes in v4:
time: 108 us
  blocking collectives  59.6 us (55%)
  starting transfers between devices  27.3 us (25%)
  Pallas kernels  11 us (10%)
  waiting for transfers between devices  6.93 us (6%)
  local copies, waits for them, and re-layouts  2.84 us (3%)
    all_to_all x2, blocking collectives, exchange(): return lax.all_to_all(value, 'fft', split_axis=0, concat_axis=0, tiled=True)  43.8 us
    ppermute x4, starting transfers between devices, along_band(): return lax.ppermute(value, ('band', 'pool'), pairs)  27.3 us
    all_gather x5, blocking collectives, both_cores(): return lax.all_gather(value, 'pool', tiled=True)  15.8 us
    ppermute x4, waiting for transfers between devices, along_band(): return lax.ppermute(value, ('band', 'pool'), pairs)  6.93 us
    pallas_call x1, Pallas kernels, middle(): pl.pallas_call(middle_kernel, out_shape=CHUNKS, in_specs=[VMEM] * 4, out_...  3.39 us
    pallas_call x1, Pallas kernels, forward(): pl.pallas_call(forward_kernel, out_shape=[CHUNKS, planes(20)], in_specs=[...  3.31 us
    pallas_call x1, Pallas kernels, backward(): pl.pallas_call(backward_kernel, out_shape=[planes(4), planes(8), planes(8...  2.87 us
    unnamed x18, local copies, waits for them, and re-layouts  2.84 us
  transfers between devices with their start and end apart: 4, of which 1 were waited for; matrix products, arithmetic and copies ran while one was open for 0% of the time, Pallas kernels for 1%

profile of v4, /device:TPU:1, one launch (start us, length us, event | category | flops | bytes accessed | tf_op | source)
XLA Modules:
  0.0 107.9 jit_solution(8257918057628125073)
XLA Ops:
  0.0 9.6 %collective-permute-start.1 = (f32[256,128]{1,0:T(8,128)}, f32[256,128]{1,0:T(8,128)S(1)}, u32[]{:S(2)}, u32[]{:S(2)}) collective-permute-start(f32[256,128]{1,0:T(8,128)} %bitcast.10), channel_id=1, source_target_pairs={{0,384},{1,129},{32,416},{33,161},{64,448},{65,193},{96,480},{97,2... | collective-permute-start | bytes 393224 | tf_op jit(solution)/shard_map/ppermute | solution.py:344
  9.6 6.3 %collective-permute-start = (f32[256,128]{1,0:T(8,128)}, f32[256,128]{1,0:T(8,128)S(1)}, u32[]{:S(2)}, u32[]{:S(2)}) collective-permute-start(f32[256,128]{1,0:T(8,128)} %bitcast.11), channel_id=1, source_target_pairs={{0,448},{1,97},{32,480},{33,129},{64,0},{65,161},{96,32},{97,193},... | collective-permute-start | bytes 393224 | tf_op jit(solution)/shard_map/ppermute | solution.py:344
  15.9 0.0 copy-start
  15.9 0.9 copy-done
  16.9 0.9 copy-done.2
  17.8 0.9 copy-done.7
  18.7 0.7 shard_map.82
  19.4 0.0 collective-permute-done.1
  19.4 4.5 %all_gather.16.far = f32[512,128]{1,0:T(8,128)S(1)} all-gather(f32[256,128]{1,0:T(8,128)S(1)} %collective-permute-done.1), channel_id=1, replica_groups=mesh['band'=16,'fft'=16,'pool'=2] {'pool'}, dimensions={0}, use_global_device_ids=true | all-gather | bytes 393216 | tf_op jit(solution)/shard_map/all_gather | solution.py:348
  23.9 0.0 collective-permute-done
  23.9 2.2 %all_gather.15.near = f32[512,128]{1,0:T(8,128)S(1)} all-gather(f32[256,128]{1,0:T(8,128)S(1)} %collective-permute-done), channel_id=1, replica_groups=mesh['band'=16,'fft'=16,'pool'=2] {'pool'}, dimensions={0}, use_global_device_ids=true | all-gather | bytes 393216 | tf_op jit(solution)/shard_map/all_gather | solution.py:348
  26.2 0.0 copy-done.1
  26.2 3.3 %shard_map.83 = (f32[16,144,128]{2,1,0:T(8,128)S(1)}, f32[20,64,128]{2,1,0:T(8,128)S(1)}) custom-call(f32[4,64,128]{2,1,0:T(8,128)S(1)} %get-tuple-element.12.own_blocks, f32[16,16,128]{2,1,0:T(8,128)S(1)} %get-tuple-element.13.last, f32[512,128]{1,0:T(8,128)S(1)} %all_gather.15.near, f32[512,128]{1,0:T(8,128)S(1)} %all_gather.16.far, ...), custom_call_target="tpu_custom_call" | custom-call | tf_op jit(solution)/shard_map/pallas_call | solution.py:287
  29.5 0.0 copy-start.5
  29.5 0.0 copy-start.6
  29.5 0.0 copy-start.8
  29.5 24.1 %all_to_all.10.spectra = f32[16,144,128]{2,1,0:T(8,128)S(1)} all-to-all(f32[16,144,128]{2,1,0:T(8,128)S(1)} %get-tuple-element.14), channel_id=1, replica_groups=mesh['band'=16,'fft'=16,'pool'=2] {'fft'}, dimensions={0} | all-to-all | bytes 2359296 | tf_op jit(solution)/shard_map/all_to_all | solution.py:352
  53.6 0.0 copy-done.5
  53.6 0.0 copy-done.6
  53.6 3.4 %shard_map.84 = f32[16,144,128]{2,1,0:T(8,128)S(1)} custom-call(f32[16,144,128]{2,1,0:T(8,128)S(1)} %all_to_all.10.spectra, f32[64,256]{1,0:T(8,128)S(1)} %copy-done.8, bf16[2,256,256]{2,1,0:T(8,128)(2,1)S(1)} %copy-done.6, bf16[2,256,256]{2,1,0:T(8,128)(2,1)S(1)} %copy-done.5), custom_call_target="tpu_custom_call" | custom-call | tf_op jit(solution)/shard_map/pallas_call | solution.py:297
  57.0 0.0 copy-start.3
  57.1 0.0 copy-start.4
  57.1 19.7 %all_to_all.11.returned = f32[16,144,128]{2,1,0:T(8,128)S(1)} all-to-all(f32[16,144,128]{2,1,0:T(8,128)S(1)} %shard_map.84), channel_id=1, replica_groups=mesh['band'=16,'fft'=16,'pool'=2] {'fft'}, dimensions={0} | all-to-all | bytes 2359296 | tf_op jit(solution)/shard_map/all_to_all | solution.py:352
  76.8 2.9 %shard_map.85 = (f32[4,64,128]{2,1,0:T(8,128)S(1)}, f32[8,64,128]{2,1,0:T(8,128)S(1)}, f32[8,64,128]{2,1,0:T(8,128)S(1)}) custom-call(f32[16,144,128]{2,1,0:T(8,128)S(1)} %all_to_all.11.returned, f32[20,64,128]{2,1,0:T(8,128)S(1)} %get-tuple-element.15.blocks, bf16[2,256,256]{2,1,0:T(8,128)(2,1)S(1)} %copy-done.4, bf16[2,256,256]{2,1,0:T(8,128)(2,1)S(1)} %copy-done.3), custom_call_target="tpu_custom_call" | custom-call | tf_op jit(solution)/shard_map/pallas_call | solution.py:307
  79.6 4.9 %all_gather.17.shares = f32[16,64,128]{2,1,0:T(8,128)S(1)} all-gather(f32[8,64,128]{2,1,0:T(8,128)S(1)} %get-tuple-element.16), channel_id=1, replica_groups=mesh['band'=16,'fft'=16,'pool'=2] {'pool'}, dimensions={0}, use_global_device_ids=true | all-gather | bytes 786432 | tf_op jit(solution)/shard_map/all_gather | solution.py:348
  84.6 8.0 %collective-permute-start.2 = (f32[4,64,128]{2,1,0:T(8,128)S(1)}, f32[4,64,128]{2,1,0:T(8,128)S(1)}, u32[]{:S(2)}, u32[]{:S(2)}) collective-permute-start(f32[4,64,128]{2,1,0:T(8,128)S(1)} %shard_map.86), channel_id=1, source_target_pairs={{0,128},{1,385},{32,160},{33,417},{64,192},{65,449},{96,224},{97,4... | collective-permute-start | bytes 393224 | tf_op jit(solution)/shard_map/ppermute | solution.py:344
  92.6 2.2 %all_gather.18.shares = f32[16,64,128]{2,1,0:T(8,128)S(1)} all-gather(f32[8,64,128]{2,1,0:T(8,128)S(1)} %get-tuple-element.17), channel_id=1, replica_groups=mesh['band'=16,'fft'=16,'pool'=2] {'pool'}, dimensions={0}, use_global_device_ids=true | all-gather | bytes 786432 | tf_op jit(solution)/shard_map/all_gather | solution.py:348
  94.8 3.4 %collective-permute-start.3 = (f32[4,64,128]{2,1,0:T(8,128)S(1)}, f32[4,64,128]{2,1,0:T(8,128)S(1)}, u32[]{:S(2)}, u32[]{:S(2)}) collective-permute-start(f32[4,64,128]{2,1,0:T(8,128)S(1)} %shard_map.87), channel_id=1, source_target_pairs={{0,64},{1,417},{32,96},{33,449},{64,128},{65,481},{96,160},{97,1},... | collective-permute-start | bytes 393224 | tf_op jit(solution)/shard_map/ppermute | solution.py:344
  98.2 0.0 collective-permute-done.2
  98.2 6.9 %collective-permute-done.3 = f32[4,64,128]{2,1,0:T(8,128)S(1)} collective-permute-done((f32[4,64,128]{2,1,0:T(8,128)S(1)}, f32[4,64,128]{2,1,0:T(8,128)S(1)}, u32[]{:S(2)}, u32[]{:S(2)}) %collective-permute-start.3) | collective-permute-done | bytes 131104 | tf_op jit(solution)/shard_map/ppermute | solution.py:344
  105.1 2.0 %all_gather.19.both = f32[8,64,128]{2,1,0:T(8,128)S(1)} all-gather(f32[4,64,128]{2,1,0:T(8,128)S(1)} %add_add_fusion), channel_id=1, replica_groups=mesh['band'=16,'fft'=16,'pool'=2] {'pool'}, dimensions={0}, use_global_device_ids=true | all-gather | bytes 393216 | tf_op jit(solution)/shard_map/all_gather | solution.py:348
  107.1 0.8 shard_map.88
  (9 shorter events, 0.1 us)
Async XLA Ops:
  0.0 19.4 %collective-permute-start.1 = (f32[256,128]{1,0:T(8,128)}, f32[256,128]{1,0:T(8,128)S(1)}, u32[]{:S(2)}, u32[]{:S(2)}) collective-permute-start(f32[256,128]{1,0:T(8,128)} %bitcast.10), channel_id=1, source_target_pairs={{0,384},{1,129},{32,416},{33,161},{64,448},{65,193},{96,480},{97,2... | collective-permute-start | bytes 393224 | tf_op jit(solution)/shard_map/ppermute | solution.py:344
  9.6 14.3 %collective-permute-start = (f32[256,128]{1,0:T(8,128)}, f32[256,128]{1,0:T(8,128)S(1)}, u32[]{:S(2)}, u32[]{:S(2)}) collective-permute-start(f32[256,128]{1,0:T(8,128)} %bitcast.11), channel_id=1, source_target_pairs={{0,448},{1,97},{32,480},{33,129},{64,0},{65,161},{96,32},{97,193},... | collective-permute-start | bytes 393224 | tf_op jit(solution)/shard_map/ppermute | solution.py:344
  15.9 1.0 copy-start
  16.9 0.9 copy-start.2
  17.8 0.9 copy-start.7
  18.7 7.4 %copy-start.1 = (bf16[2,256,256]{2,1,0:T(8,128)(2,1)S(1)}, bf16[2,256,256]{2,1,0:T(8,128)(2,1)}, u32[]{:S(2)}) copy-start(bf16[2,256,256]{2,1,0:T(8,128)(2,1)} %constant.13.clone.table_y) | copy-start | bytes 786436
  29.5 24.2 %copy-start.5 = (bf16[2,256,256]{2,1,0:T(8,128)(2,1)S(1)}, bf16[2,256,256]{2,1,0:T(8,128)(2,1)}, u32[]{:S(2)}) copy-start(bf16[2,256,256]{2,1,0:T(8,128)(2,1)} %constant.15.clone.table_x_back) | copy-start | bytes 786436
  29.5 24.2 %copy-start.6 = (bf16[2,256,256]{2,1,0:T(8,128)(2,1)S(1)}, bf16[2,256,256]{2,1,0:T(8,128)(2,1)}, u32[]{:S(2)}) copy-start(bf16[2,256,256]{2,1,0:T(8,128)(2,1)} %constant.14.clone.table_x) | copy-start | bytes 786436
  29.5 24.1 %copy-start.8 = (f32[64,256]{1,0:T(8,128)S(1)}, f32[64,256]{1,0:T(8,128)}, u32[]{:S(2)}) copy-start(f32[64,256]{1,0:T(8,128)} %kernel.1) | copy-start | bytes 196612
  57.0 19.7 %copy-start.3 = (bf16[2,256,256]{2,1,0:T(8,128)(2,1)S(1)}, bf16[2,256,256]{2,1,0:T(8,128)(2,1)}, u32[]{:S(2)}) copy-start(bf16[2,256,256]{2,1,0:T(8,128)(2,1)} %constant.17.clone.table_z_back) | copy-start | bytes 786436
  57.1 19.7 %copy-start.4 = (bf16[2,256,256]{2,1,0:T(8,128)(2,1)S(1)}, bf16[2,256,256]{2,1,0:T(8,128)(2,1)}, u32[]{:S(2)}) copy-start(bf16[2,256,256]{2,1,0:T(8,128)(2,1)} %constant.16.clone.table_y_back) | copy-start | bytes 786436
  84.6 13.6 %collective-permute-start.2 = (f32[4,64,128]{2,1,0:T(8,128)S(1)}, f32[4,64,128]{2,1,0:T(8,128)S(1)}, u32[]{:S(2)}, u32[]{:S(2)}) collective-permute-start(f32[4,64,128]{2,1,0:T(8,128)S(1)} %shard_map.86), channel_id=1, source_target_pairs={{0,128},{1,385},{32,160},{33,417},{64,192},{65,449},{96,224},{97,4... | collective-permute-start | bytes 393224 | tf_op jit(solution)/shard_map/ppermute | solution.py:344
  94.8 10.3 %collective-permute-start.3 = (f32[4,64,128]{2,1,0:T(8,128)S(1)}, f32[4,64,128]{2,1,0:T(8,128)S(1)}, u32[]{:S(2)}, u32[]{:S(2)}) collective-permute-start(f32[4,64,128]{2,1,0:T(8,128)S(1)} %shard_map.87), channel_id=1, source_target_pairs={{0,64},{1,417},{32,96},{33,449},{64,128},{65,481},{96,160},{97,1},... | collective-permute-start | bytes 393224 | tf_op jit(solution)/shard_map/ppermute | solution.py:344

commit v5 on v4

v5 whole, which is shorter than its diff:
```python
import jax
import jax.numpy as jnp
import ml_dtypes
import numpy as np
from jax import lax
from jax.experimental import pallas as pl
from jax.experimental.pallas import tpu as pltpu
from jax.sharding import PartitionSpec as P

N = 64
HALF = N // 2
CELLS = N * N * N
LANES = 2 * N
PEERS = 16
UNITS = 4
ROWS = 32 * UNITS + 16

FAR = (-5, 4)
NEAR = (3, -2)
MEETINGS = (((0, 1), (0, 1)), ((0, 2), (0, 2)), ((1, 2), (1, 2)), ((2, 3), (1, 3)))
EIGHT = 2


def wave_parts(rows, columns):
    angle = 2.0 * np.pi / N * ((rows * columns) % N)
    return np.cos(angle), np.sin(angle)


def split_table(table):
    high = table.astype(ml_dtypes.bfloat16)
    low = (table - high.astype(np.float64)).astype(ml_dtypes.bfloat16)
    return np.stack([high, low])


def tables():
    index = np.arange(N)
    cosine, sine = wave_parts(index[:, None], index[None, :])
    turn = np.stack([np.stack([cosine, sine]), np.stack([-sine, cosine])])
    two = np.eye(2)
    along_z = np.einsum("oikz,ab->iazobk", turn, two).reshape(256, 256)
    along_y = np.einsum("oiky,ab->kaoiby", turn, two)
    along_y = along_y.reshape(PEERS, 2, 2, 2, 2, 2, 2, HALF, 2)
    along_y = along_y.transpose(0, 1, 3, 4, 2, 6, 5, 8, 7).reshape(256, 256)
    along_x = np.einsum("oikx,ab->oakxib", turn, two).reshape(256, 256)
    return [split_table(t) for t in (along_z, along_y, along_x, along_x.T, along_y.T, along_z.T)]


def halves(value):
    high = value.astype(jnp.bfloat16)
    low = (value - high.astype(jnp.float32)).astype(jnp.bfloat16)
    return high, low


def dot(left, right):
    return jnp.dot(left, right, preferred_element_type=jnp.float32)


def times_table(value, table):
    high, low = halves(value)
    return dot(high, table[0]) + dot(low, table[0]) + dot(high, table[1])


def table_times(table, value):
    high, low = halves(value)
    return dot(table[0], high) + dot(table[0], low) + dot(table[1], high)


def swap(value):
    return pltpu.roll(value, N, 1)


def low_lanes(rows):
    return lax.broadcasted_iota(jnp.int32, (rows, LANES), 1) < N


def on_first():
    return lax.axis_index("pool") == 0


def pick(first, second):
    return first if first is second else jnp.where(on_first(), first, second)


def places(unit, half):
    first, second = MEETINGS[unit]
    if unit == EIGHT and half:
        first = (0, 0)
    return pick(first[0], second[0]), pick(first[1], second[1])


def turned(unit, half, value):
    if unit == EIGHT:
        late = lax.axis_index("band") >= 8
        crossed = jnp.logical_not(on_first()) if half else on_first() & late
        return jnp.where(crossed, swap(value), value)
    return swap(value) if half else value


def reader(own_blocks, blocks):
    def read(place, plane):
        if isinstance(place, int):
            return blocks[4 * place - 4 + plane] if place else own_blocks[plane]
        return blocks[4 * place - 4 + plane]

    return read


def unfold(source, base, blocks, place):
    low = low_lanes(HALF)
    for plane in range(4):
        first = source[pl.ds(base + plane, HALF, stride=4), :]
        second = source[pl.ds(base + 128 + plane, HALF, stride=4), :]
        blocks[4 * place + plane, :HALF] = jnp.where(low, first, swap(second))
        blocks[4 * place + plane, HALF:] = jnp.where(low, swap(first), second)


def first_kernel(own, blocks):
    unfold(own, 0, blocks, 0)


def spectrum(density, table_z, table_y):
    rows = times_table(jnp.concatenate(density, axis=0), table_z)
    pairs = [
        jnp.concatenate(
            [
                rows[base + at * N : base + at * N + N, part * LANES : part * LANES + LANES]
                for at in range(2)
                for part in range(2)
            ],
            axis=0,
        )
        for base in range(0, rows.shape[0], LANES)
    ]
    rows = jnp.concatenate(pairs, axis=1)
    return table_times(table_y, rows).reshape(PEERS, 16, rows.shape[1])


def forward_kernel(own_blocks, far, near, table_z, table_y, out, blocks):
    core = lax.axis_index("pool")
    unfold(far, 256 * core, blocks, 0)
    unfold(near, 0, blocks, 1)
    unfold(far, 256 * (1 - core), blocks, 2)
    read = reader(own_blocks, blocks)

    def density(unit, half, plane):
        left, right = places(unit, half)
        if unit == EIGHT and half:
            left = jnp.where(on_first(), read(0, plane), read(1, plane))
            right = jnp.where(on_first(), read(0, plane), swap(read(2, plane)))
            return left * right
        return read(left, plane) * turned(unit, half, read(right, plane))

    for u in range(UNITS):
        rows = spectrum(
            [
                jnp.concatenate([density(u, 0, plane), density(u, 1, plane)], axis=1)
                for plane in range(4)
            ],
            table_z,
            table_y,
        )
        for ky_high in range(2):
            for high in range(2):
                at = 32 * u + 16 * ky_high + 8 * high
                out[:, at : at + 8, :] = rows[
                    :, 8 * ky_high : 8 * ky_high + 8, LANES * high : LANES * high + LANES
                ]

    last = []
    for at, behind in ((own_blocks[0], own_blocks[2]), (own_blocks[1], own_blocks[3])):
        pairs = 0.5 * jnp.where(low_lanes(N), at * swap(at), behind * swap(behind))
        last.append(jnp.concatenate([pairs, jnp.zeros((N, LANES), jnp.float32)], axis=1))
    out[:, 32 * UNITS :, :] = spectrum(last, table_z, table_y)


def middle_kernel(spectra, kernel, table_x, table_x_back, out):
    low = low_lanes(N)
    first, second = (kernel[:, at : at + LANES] * (-1.0 / CELLS) for at in (0, LANES))

    def twice(value):
        other = swap(value)
        return jnp.where(low, value, other), jnp.where(low, other, value)

    def rows_of(pair):
        return jnp.concatenate([*pair, *pair], axis=0)

    def apply(rows, coulomb):
        return table_times(table_x_back, table_times(table_x, rows) * coulomb)

    coulombs = jnp.concatenate([rows_of(twice(first)), rows_of(twice(second))], axis=1)
    for u in range(UNITS):
        starts = 32 * u, 32 * u + 16
        rows = jnp.concatenate(
            [spectra[:, at : at + 16, :].reshape(256, LANES) for at in starts], axis=1
        )
        rows = apply(rows, coulombs)
        for part, at in enumerate(starts):
            out[:, at : at + 16, :] = rows[:, part * LANES : part * LANES + LANES].reshape(
                PEERS, 16, LANES
            )

    def exchanged(one, two):
        wide = lax.broadcasted_iota(jnp.int32, one.shape, 2) < N
        one_other, two_other = pltpu.roll(one, N, 2), pltpu.roll(two, N, 2)
        return jnp.where(wide, one, two_other), jnp.where(wide, one_other, two)

    at = 32 * UNITS
    rows = jnp.concatenate(
        exchanged(spectra[:, at : at + 8, :], spectra[:, at + 8 : at + 16, :]), axis=1
    )
    rows = apply(
        rows.reshape(256, LANES),
        rows_of((jnp.where(low, first, swap(second)), jnp.where(low, swap(first), second))),
    ).reshape(PEERS, 16, LANES)
    one, two = exchanged(rows[:, :8], rows[:, 8:])
    out[:, at : at + 8, :] = one
    out[:, at + 8 : at + 16, :] = two


def backward_kernel(
    returned,
    own_blocks,
    blocks,
    table_y_back,
    table_z_back,
    own_field,
    far_field,
    near_field,
    other_field,
    fields,
):
    fields[...] = jnp.zeros_like(fields)
    read = reader(own_blocks, blocks)

    def collect(unit, half, plane, potential):
        if unit == EIGHT and half:
            first = on_first()
            partner = jnp.where(first, read(0, plane), swap(read(2, plane)))
            mine = potential * partner
            fields[plane] += jnp.where(first, mine, 0.0)
            fields[4 + plane] += jnp.where(first, 0.0, mine)
            given = swap(potential * read(1, plane))
            fields[8 + plane] += jnp.where(first, 0.0, given)
            return
        left, right = places(unit, half)
        fields[4 * left + plane] += potential * turned(unit, half, read(right, plane))
        fields[4 * right + plane] += turned(unit, half, potential * read(left, plane))

    def potentials(pairs):
        rows = table_times(table_y_back, jnp.concatenate(pairs, axis=1))
        planes_of = [
            jnp.concatenate(
                [
                    rows[
                        at * LANES + part * N : at * LANES + part * N + N,
                        high * LANES : high * LANES + LANES,
                    ]
                    for part in range(2)
                ],
                axis=1,
            )
            for high in range(len(pairs))
            for at in range(2)
        ]
        return times_table(jnp.concatenate(planes_of, axis=0), table_z_back)

    for u in range(UNITS):
        pairs = []
        for high in range(2):
            at = 32 * u + 8 * high
            both = [returned[:, at : at + 8, :], returned[:, at + 16 : at + 24, :]]
            pairs.append(jnp.concatenate(both, axis=1).reshape(256, LANES))
        rows = potentials(pairs)
        for plane in range(4):
            for half in range(2):
                collect(
                    u,
                    half,
                    plane,
                    rows[plane * N : plane * N + N, half * LANES : half * LANES + LANES],
                )
    rows = potentials([returned[:, 32 * UNITS :, :].reshape(256, LANES)])
    low = low_lanes(N)
    for at in range(2):
        potential = rows[at * N : at * N + N, :LANES]
        other = swap(potential)
        fields[at] += jnp.where(low, potential, other) * swap(own_blocks[at])
        fields[2 + at] += jnp.where(low, other, potential) * swap(own_blocks[2 + at])
    for place, field in enumerate((own_field, far_field, near_field, other_field)):
        field[...] = fields[4 * place : 4 * place + 4]


def share_kernel(mine, others, field):
    at = 4 * (1 - lax.axis_index("pool"))
    for plane in range(4):
        field[plane] = mine[plane] + others[at + plane]


def final_kernel(both, out):
    low = low_lanes(HALF)
    for plane in range(4):
        even, odd = (
            both[plane, at : at + HALF] + both[4 + plane, at : at + HALF] for at in (0, HALF)
        )
        out[pl.ds(plane, HALF, stride=4), :] = jnp.where(low, even, swap(odd))
        out[pl.ds(128 + plane, HALF, stride=4), :] = jnp.where(low, swap(even), odd)


VMEM = pl.BlockSpec(memory_space=pltpu.VMEM)
PARAMS = pltpu.CompilerParams(vmem_limit_bytes=32 * 1024 * 1024)
CHUNKS = jax.ShapeDtypeStruct((PEERS, ROWS, LANES), jnp.float32)


def planes(count):
    return jax.ShapeDtypeStruct((count, N, LANES), jnp.float32)


def first(own):
    return pl.pallas_call(
        first_kernel,
        out_shape=planes(4),
        in_specs=[VMEM],
        out_specs=VMEM,
        compiler_params=PARAMS,
        cost_estimate=pl.CostEstimate(flops=10**10, bytes_accessed=10**6, transcendentals=0),
    )(own)


def forward(own_blocks, far, near, table_z, table_y):
    return pl.pallas_call(
        forward_kernel,
        out_shape=[CHUNKS, planes(12)],
        in_specs=[VMEM] * 5,
        out_specs=[VMEM] * 2,
        compiler_params=PARAMS,
    )(own_blocks, far, near, table_z, table_y)


def middle(spectra, kernel, table_x, table_x_back):
    return pl.pallas_call(
        middle_kernel,
        out_shape=CHUNKS,
        in_specs=[VMEM] * 4,
        out_specs=VMEM,
        compiler_params=PARAMS,
    )(spectra, kernel, table_x, table_x_back)


def backward(returned, own_blocks, blocks, table_y_back, table_z_back):
    return pl.pallas_call(
        backward_kernel,
        out_shape=[planes(4)] * 4,
        in_specs=[VMEM] * 5,
        out_specs=[VMEM] * 4,
        scratch_shapes=[pltpu.VMEM((16, N, LANES), jnp.float32)],
        compiler_params=PARAMS,
    )(returned, own_blocks, blocks, table_y_back, table_z_back)


def share(mine, others):
    return pl.pallas_call(
        share_kernel,
        out_shape=planes(4),
        in_specs=[VMEM] * 2,
        out_specs=VMEM,
        compiler_params=PARAMS,
    )(mine, others)


def final(both):
    return pl.pallas_call(
        final_kernel,
        out_shape=jax.ShapeDtypeStruct((256, LANES), jnp.float32),
        in_specs=[VMEM],
        out_specs=VMEM,
        compiler_params=PARAMS,
    )(both)


def along_band(value, steps):
    count = lax.axis_size("band")
    pairs = [
        (2 * source + core, 2 * ((source + steps[core]) % count) + core)
        for source in range(count)
        for core in range(2)
    ]
    return lax.ppermute(value, ("band", "pool"), pairs)


def both_cores(value):
    return lax.all_gather(value, "pool", tiled=True)


def exchange(value):
    return lax.all_to_all(value, "fft", split_axis=0, concat_axis=0, tiled=True)


def local(orbitals, kernel):
    table_z, table_y, table_x, table_x_back, table_y_back, table_z_back = [
        jnp.asarray(t) for t in tables()
    ]
    own = orbitals.reshape(2, 4, HALF, LANES).transpose(0, 2, 1, 3).reshape(256, LANES)
    far = both_cores(along_band(own, [-s for s in FAR]))
    near = along_band(own, [-s for s in NEAR])
    own_blocks = first(own)
    spectra, blocks = forward(own_blocks, far, near, table_z, table_y)
    returned = exchange(middle(exchange(spectra), kernel, table_x, table_x_back))
    own_field, far_field, near_field, other_field = backward(
        returned, own_blocks, blocks, table_y_back, table_z_back
    )
    near_field = along_band(near_field, NEAR)
    far_field = along_band(share(far_field, both_cores(other_field)), FAR)
    field = final(both_cores(far_field + near_field + own_field))
    return field.reshape(2, HALF, 4, LANES).transpose(0, 2, 1, 3).reshape(2, 4, N * N)


def solution(mesh):
    return jax.shard_map(
        local,
        mesh=mesh,
        in_specs=(P("band", "fft", None), P(None, "fft")),
        out_specs=P("band", "fft", None),
        check_vma=False,
    )
```

time: 108 us -> 105 us (0.972)
  the two profiles are of different devices: /device:TPU:1 before, /device:TPU:97 now
where the time goes in v5:
time: 105 us
  blocking collectives  54 us (51%)
  starting transfers between devices  28.9 us (28%)
  waiting for transfers between devices  14.8 us (14%)
  Pallas kernels  6.04 us (6%)
    all_to_all x2, blocking collectives, exchange(): return lax.all_to_all(value, 'fft', split_axis=0, concat_axis=0, tiled=True)  44 us
    ppermute x4, starting transfers between devices, along_band(): return lax.ppermute(value, ('band', 'pool'), pairs)  28.9 us
    ppermute x4, waiting for transfers between devices, along_band(): return lax.ppermute(value, ('band', 'pool'), pairs)  14.8 us
    all_gather x3, blocking collectives, both_cores(): return lax.all_gather(value, 'pool', tiled=True)  10 us
  transfers between devices with their start and end apart: 4, of which 2 were waited for; matrix products, arithmetic and copies ran while one was open for 0% of the time, Pallas kernels for 0%

profile of v5, /device:TPU:97, one launch (start us, length us, event | category | flops | bytes accessed | tf_op | source)
XLA Modules:
  0.0 104.9 jit_solution(7647200666141506475)
XLA Ops:
  0.0 6.2 %collective-permute-start.1 = (f32[256,128]{1,0:T(8,128)}, f32[256,128]{1,0:T(8,128)S(1)}, u32[]{:S(2)}, u32[]{:S(2)}) collective-permute-start(f32[256,128]{1,0:T(8,128)} %bitcast.10), channel_id=1, source_target_pairs={{0,416},{1,65},{32,448},{33,97},{64,480},{65,129},{96,0},{97,161},... | collective-permute-start | bytes 393224 | tf_op jit(solution)/shard_map/ppermute | solution.py:387
  6.2 5.6 %collective-permute-start = (f32[256,128]{1,0:T(8,128)}, f32[256,128]{1,0:T(8,128)S(1)}, u32[]{:S(2)}, u32[]{:S(2)}) collective-permute-start(f32[256,128]{1,0:T(8,128)} %bitcast.11), channel_id=1, source_target_pairs={{0,160},{1,385},{32,192},{33,417},{64,224},{65,449},{96,256},{97,4... | collective-permute-start | bytes 393224 | tf_op jit(solution)/shard_map/ppermute | solution.py:387
  11.8 0.0 copy-start.7
  11.8 0.9 copy-done.7
  12.7 0.1 shard_map.82.own_blocks
  12.8 4.2 %collective-permute-done = f32[256,128]{1,0:T(8,128)S(1)} collective-permute-done((f32[256,128]{1,0:T(8,128)}, f32[256,128]{1,0:T(8,128)S(1)}, u32[]{:S(2)}, u32[]{:S(2)}) %collective-permute-start) | collective-permute-done | bytes 131104 | tf_op jit(solution)/shard_map/ppermute | solution.py:387
  17.1 4.1 %all_gather.9.far = f32[512,128]{1,0:T(8,128)S(1)} all-gather(f32[256,128]{1,0:T(8,128)S(1)} %collective-permute-done), channel_id=1, replica_groups=mesh['band'=16,'fft'=16,'pool'=2] {'pool'}, dimensions={0}, use_global_device_ids=true | all-gather | bytes 393216 | tf_op jit(solution)/shard_map/all_gather | solution.py:391
  21.2 0.0 collective-permute-done.1.near
  21.2 0.0 copy-done.4
  21.2 0.0 copy-done.5
  21.2 1.8 %shard_map.83 = (f32[16,144,128]{2,1,0:T(8,128)S(1)}, f32[12,64,128]{2,1,0:T(8,128)S(1)}) custom-call(f32[4,64,128]{2,1,0:T(8,128)S(1)} %shard_map.82.own_blocks, f32[512,128]{1,0:T(8,128)S(1)} %all_gather.9.far, f32[256,128]{1,0:T(8,128)S(1)} %collective-permute-done.1.near, bf16[2,256,256]{2,1,0:T(8,128)(2,1)S(1)} %copy-done.5, ...), custom_call_target="tpu_custom_call" | custom-call | tf_op jit(solution)/shard_map/pallas_call | solution.py:330
  23.0 0.0 copy-start.2
  23.0 0.0 copy-start.3
  23.0 0.0 copy-start.6
  23.0 24.3 %all_to_all.10.spectra = f32[16,144,128]{2,1,0:T(8,128)S(1)} all-to-all(f32[16,144,128]{2,1,0:T(8,128)S(1)} %get-tuple-element.11), channel_id=1, replica_groups=mesh['band'=16,'fft'=16,'pool'=2] {'fft'}, dimensions={0} | all-to-all | bytes 2359296 | tf_op jit(solution)/shard_map/all_to_all | solution.py:395
  47.3 0.0 copy-done.2
  47.3 0.0 copy-done.3
  47.3 0.0 copy-done.6
  47.3 1.7 %shard_map.84 = f32[16,144,128]{2,1,0:T(8,128)S(1)} custom-call(f32[16,144,128]{2,1,0:T(8,128)S(1)} %all_to_all.10.spectra, f32[64,256]{1,0:T(8,128)S(1)} %copy-done.6, bf16[2,256,256]{2,1,0:T(8,128)(2,1)S(1)} %copy-done.3, bf16[2,256,256]{2,1,0:T(8,128)(2,1)S(1)} %copy-done.2), custom_call_target="tpu_custom_call" | custom-call | tf_op jit(solution)/shard_map/pallas_call | solution.py:340
  49.0 0.0 copy-start
  49.1 0.0 copy-start.1
  49.1 19.7 %all_to_all.11.returned = f32[16,144,128]{2,1,0:T(8,128)S(1)} all-to-all(f32[16,144,128]{2,1,0:T(8,128)S(1)} %shard_map.84), channel_id=1, replica_groups=mesh['band'=16,'fft'=16,'pool'=2] {'fft'}, dimensions={0} | all-to-all | bytes 2359296 | tf_op jit(solution)/shard_map/all_to_all | solution.py:395
  68.8 0.0 copy-done
  68.8 0.0 copy-done.1
  68.8 1.7 %shard_map.85 = (f32[4,64,128]{2,1,0:T(8,128)S(1)}, f32[4,64,128]{2,1,0:T(8,128)S(1)}, f32[4,64,128]{2,1,0:T(8,128)S(1)}, f32[4,64,128]{2,1,0:T(8,128)S(1)}) custom-call(f32[16,144,128]{2,1,0:T(8,128)S(1)} %all_to_all.11.returned, f32[4,64,128]{2,1,0:T(8,128)S(1)} %shard_map.82.own_blocks, f32[12,64,128]{2,1,0:T(8,128)S(1)} %get-tuple-element.12.blocks, ...), custom_call_target="tpu_custom_call" | custom-call | tf_op jit(solution)/shard_map/pallas_call | solution.py:350
  70.5 11.5 %collective-permute-start.3 = (f32[4,64,128]{2,1,0:T(8,128)S(1)}, f32[4,64,128]{2,1,0:T(8,128)S(1)}, u32[]{:S(2)}, u32[]{:S(2)}) collective-permute-start(f32[4,64,128]{2,1,0:T(8,128)S(1)} %get-tuple-element.15), channel_id=1, source_target_pairs={{0,96},{1,449},{32,128},{33,481},{64,160},{65,1},{96,192},{97,33},... | collective-permute-start | bytes 393224 | tf_op jit(solution)/shard_map/ppermute | solution.py:387
  81.9 2.0 %all_gather.10.others = f32[8,64,128]{2,1,0:T(8,128)S(1)} all-gather(f32[4,64,128]{2,1,0:T(8,128)S(1)} %get-tuple-element.14), channel_id=1, replica_groups=mesh['band'=16,'fft'=16,'pool'=2] {'pool'}, dimensions={0}, use_global_device_ids=true | all-gather | bytes 393216 | tf_op jit(solution)/shard_map/all_gather | solution.py:391
  83.9 5.6 %collective-permute-start.2 = (f32[4,64,128]{2,1,0:T(8,128)S(1)}, f32[4,64,128]{2,1,0:T(8,128)S(1)}, u32[]{:S(2)}, u32[]{:S(2)}) collective-permute-start(f32[4,64,128]{2,1,0:T(8,128)S(1)} %shard_map.86), channel_id=1, source_target_pairs={{0,352},{1,129},{32,384},{33,161},{64,416},{65,193},{96,448},{97,2... | collective-permute-start | bytes 393224 | tf_op jit(solution)/shard_map/ppermute | solution.py:387
  89.6 0.0 collective-permute-done.3
  89.6 10.6 %collective-permute-done.2 = f32[4,64,128]{2,1,0:T(8,128)S(1)} collective-permute-done((f32[4,64,128]{2,1,0:T(8,128)S(1)}, f32[4,64,128]{2,1,0:T(8,128)S(1)}, u32[]{:S(2)}, u32[]{:S(2)}) %collective-permute-start.2) | collective-permute-done | bytes 131104 | tf_op jit(solution)/shard_map/ppermute | solution.py:387
  100.2 3.9 %all_gather.11.both = f32[8,64,128]{2,1,0:T(8,128)S(1)} all-gather(f32[4,64,128]{2,1,0:T(8,128)S(1)} %add_add_fusion), channel_id=1, replica_groups=mesh['band'=16,'fft'=16,'pool'=2] {'pool'}, dimensions={0}, use_global_device_ids=true | all-gather | bytes 393216 | tf_op jit(solution)/shard_map/all_gather | solution.py:391
  104.1 0.8 shard_map.87
  (4 shorter events, 0.0 us)
Async XLA Ops:
  0.0 21.2 %copy-start.4 = (bf16[2,256,256]{2,1,0:T(8,128)(2,1)S(1)}, bf16[2,256,256]{2,1,0:T(8,128)(2,1)}, u32[]{:S(2)}) copy-start(bf16[2,256,256]{2,1,0:T(8,128)(2,1)} %constant.13.clone.table_y) | copy-start | bytes 786436
  0.0 21.2 %copy-start.5 = (bf16[2,256,256]{2,1,0:T(8,128)(2,1)S(1)}, bf16[2,256,256]{2,1,0:T(8,128)(2,1)}, u32[]{:S(2)}) copy-start(bf16[2,256,256]{2,1,0:T(8,128)(2,1)} %constant.12.clone.table_z) | copy-start | bytes 786436
  0.0 21.2 %collective-permute-start.1 = (f32[256,128]{1,0:T(8,128)}, f32[256,128]{1,0:T(8,128)S(1)}, u32[]{:S(2)}, u32[]{:S(2)}) collective-permute-start(f32[256,128]{1,0:T(8,128)} %bitcast.10), channel_id=1, source_target_pairs={{0,416},{1,65},{32,448},{33,97},{64,480},{65,129},{96,0},{97,161},... | collective-permute-start | bytes 393224 | tf_op jit(solution)/shard_map/ppermute | solution.py:387
  6.2 10.8 %collective-permute-start = (f32[256,128]{1,0:T(8,128)}, f32[256,128]{1,0:T(8,128)S(1)}, u32[]{:S(2)}, u32[]{:S(2)}) collective-permute-start(f32[256,128]{1,0:T(8,128)} %bitcast.11), channel_id=1, source_target_pairs={{0,160},{1,385},{32,192},{33,417},{64,224},{65,449},{96,256},{97,4... | collective-permute-start | bytes 393224 | tf_op jit(solution)/shard_map/ppermute | solution.py:387
  11.8 0.9 copy-start.7
  23.0 24.3 %copy-start.2 = (bf16[2,256,256]{2,1,0:T(8,128)(2,1)S(1)}, bf16[2,256,256]{2,1,0:T(8,128)(2,1)}, u32[]{:S(2)}) copy-start(bf16[2,256,256]{2,1,0:T(8,128)(2,1)} %constant.15.clone.table_x_back) | copy-start | bytes 786436
  23.0 24.3 %copy-start.3 = (bf16[2,256,256]{2,1,0:T(8,128)(2,1)S(1)}, bf16[2,256,256]{2,1,0:T(8,128)(2,1)}, u32[]{:S(2)}) copy-start(bf16[2,256,256]{2,1,0:T(8,128)(2,1)} %constant.14.clone.table_x) | copy-start | bytes 786436
  23.0 24.3 %copy-start.6 = (f32[64,256]{1,0:T(8,128)S(1)}, f32[64,256]{1,0:T(8,128)}, u32[]{:S(2)}) copy-start(f32[64,256]{1,0:T(8,128)} %kernel.1) | copy-start | bytes 196612
  49.0 19.7 %copy-start = (bf16[2,256,256]{2,1,0:T(8,128)(2,1)S(1)}, bf16[2,256,256]{2,1,0:T(8,128)(2,1)}, u32[]{:S(2)}) copy-start(bf16[2,256,256]{2,1,0:T(8,128)(2,1)} %constant.17.clone.table_z_back) | copy-start | bytes 786436
  49.1 19.7 %copy-start.1 = (bf16[2,256,256]{2,1,0:T(8,128)(2,1)S(1)}, bf16[2,256,256]{2,1,0:T(8,128)(2,1)}, u32[]{:S(2)}) copy-start(bf16[2,256,256]{2,1,0:T(8,128)(2,1)} %constant.16.clone.table_y_back) | copy-start | bytes 786436
  70.5 19.1 %collective-permute-start.3 = (f32[4,64,128]{2,1,0:T(8,128)S(1)}, f32[4,64,128]{2,1,0:T(8,128)S(1)}, u32[]{:S(2)}, u32[]{:S(2)}) collective-permute-start(f32[4,64,128]{2,1,0:T(8,128)S(1)} %get-tuple-element.15), channel_id=1, source_target_pairs={{0,96},{1,449},{32,128},{33,481},{64,160},{65,1},{96,192},{97,33},... | collective-permute-start | bytes 393224 | tf_op jit(solution)/shard_map/ppermute | solution.py:387
  83.9 16.2 %collective-permute-start.2 = (f32[4,64,128]{2,1,0:T(8,128)S(1)}, f32[4,64,128]{2,1,0:T(8,128)S(1)}, u32[]{:S(2)}, u32[]{:S(2)}) collective-permute-start(f32[4,64,128]{2,1,0:T(8,128)S(1)} %shard_map.86), channel_id=1, source_target_pairs={{0,352},{1,129},{32,384},{33,161},{64,416},{65,193},{96,448},{97,2... | collective-permute-start | bytes 393224 | tf_op jit(solution)/shard_map/ppermute | solution.py:387

commit v6 on v5

--- a/solution.py
+++ b/solution.py
@@ -114,8 +114,13 @@
         blocks[4 * place + plane, HALF:] = jnp.where(low, swap(first), second)
 
 
-def first_kernel(own, blocks):
+def first_kernel(own, blocks, again):
     unfold(own, 0, blocks, 0)
+    again[...] = own[...]
+
+
+def again_kernel(value, again):
+    again[...] = value[...]
 
 
 def spectrum(density, table_z, table_y):
@@ -290,7 +295,8 @@
         field[...] = fields[4 * place : 4 * place + 4]
 
 
-def share_kernel(mine, others, field):
+def share_kernel(mine, near, others, field, near_again):
+    near_again[...] = near[...]
     at = 4 * (1 - lax.axis_index("pool"))
     for plane in range(4):
         field[plane] = mine[plane] + others[at + plane]
@@ -315,15 +321,29 @@
     return jax.ShapeDtypeStruct((count, N, LANES), jnp.float32)
 
 
+LONG = pl.CostEstimate(flops=10**10, bytes_accessed=10**6, transcendentals=0)
+
+
 def first(own):
     return pl.pallas_call(
         first_kernel,
+        out_shape=[planes(4), jax.ShapeDtypeStruct((256, LANES), jnp.float32)],
+        in_specs=[VMEM],
+        out_specs=[VMEM] * 2,
+        compiler_params=PARAMS,
+        cost_estimate=LONG,
+    )(own)
+
+
+def again(value):
+    return pl.pallas_call(
+        again_kernel,
         out_shape=planes(4),
         in_specs=[VMEM],
         out_specs=VMEM,
         compiler_params=PARAMS,
-        cost_estimate=pl.CostEstimate(flops=10**10, bytes_accessed=10**6, transcendentals=0),
-    )(own)
+        cost_estimate=LONG,
+    )(value)
 
 
 def forward(own_blocks, far, near, table_z, table_y):
@@ -357,14 +377,14 @@
     )(returned, own_blocks, blocks, table_y_back, table_z_back)
 
 
-def share(mine, others):
+def share(mine, near, others):
     return pl.pallas_call(
         share_kernel,
-        out_shape=planes(4),
-        in_specs=[VMEM] * 2,
-        out_specs=VMEM,
-        compiler_params=PARAMS,
-    )(mine, others)
+        out_shape=[planes(4)] * 2,
+        in_specs=[VMEM] * 3,
+        out_specs=[VMEM] * 2,
+        compiler_params=PARAMS,
+    )(mine, near, others)
 
 
 def final(both):
@@ -401,16 +421,17 @@
     ]
     own = orbitals.reshape(2, 4, HALF, LANES).transpose(0, 2, 1, 3).reshape(256, LANES)
     far = both_cores(along_band(own, [-s for s in FAR]))
-    near = along_band(own, [-s for s in NEAR])
-    own_blocks = first(own)
+    own_blocks, own_again = first(own)
+    near = along_band(own_again, [-s for s in NEAR])
     spectra, blocks = forward(own_blocks, far, near, table_z, table_y)
     returned = exchange(middle(exchange(spectra), kernel, table_x, table_x_back))
     own_field, far_field, near_field, other_field = backward(
         returned, own_blocks, blocks, table_y_back, table_z_back
     )
+    far_field, near_field = share(far_field, near_field, both_cores(other_field))
+    far_field = along_band(again(far_field), FAR)
     near_field = along_band(near_field, NEAR)
-    far_field = along_band(share(far_field, both_cores(other_field)), FAR)
-    field = final(both_cores(far_field + near_field + own_field))
+    field = final(both_cores(near_field + far_field + own_field))
     return field.reshape(2, HALF, 4, LANES).transpose(0, 2, 1, 3).reshape(2, 4, N * N)
 
 

time: 105 us -> 105 us (level)
  the two profiles are of different devices: /device:TPU:97 before, /device:TPU:1 now
where the time goes in v6:
time: 105 us
  blocking collectives  54.8 us (52%)
  starting transfers between devices  27.1 us (26%)
  waiting for transfers between devices  15.6 us (15%)
  Pallas kernels  6.06 us (6%)
    all_to_all x2, blocking collectives, exchange(): return lax.all_to_all(value, 'fft', split_axis=0, concat_axis=0, tiled=True)  42.2 us
    ppermute x4, starting transfers between devices, along_band(): return lax.ppermute(value, ('band', 'pool'), pairs)  27.1 us
    ppermute x4, waiting for transfers between devices, along_band(): return lax.ppermute(value, ('band', 'pool'), pairs)  15.6 us
    all_gather x3, blocking collectives, both_cores(): return lax.all_gather(value, 'pool', tiled=True)  12.6 us
  transfers between devices with their start and end apart: 4, of which 3 were waited for; matrix products, arithmetic and copies ran while one was open for 0% of the time, Pallas kernels for 0%

profile of v6, /device:TPU:1, one launch (start us, length us, event | category | flops | bytes accessed | tf_op | source)
XLA Modules:
  0.0 104.7 jit_solution(7035009765685045274)
XLA Ops:
  0.0 13.4 %collective-permute-start = (f32[256,128]{1,0:T(8,128)}, f32[256,128]{1,0:T(8,128)S(1)}, u32[]{:S(2)}, u32[]{:S(2)}) collective-permute-start(f32[256,128]{1,0:T(8,128)} %bitcast.10), channel_id=1, source_target_pairs={{0,160},{1,385},{32,192},{33,417},{64,224},{65,449},{96,256},{97,4... | collective-permute-start | bytes 393224 | tf_op jit(solution)/shard_map/ppermute | solution.py:407
  13.4 0.0 copy-start.7
  13.4 0.9 copy-done.7
  14.3 0.1 shard_map.82
  14.4 3.1 %collective-permute-start.1 = (f32[256,128]{1,0:T(8,128)S(1)}, f32[256,128]{1,0:T(8,128)S(1)}, u32[]{:S(2)}, u32[]{:S(2)}) collective-permute-start(f32[256,128]{1,0:T(8,128)S(1)} %get-tuple-element.16), channel_id=1, source_target_pairs={{0,416},{1,65},{32,448},{33,97},{64,480},{65,129},{96,0},{97,161},... | collective-permute-start | bytes 393224 | tf_op jit(solution)/shard_map/ppermute | solution.py:407
  17.5 5.7 %collective-permute-done = f32[256,128]{1,0:T(8,128)S(1)} collective-permute-done((f32[256,128]{1,0:T(8,128)}, f32[256,128]{1,0:T(8,128)S(1)}, u32[]{:S(2)}, u32[]{:S(2)}) %collective-permute-start) | collective-permute-done | bytes 131104 | tf_op jit(solution)/shard_map/ppermute | solution.py:407
  23.3 2.0 %all_gather.9.far = f32[512,128]{1,0:T(8,128)S(1)} all-gather(f32[256,128]{1,0:T(8,128)S(1)} %collective-permute-done), channel_id=1, replica_groups=mesh['band'=16,'fft'=16,'pool'=2] {'pool'}, dimensions={0}, use_global_device_ids=true | all-gather | bytes 393216 | tf_op jit(solution)/shard_map/all_gather | solution.py:411
  25.3 0.0 collective-permute-done.1.near
  25.3 0.0 copy-done.4
  25.3 0.0 copy-done.5
  25.3 1.8 %shard_map.83 = (f32[16,144,128]{2,1,0:T(8,128)S(1)}, f32[12,64,128]{2,1,0:T(8,128)S(1)}) custom-call(f32[4,64,128]{2,1,0:T(8,128)S(1)} %get-tuple-element.15.own_blocks, f32[512,128]{1,0:T(8,128)S(1)} %all_gather.9.far, f32[256,128]{1,0:T(8,128)S(1)} %collective-permute-done.1.near, bf16[2,256,256]{2,1,0:T(8,128)(2,1)S(1)} %copy-done.5, ...), custom_call_target="tpu_custom_call" | custom-call | tf_op jit(solution)/shard_map/pallas_call | solution.py:350
  27.1 0.0 copy-start.2
  27.1 0.0 copy-start.3
  27.1 0.0 copy-start.6
  27.1 23.3 %all_to_all.10.spectra = f32[16,144,128]{2,1,0:T(8,128)S(1)} all-to-all(f32[16,144,128]{2,1,0:T(8,128)S(1)} %get-tuple-element.17), channel_id=1, replica_groups=mesh['band'=16,'fft'=16,'pool'=2] {'fft'}, dimensions={0} | all-to-all | bytes 2359296 | tf_op jit(solution)/shard_map/all_to_all | solution.py:415
  50.4 0.0 copy-done.2
  50.4 0.0 copy-done.3
  50.4 0.0 copy-done.6
  50.4 1.7 %shard_map.84 = f32[16,144,128]{2,1,0:T(8,128)S(1)} custom-call(f32[16,144,128]{2,1,0:T(8,128)S(1)} %all_to_all.10.spectra, f32[64,256]{1,0:T(8,128)S(1)} %copy-done.6, bf16[2,256,256]{2,1,0:T(8,128)(2,1)S(1)} %copy-done.3, bf16[2,256,256]{2,1,0:T(8,128)(2,1)S(1)} %copy-done.2), custom_call_target="tpu_custom_call" | custom-call | tf_op jit(solution)/shard_map/pallas_call | solution.py:360
  52.1 0.0 copy-start
  52.1 0.0 copy-start.1
  52.1 18.9 %all_to_all.11.returned = f32[16,144,128]{2,1,0:T(8,128)S(1)} all-to-all(f32[16,144,128]{2,1,0:T(8,128)S(1)} %shard_map.84), channel_id=1, replica_groups=mesh['band'=16,'fft'=16,'pool'=2] {'fft'}, dimensions={0} | all-to-all | bytes 2359296 | tf_op jit(solution)/shard_map/all_to_all | solution.py:415
  71.1 0.0 copy-done
  71.1 0.0 copy-done.1
  71.1 1.7 %shard_map.85 = (f32[4,64,128]{2,1,0:T(8,128)S(1)}, f32[4,64,128]{2,1,0:T(8,128)S(1)}, f32[4,64,128]{2,1,0:T(8,128)S(1)}, f32[4,64,128]{2,1,0:T(8,128)S(1)}) custom-call(f32[16,144,128]{2,1,0:T(8,128)S(1)} %all_to_all.11.returned, f32[4,64,128]{2,1,0:T(8,128)S(1)} %get-tuple-element.15.own_blocks, f32[12,64,128]{2,1,0:T(8,128)S(1)} %get-tuple-element.18.blocks, ...), custom_call_target="tpu_custom_call" | custom-call | tf_op jit(solution)/shard_map/pallas_call | solution.py:370
  72.8 5.6 %all_gather.10.others = f32[8,64,128]{2,1,0:T(8,128)S(1)} all-gather(f32[4,64,128]{2,1,0:T(8,128)S(1)} %get-tuple-element.21), channel_id=1, replica_groups=mesh['band'=16,'fft'=16,'pool'=2] {'pool'}, dimensions={0}, use_global_device_ids=true | all-gather | bytes 393216 | tf_op jit(solution)/shard_map/all_gather | solution.py:411
  78.4 8.7 %collective-permute-start.3 = (f32[4,64,128]{2,1,0:T(8,128)S(1)}, f32[4,64,128]{2,1,0:T(8,128)S(1)}, u32[]{:S(2)}, u32[]{:S(2)}) collective-permute-start(f32[4,64,128]{2,1,0:T(8,128)S(1)} %shard_map.87), channel_id=1, source_target_pairs={{0,352},{1,129},{32,384},{33,161},{64,416},{65,193},{96,448},{97,2... | collective-permute-start | bytes 393224 | tf_op jit(solution)/shard_map/ppermute | solution.py:407
  87.1 1.9 %collective-permute-start.2 = (f32[4,64,128]{2,1,0:T(8,128)S(1)}, f32[4,64,128]{2,1,0:T(8,128)S(1)}, u32[]{:S(2)}, u32[]{:S(2)}) collective-permute-start(f32[4,64,128]{2,1,0:T(8,128)S(1)} %get-tuple-element.22), channel_id=1, source_target_pairs={{0,96},{1,449},{32,128},{33,481},{64,160},{65,1},{96,192},{97,33},... | collective-permute-start | bytes 393224 | tf_op jit(solution)/shard_map/ppermute | solution.py:407
  89.0 1.2 %collective-permute-done.3 = f32[4,64,128]{2,1,0:T(8,128)S(1)} collective-permute-done((f32[4,64,128]{2,1,0:T(8,128)S(1)}, f32[4,64,128]{2,1,0:T(8,128)S(1)}, u32[]{:S(2)}, u32[]{:S(2)}) %collective-permute-start.3) | collective-permute-done | bytes 131104 | tf_op jit(solution)/shard_map/ppermute | solution.py:407
  90.2 8.7 %collective-permute-done.2 = f32[4,64,128]{2,1,0:T(8,128)S(1)} collective-permute-done((f32[4,64,128]{2,1,0:T(8,128)S(1)}, f32[4,64,128]{2,1,0:T(8,128)S(1)}, u32[]{:S(2)}, u32[]{:S(2)}) %collective-permute-start.2) | collective-permute-done | bytes 131104 | tf_op jit(solution)/shard_map/ppermute | solution.py:407
  98.9 5.1 %all_gather.11.both = f32[8,64,128]{2,1,0:T(8,128)S(1)} all-gather(f32[4,64,128]{2,1,0:T(8,128)S(1)} %add_add_fusion), channel_id=1, replica_groups=mesh['band'=16,'fft'=16,'pool'=2] {'pool'}, dimensions={0}, use_global_device_ids=true | all-gather | bytes 393216 | tf_op jit(solution)/shard_map/all_gather | solution.py:411
  104.0 0.8 shard_map.88
  (5 shorter events, 0.1 us)
Async XLA Ops:
  0.0 25.3 %copy-start.4 = (bf16[2,256,256]{2,1,0:T(8,128)(2,1)S(1)}, bf16[2,256,256]{2,1,0:T(8,128)(2,1)}, u32[]{:S(2)}) copy-start(bf16[2,256,256]{2,1,0:T(8,128)(2,1)} %constant.13.clone.table_y) | copy-start | bytes 786436
  0.0 25.3 %copy-start.5 = (bf16[2,256,256]{2,1,0:T(8,128)(2,1)S(1)}, bf16[2,256,256]{2,1,0:T(8,128)(2,1)}, u32[]{:S(2)}) copy-start(bf16[2,256,256]{2,1,0:T(8,128)(2,1)} %constant.12.clone.table_z) | copy-start | bytes 786436
  0.0 23.3 %collective-permute-start = (f32[256,128]{1,0:T(8,128)}, f32[256,128]{1,0:T(8,128)S(1)}, u32[]{:S(2)}, u32[]{:S(2)}) collective-permute-start(f32[256,128]{1,0:T(8,128)} %bitcast.10), channel_id=1, source_target_pairs={{0,160},{1,385},{32,192},{33,417},{64,224},{65,449},{96,256},{97,4... | collective-permute-start | bytes 393224 | tf_op jit(solution)/shard_map/ppermute | solution.py:407
  13.4 0.9 copy-start.7
  14.4 10.8 %collective-permute-start.1 = (f32[256,128]{1,0:T(8,128)S(1)}, f32[256,128]{1,0:T(8,128)S(1)}, u32[]{:S(2)}, u32[]{:S(2)}) collective-permute-start(f32[256,128]{1,0:T(8,128)S(1)} %get-tuple-element.16), channel_id=1, source_target_pairs={{0,416},{1,65},{32,448},{33,97},{64,480},{65,129},{96,0},{97,161},... | collective-permute-start | bytes 393224 | tf_op jit(solution)/shard_map/ppermute | solution.py:407
  27.1 23.3 %copy-start.2 = (bf16[2,256,256]{2,1,0:T(8,128)(2,1)S(1)}, bf16[2,256,256]{2,1,0:T(8,128)(2,1)}, u32[]{:S(2)}) copy-start(bf16[2,256,256]{2,1,0:T(8,128)(2,1)} %constant.15.clone.table_x_back) | copy-start | bytes 786436
  27.1 23.3 %copy-start.3 = (bf16[2,256,256]{2,1,0:T(8,128)(2,1)S(1)}, bf16[2,256,256]{2,1,0:T(8,128)(2,1)}, u32[]{:S(2)}) copy-start(bf16[2,256,256]{2,1,0:T(8,128)(2,1)} %constant.14.clone.table_x) | copy-start | bytes 786436
  27.1 23.3 %copy-start.6 = (f32[64,256]{1,0:T(8,128)S(1)}, f32[64,256]{1,0:T(8,128)}, u32[]{:S(2)}) copy-start(f32[64,256]{1,0:T(8,128)} %kernel.1) | copy-start | bytes 196612
  52.1 19.0 %copy-start = (bf16[2,256,256]{2,1,0:T(8,128)(2,1)S(1)}, bf16[2,256,256]{2,1,0:T(8,128)(2,1)}, u32[]{:S(2)}) copy-start(bf16[2,256,256]{2,1,0:T(8,128)(2,1)} %constant.17.clone.table_z_back) | copy-start | bytes 786436
  52.1 18.9 %copy-start.1 = (bf16[2,256,256]{2,1,0:T(8,128)(2,1)S(1)}, bf16[2,256,256]{2,1,0:T(8,128)(2,1)}, u32[]{:S(2)}) copy-start(bf16[2,256,256]{2,1,0:T(8,128)(2,1)} %constant.16.clone.table_y_back) | copy-start | bytes 786436
  78.4 11.8 %collective-permute-start.3 = (f32[4,64,128]{2,1,0:T(8,128)S(1)}, f32[4,64,128]{2,1,0:T(8,128)S(1)}, u32[]{:S(2)}, u32[]{:S(2)}) collective-permute-start(f32[4,64,128]{2,1,0:T(8,128)S(1)} %shard_map.87), channel_id=1, source_target_pairs={{0,352},{1,129},{32,384},{33,161},{64,416},{65,193},{96,448},{97,2... | collective-permute-start | bytes 393224 | tf_op jit(solution)/shard_map/ppermute | solution.py:407
  87.1 11.8 %collective-permute-start.2 = (f32[4,64,128]{2,1,0:T(8,128)S(1)}, f32[4,64,128]{2,1,0:T(8,128)S(1)}, u32[]{:S(2)}, u32[]{:S(2)}) collective-permute-start(f32[4,64,128]{2,1,0:T(8,128)S(1)} %get-tuple-element.22), channel_id=1, source_target_pairs={{0,96},{1,449},{32,128},{33,481},{64,160},{65,1},{96,192},{97,33},... | collective-permute-start | bytes 393224 | tf_op jit(solution)/shard_map/ppermute | solution.py:407

commit v7 on v5

--- a/solution.py
+++ b/solution.py
@@ -13,12 +13,14 @@
 LANES = 2 * N
 PEERS = 16
 UNITS = 4
-ROWS = 32 * UNITS + 16
-
-FAR = (-5, 4)
-NEAR = (3, -2)
-MEETINGS = (((0, 1), (0, 1)), ((0, 2), (0, 2)), ((1, 2), (1, 2)), ((2, 3), (1, 3)))
-EIGHT = 2
+ROWS = 32 * UNITS + 8
+
+SHARED = (-3, 4)
+ALONE = (-2, 5)
+RELAY = tuple(lone - shared for lone, shared in zip(ALONE, SHARED))
+MEETINGS = (((0, 2), (0, 2)), ((0, 1), (0, 1)), ((1, 2), (1, 3)), ((2, 3), (2, 3)))
+EIGHT = 3
+EIGHT_CORE = 1
 
 
 def wave_parts(rows, columns):
@@ -40,8 +42,9 @@
     along_z = np.einsum("oikz,ab->iazobk", turn, two).reshape(256, 256)
     along_y = np.einsum("oiky,ab->kaoiby", turn, two)
     along_y = along_y.reshape(PEERS, 2, 2, 2, 2, 2, 2, HALF, 2)
-    along_y = along_y.transpose(0, 1, 3, 4, 2, 6, 5, 8, 7).reshape(256, 256)
-    along_x = np.einsum("oikx,ab->oakxib", turn, two).reshape(256, 256)
+    along_y = along_y.transpose(0, 1, 4, 3, 2, 6, 5, 8, 7).reshape(256, 256)
+    along_x = np.einsum("oikx,ab->oakxib", turn, two).reshape(2, 2, N, HALF, 2, 2, 2)
+    along_x = along_x.transpose(0, 1, 2, 3, 5, 4, 6).reshape(256, 256)
     return [split_table(t) for t in (along_z, along_y, along_x, along_x.T, along_y.T, along_z.T)]
 
 
@@ -77,22 +80,22 @@
     return lax.axis_index("pool") == 0
 
 
+def on_eight():
+    return lax.axis_index("pool") == EIGHT_CORE
+
+
 def pick(first, second):
     return first if first is second else jnp.where(on_first(), first, second)
 
 
-def places(unit, half):
+def places(unit):
     first, second = MEETINGS[unit]
-    if unit == EIGHT and half:
-        first = (0, 0)
     return pick(first[0], second[0]), pick(first[1], second[1])
 
 
 def turned(unit, half, value):
-    if unit == EIGHT:
-        late = lax.axis_index("band") >= 8
-        crossed = jnp.logical_not(on_first()) if half else on_first() & late
-        return jnp.where(crossed, swap(value), value)
+    if unit == EIGHT and not half:
+        return jnp.where(on_eight() & (lax.axis_index("band") >= 8), swap(value), value)
     return swap(value) if half else value
 
 
@@ -114,8 +117,9 @@
         blocks[4 * place + plane, HALF:] = jnp.where(low, swap(first), second)
 
 
-def first_kernel(own, blocks):
+def first_kernel(own, blocks, again):
     unfold(own, 0, blocks, 0)
+    again[...] = own[...]
 
 
 def spectrum(density, table_z, table_y):
@@ -135,20 +139,20 @@
     return table_times(table_y, rows).reshape(PEERS, 16, rows.shape[1])
 
 
-def forward_kernel(own_blocks, far, near, table_z, table_y, out, blocks):
+def forward_kernel(own_blocks, shared, alone, table_z, table_y, out, blocks):
     core = lax.axis_index("pool")
-    unfold(far, 256 * core, blocks, 0)
-    unfold(near, 0, blocks, 1)
-    unfold(far, 256 * (1 - core), blocks, 2)
+    unfold(shared, 256 * core, blocks, 0)
+    unfold(alone, 0, blocks, 1)
+    unfold(shared, 256 * (1 - core), blocks, 2)
     read = reader(own_blocks, blocks)
 
     def density(unit, half, plane):
-        left, right = places(unit, half)
+        left, right = places(unit)
+        left, right = read(left, plane), turned(unit, half, read(right, plane))
         if unit == EIGHT and half:
-            left = jnp.where(on_first(), read(0, plane), read(1, plane))
-            right = jnp.where(on_first(), read(0, plane), swap(read(2, plane)))
-            return left * right
-        return read(left, plane) * turned(unit, half, read(right, plane))
+            own = read(0, plane)
+            left, right = jnp.where(on_eight(), own, left), jnp.where(on_eight(), own, right)
+        return left * right
 
     for u in range(UNITS):
         rows = spectrum(
@@ -168,9 +172,10 @@
 
     last = []
     for at, behind in ((own_blocks[0], own_blocks[2]), (own_blocks[1], own_blocks[3])):
-        pairs = 0.5 * jnp.where(low_lanes(N), at * swap(at), behind * swap(behind))
+        pairs = jnp.where(low_lanes(N), at * swap(at), behind * swap(behind))
         last.append(jnp.concatenate([pairs, jnp.zeros((N, LANES), jnp.float32)], axis=1))
-    out[:, 32 * UNITS :, :] = spectrum(last, table_z, table_y)
+    rows = spectrum(last, table_z, table_y)
+    out[:, 32 * UNITS :, :] = jnp.where(on_first(), rows[:, :8], rows[:, 8:])
 
 
 def middle_kernel(spectra, kernel, table_x, table_x_back, out):
@@ -199,22 +204,14 @@
                 PEERS, 16, LANES
             )
 
-    def exchanged(one, two):
-        wide = lax.broadcasted_iota(jnp.int32, one.shape, 2) < N
-        one_other, two_other = pltpu.roll(one, N, 2), pltpu.roll(two, N, 2)
-        return jnp.where(wide, one, two_other), jnp.where(wide, one_other, two)
-
     at = 32 * UNITS
-    rows = jnp.concatenate(
-        exchanged(spectra[:, at : at + 8, :], spectra[:, at + 8 : at + 16, :]), axis=1
-    )
-    rows = apply(
-        rows.reshape(256, LANES),
-        rows_of((jnp.where(low, first, swap(second)), jnp.where(low, swap(first), second))),
-    ).reshape(PEERS, 16, LANES)
-    one, two = exchanged(rows[:, :8], rows[:, 8:])
-    out[:, at : at + 8, :] = one
-    out[:, at + 8 : at + 16, :] = two
+    rows = spectra[:, at:, :]
+    rows = jnp.concatenate([rows, pltpu.roll(rows, N, 2)], axis=1).reshape(256, LANES)
+    mine = jnp.where(on_first(), first, second)
+    rows = apply(rows, rows_of((mine, swap(mine)))).reshape(PEERS, 16, LANES)
+    behind = pltpu.roll(rows[:, 8:], N, 2)
+    front = lax.broadcasted_iota(jnp.int32, behind.shape, 2) < N
+    out[:, at:, :] = jnp.where(front, rows[:, :8], behind)
 
 
 def backward_kernel(
@@ -224,8 +221,8 @@
     table_y_back,
     table_z_back,
     own_field,
-    far_field,
-    near_field,
+    shared_field,
+    lone_field,
     other_field,
     fields,
 ):
@@ -233,18 +230,16 @@
     read = reader(own_blocks, blocks)
 
     def collect(unit, half, plane, potential):
+        left, right = places(unit)
+        partner = turned(unit, half, read(right, plane))
+        given = turned(unit, half, potential * read(left, plane))
         if unit == EIGHT and half:
-            first = on_first()
-            partner = jnp.where(first, read(0, plane), swap(read(2, plane)))
-            mine = potential * partner
-            fields[plane] += jnp.where(first, mine, 0.0)
-            fields[4 + plane] += jnp.where(first, 0.0, mine)
-            given = swap(potential * read(1, plane))
-            fields[8 + plane] += jnp.where(first, 0.0, given)
-            return
-        left, right = places(unit, half)
-        fields[4 * left + plane] += potential * turned(unit, half, read(right, plane))
-        fields[4 * right + plane] += turned(unit, half, potential * read(left, plane))
+            squares = jnp.where(on_eight(), potential, 0.0)
+            potential = potential - squares
+            given = jnp.where(on_eight(), 0.0, given)
+            fields[plane] += squares * read(0, plane)
+        fields[4 * left + plane] += potential * partner
+        fields[4 * right + plane] += given
 
     def potentials(pairs):
         rows = table_times(table_y_back, jnp.concatenate(pairs, axis=1))
@@ -279,21 +274,23 @@
                     plane,
                     rows[plane * N : plane * N + N, half * LANES : half * LANES + LANES],
                 )
-    rows = potentials([returned[:, 32 * UNITS :, :].reshape(256, LANES)])
+    last = returned[:, 32 * UNITS :, :]
+    last = [jnp.where(on_first(), last, 0.0), jnp.where(on_first(), 0.0, last)]
+    rows = potentials([jnp.concatenate(last, axis=1).reshape(256, LANES)])
     low = low_lanes(N)
     for at in range(2):
         potential = rows[at * N : at * N + N, :LANES]
         other = swap(potential)
         fields[at] += jnp.where(low, potential, other) * swap(own_blocks[at])
         fields[2 + at] += jnp.where(low, other, potential) * swap(own_blocks[2 + at])
-    for place, field in enumerate((own_field, far_field, near_field, other_field)):
+    for place, field in enumerate((own_field, shared_field, lone_field, other_field)):
         field[...] = fields[4 * place : 4 * place + 4]
 
 
-def share_kernel(mine, others, field):
+def share_kernel(mine, others, relayed, field):
     at = 4 * (1 - lax.axis_index("pool"))
     for plane in range(4):
-        field[plane] = mine[plane] + others[at + plane]
+        field[plane] = mine[plane] + others[at + plane] + relayed[plane]
 
 
 def final_kernel(both, out):
@@ -315,25 +312,28 @@
     return jax.ShapeDtypeStruct((count, N, LANES), jnp.float32)
 
 
+LONG = pl.CostEstimate(flops=10**10, bytes_accessed=10**6, transcendentals=0)
+
+
 def first(own):
     return pl.pallas_call(
         first_kernel,
-        out_shape=planes(4),
+        out_shape=[planes(4), jax.ShapeDtypeStruct((256, LANES), jnp.float32)],
         in_specs=[VMEM],
-        out_specs=VMEM,
-        compiler_params=PARAMS,
-        cost_estimate=pl.CostEstimate(flops=10**10, bytes_accessed=10**6, transcendentals=0),
+        out_specs=[VMEM] * 2,
+        compiler_params=PARAMS,
+        cost_estimate=LONG,
     )(own)
 
 
-def forward(own_blocks, far, near, table_z, table_y):
+def forward(own_blocks, shared, alone, table_z, table_y):
     return pl.pallas_call(
         forward_kernel,
         out_shape=[CHUNKS, planes(12)],
         in_specs=[VMEM] * 5,
         out_specs=[VMEM] * 2,
         compiler_params=PARAMS,
-    )(own_blocks, far, near, table_z, table_y)
+    )(own_blocks, shared, alone, table_z, table_y)
 
 
 def middle(spectra, kernel, table_x, table_x_back):
@@ -357,14 +357,14 @@
     )(returned, own_blocks, blocks, table_y_back, table_z_back)
 
 
-def share(mine, others):
+def share(mine, others, relayed):
     return pl.pallas_call(
         share_kernel,
         out_shape=planes(4),
-        in_specs=[VMEM] * 2,
+        in_specs=[VMEM] * 3,
         out_specs=VMEM,
         compiler_params=PARAMS,
-    )(mine, others)
+    )(mine, others, relayed)
 
 
 def final(both):
@@ -400,17 +400,17 @@
         jnp.asarray(t) for t in tables()
     ]
     own = orbitals.reshape(2, 4, HALF, LANES).transpose(0, 2, 1, 3).reshape(256, LANES)
-    far = both_cores(along_band(own, [-s for s in FAR]))
-    near = along_band(own, [-s for s in NEAR])
-    own_blocks = first(own)
-    spectra, blocks = forward(own_blocks, far, near, table_z, table_y)
+    shared = both_cores(along_band(own, [-s for s in SHARED]))
+    own_blocks, own_again = first(own)
+    alone = along_band(own_again, [-s for s in ALONE])
+    spectra, blocks = forward(own_blocks, shared, alone, table_z, table_y)
     returned = exchange(middle(exchange(spectra), kernel, table_x, table_x_back))
-    own_field, far_field, near_field, other_field = backward(
+    own_field, shared_field, lone_field, other_field = backward(
         returned, own_blocks, blocks, table_y_back, table_z_back
     )
-    near_field = along_band(near_field, NEAR)
-    far_field = along_band(share(far_field, both_cores(other_field)), FAR)
-    field = final(both_cores(far_field + near_field + own_field))
+    relayed = along_band(lone_field, RELAY)
+    shared_field = along_band(share(shared_field, both_cores(other_field), relayed), SHARED)
+    field = final(both_cores(shared_field + own_field))
     return field.reshape(2, HALF, 4, LANES).transpose(0, 2, 1, 3).reshape(2, 4, N * N)
 
 

time: 105 us -> 95.9 us (0.913)
  the two profiles are of different devices: /device:TPU:97 before, /device:TPU:33 now
where the time goes in v7:
time: 95.9 us; the launch traced here: 95.5 us
  blocking collectives  43.3 us (45%)
  starting transfers between devices  32.6 us (34%)
  waiting for transfers between devices  12.5 us (13%)
  Pallas kernels  6.01 us (6%)
    all_to_all x2, blocking collectives, exchange(): return lax.all_to_all(value, 'fft', split_axis=0, concat_axis=0, tiled=True)  34.6 us
    ppermute x4, starting transfers between devices, along_band(): return lax.ppermute(value, ('band', 'pool'), pairs)  32.6 us
    ppermute x4, waiting for transfers between devices, along_band(): return lax.ppermute(value, ('band', 'pool'), pairs)  12.5 us
    all_gather x3, blocking collectives, both_cores(): return lax.all_gather(value, 'pool', tiled=True)  8.69 us
  transfers between devices with their start and end apart: 4, of which 3 were waited for; matrix products, arithmetic and copies ran while one was open for 0% of the time, Pallas kernels for 0%

profile of v7, /device:TPU:33, one launch (start us, length us, event | category | flops | bytes accessed | tf_op | source)
XLA Modules:
  0.0 95.5 jit_solution(5509625772700455847)
XLA Ops:
  0.0 0.0 copy-start.2
  0.0 11.7 %collective-permute-start = (f32[256,128]{1,0:T(8,128)}, f32[256,128]{1,0:T(8,128)S(1)}, u32[]{:S(2)}, u32[]{:S(2)}) collective-permute-start(f32[256,128]{1,0:T(8,128)} %bitcast.10), channel_id=1, source_target_pairs={{0,96},{1,385},{32,128},{33,417},{64,160},{65,449},{96,192},{97,48... | collective-permute-start | bytes 393224 | tf_op jit(solution)/shard_map/ppermute | solution.py:387
  11.7 0.0 copy-start.7
  11.7 0.9 copy-done.7
  12.6 0.1 shard_map.82
  12.7 5.6 %collective-permute-start.1 = (f32[256,128]{1,0:T(8,128)S(1)}, f32[256,128]{1,0:T(8,128)S(1)}, u32[]{:S(2)}, u32[]{:S(2)}) collective-permute-start(f32[256,128]{1,0:T(8,128)S(1)} %get-tuple-element.14), channel_id=1, source_target_pairs={{0,64},{1,353},{32,96},{33,385},{64,128},{65,417},{96,160},{97,449... | collective-permute-start | bytes 393224 | tf_op jit(solution)/shard_map/ppermute | solution.py:387
  18.3 0.0 collective-permute-done
  18.4 2.0 %all_gather.9.shared = f32[512,128]{1,0:T(8,128)S(1)} all-gather(f32[256,128]{1,0:T(8,128)S(1)} %collective-permute-done), channel_id=1, replica_groups=mesh['band'=16,'fft'=16,'pool'=2] {'pool'}, dimensions={0}, use_global_device_ids=true | all-gather | bytes 393216 | tf_op jit(solution)/shard_map/all_gather | solution.py:391
  20.3 7.8 %collective-permute-done.1.alone = f32[256,128]{1,0:T(8,128)S(1)} collective-permute-done((f32[256,128]{1,0:T(8,128)S(1)}, f32[256,128]{1,0:T(8,128)S(1)}, u32[]{:S(2)}, u32[]{:S(2)}) %collective-permute-start.1) | collective-permute-done | bytes 131104 | tf_op jit(solution)/shard_map/ppermute | solution.py:387
  28.1 0.0 copy-done.2
  28.1 0.0 copy-done.3
  28.1 1.8 %shard_map.83 = (f32[16,136,128]{2,1,0:T(8,128)S(1)}, f32[12,64,128]{2,1,0:T(8,128)S(1)}) custom-call(f32[4,64,128]{2,1,0:T(8,128)S(1)} %get-tuple-element.13.own_blocks, f32[512,128]{1,0:T(8,128)S(1)} %all_gather.9.shared, f32[256,128]{1,0:T(8,128)S(1)} %collective-permute-done.1.alone, bf16[2,256,256]{2,1,0:T(8,128)(2,1)S(1)} %copy-done.3, ...), custom_call_target="tpu_custom_call" | custom-call | tf_op jit(solution)/shard_map/pallas_call | solution.py:330
  29.9 0.0 copy-start.4
  29.9 0.0 copy-start.5
  29.9 0.0 copy-start.6
  29.9 18.8 %all_to_all.10.spectra = f32[16,136,128]{2,1,0:T(8,128)S(1)} all-to-all(f32[16,136,128]{2,1,0:T(8,128)S(1)} %get-tuple-element.15), channel_id=1, replica_groups=mesh['band'=16,'fft'=16,'pool'=2] {'fft'}, dimensions={0} | all-to-all | bytes 2228224 | tf_op jit(solution)/shard_map/all_to_all | solution.py:395
  48.8 0.0 copy-done.4
  48.8 0.0 copy-done.5
  48.8 0.0 copy-done.6
  48.8 1.7 %shard_map.84 = f32[16,136,128]{2,1,0:T(8,128)S(1)} custom-call(f32[16,136,128]{2,1,0:T(8,128)S(1)} %all_to_all.10.spectra, f32[64,256]{1,0:T(8,128)S(1)} %copy-done.6, bf16[2,256,256]{2,1,0:T(8,128)(2,1)S(1)} %copy-done.5, bf16[2,256,256]{2,1,0:T(8,128)(2,1)S(1)} %copy-done.4), custom_call_target="tpu_custom_call" | custom-call | tf_op jit(solution)/shard_map/pallas_call | solution.py:340
  50.5 0.0 copy-start.1
  50.5 15.7 %all_to_all.11.returned = f32[16,136,128]{2,1,0:T(8,128)S(1)} all-to-all(f32[16,136,128]{2,1,0:T(8,128)S(1)} %shard_map.84), channel_id=1, replica_groups=mesh['band'=16,'fft'=16,'pool'=2] {'fft'}, dimensions={0} | all-to-all | bytes 2228224 | tf_op jit(solution)/shard_map/all_to_all | solution.py:395
  66.2 0.0 copy-done
  66.2 0.0 copy-done.1
  66.2 1.6 %shard_map.85 = (f32[4,64,128]{2,1,0:T(8,128)S(1)}, f32[4,64,128]{2,1,0:T(8,128)S(1)}, f32[4,64,128]{2,1,0:T(8,128)S(1)}, f32[4,64,128]{2,1,0:T(8,128)S(1)}) custom-call(f32[16,136,128]{2,1,0:T(8,128)S(1)} %all_to_all.11.returned, f32[4,64,128]{2,1,0:T(8,128)S(1)} %get-tuple-element.13.own_blocks, f32[12,64,128]{2,1,0:T(8,128)S(1)} %get-tuple-element.16.blocks, ...), custom_call_target="tpu_custom_call" | custom-call | tf_op jit(solution)/shard_map/pallas_call | solution.py:350
  67.9 3.0 %collective-permute-start.2 = (f32[4,64,128]{2,1,0:T(8,128)S(1)}, f32[4,64,128]{2,1,0:T(8,128)S(1)}, u32[]{:S(2)}, u32[]{:S(2)}) collective-permute-start(f32[4,64,128]{2,1,0:T(8,128)S(1)} %get-tuple-element.19), channel_id=1, source_target_pairs={{0,32},{1,33},{32,64},{33,65},{64,96},{65,97},{96,128},{97,129},{1... | collective-permute-start | bytes 393224 | tf_op jit(solution)/shard_map/ppermute | solution.py:387
  70.9 2.0 %all_gather.10.others = f32[8,64,128]{2,1,0:T(8,128)S(1)} all-gather(f32[4,64,128]{2,1,0:T(8,128)S(1)} %get-tuple-element.18), channel_id=1, replica_groups=mesh['band'=16,'fft'=16,'pool'=2] {'pool'}, dimensions={0}, use_global_device_ids=true | all-gather | bytes 393216 | tf_op jit(solution)/shard_map/all_gather | solution.py:391
  72.9 0.7 collective-permute-done.2.relayed
  73.6 12.3 %collective-permute-start.3 = (f32[4,64,128]{2,1,0:T(8,128)S(1)}, f32[4,64,128]{2,1,0:T(8,128)S(1)}, u32[]{:S(2)}, u32[]{:S(2)}) collective-permute-start(f32[4,64,128]{2,1,0:T(8,128)S(1)} %shard_map.86), channel_id=1, source_target_pairs={{0,416},{1,129},{32,448},{33,161},{64,480},{65,193},{96,0},{97,225... | collective-permute-start | bytes 393224 | tf_op jit(solution)/shard_map/ppermute | solution.py:387
  86.0 4.1 %collective-permute-done.3 = f32[4,64,128]{2,1,0:T(8,128)S(1)} collective-permute-done((f32[4,64,128]{2,1,0:T(8,128)S(1)}, f32[4,64,128]{2,1,0:T(8,128)S(1)}, u32[]{:S(2)}, u32[]{:S(2)}) %collective-permute-start.3) | collective-permute-done | bytes 131104 | tf_op jit(solution)/shard_map/ppermute | solution.py:387
  90.1 4.7 %all_gather.11.both = f32[8,64,128]{2,1,0:T(8,128)S(1)} all-gather(f32[4,64,128]{2,1,0:T(8,128)S(1)} %add.3), channel_id=1, replica_groups=mesh['band'=16,'fft'=16,'pool'=2] {'pool'}, dimensions={0}, use_global_device_ids=true | all-gather | bytes 393216 | tf_op jit(solution)/shard_map/all_gather | solution.py:391
  94.8 0.8 shard_map.87
  (4 shorter events, 0.0 us)
Async XLA Ops:
  0.0 28.1 %copy-start.2 = (bf16[2,256,256]{2,1,0:T(8,128)(2,1)S(1)}, bf16[2,256,256]{2,1,0:T(8,128)(2,1)}, u32[]{:S(2)}) copy-start(bf16[2,256,256]{2,1,0:T(8,128)(2,1)} %constant.13.clone.table_y) | copy-start | bytes 786436
  0.0 28.1 %copy-start.3 = (bf16[2,256,256]{2,1,0:T(8,128)(2,1)S(1)}, bf16[2,256,256]{2,1,0:T(8,128)(2,1)}, u32[]{:S(2)}) copy-start(bf16[2,256,256]{2,1,0:T(8,128)(2,1)} %constant.12.clone.table_z) | copy-start | bytes 786436
  0.0 18.3 %collective-permute-start = (f32[256,128]{1,0:T(8,128)}, f32[256,128]{1,0:T(8,128)S(1)}, u32[]{:S(2)}, u32[]{:S(2)}) collective-permute-start(f32[256,128]{1,0:T(8,128)} %bitcast.10), channel_id=1, source_target_pairs={{0,96},{1,385},{32,128},{33,417},{64,160},{65,449},{96,192},{97,48... | collective-permute-start | bytes 393224 | tf_op jit(solution)/shard_map/ppermute | solution.py:387
  11.7 0.9 copy-start.7
  12.7 15.4 %collective-permute-start.1 = (f32[256,128]{1,0:T(8,128)S(1)}, f32[256,128]{1,0:T(8,128)S(1)}, u32[]{:S(2)}, u32[]{:S(2)}) collective-permute-start(f32[256,128]{1,0:T(8,128)S(1)} %get-tuple-element.14), channel_id=1, source_target_pairs={{0,64},{1,353},{32,96},{33,385},{64,128},{65,417},{96,160},{97,449... | collective-permute-start | bytes 393224 | tf_op jit(solution)/shard_map/ppermute | solution.py:387
  29.9 18.9 %copy-start.4 = (bf16[2,256,256]{2,1,0:T(8,128)(2,1)S(1)}, bf16[2,256,256]{2,1,0:T(8,128)(2,1)}, u32[]{:S(2)}) copy-start(bf16[2,256,256]{2,1,0:T(8,128)(2,1)} %constant.15.clone.table_x_back) | copy-start | bytes 786436
  29.9 18.9 %copy-start.5 = (bf16[2,256,256]{2,1,0:T(8,128)(2,1)S(1)}, bf16[2,256,256]{2,1,0:T(8,128)(2,1)}, u32[]{:S(2)}) copy-start(bf16[2,256,256]{2,1,0:T(8,128)(2,1)} %constant.14.clone.table_x) | copy-start | bytes 786436
  29.9 18.8 %copy-start.6 = (f32[64,256]{1,0:T(8,128)S(1)}, f32[64,256]{1,0:T(8,128)}, u32[]{:S(2)}) copy-start(f32[64,256]{1,0:T(8,128)} %kernel.1) | copy-start | bytes 196612
  50.5 15.8 %copy-start = (bf16[2,256,256]{2,1,0:T(8,128)(2,1)S(1)}, bf16[2,256,256]{2,1,0:T(8,128)(2,1)}, u32[]{:S(2)}) copy-start(bf16[2,256,256]{2,1,0:T(8,128)(2,1)} %constant.17.clone.table_z_back) | copy-start | bytes 786436
  50.5 15.8 %copy-start.1 = (bf16[2,256,256]{2,1,0:T(8,128)(2,1)S(1)}, bf16[2,256,256]{2,1,0:T(8,128)(2,1)}, u32[]{:S(2)}) copy-start(bf16[2,256,256]{2,1,0:T(8,128)(2,1)} %constant.16.clone.table_y_back) | copy-start | bytes 786436
  67.9 5.7 %collective-permute-start.2 = (f32[4,64,128]{2,1,0:T(8,128)S(1)}, f32[4,64,128]{2,1,0:T(8,128)S(1)}, u32[]{:S(2)}, u32[]{:S(2)}) collective-permute-start(f32[4,64,128]{2,1,0:T(8,128)S(1)} %get-tuple-element.19), channel_id=1, source_target_pairs={{0,32},{1,33},{32,64},{33,65},{64,96},{65,97},{96,128},{97,129},{1... | collective-permute-start | bytes 393224 | tf_op jit(solution)/shard_map/ppermute | solution.py:387
  73.6 16.4 %collective-permute-start.3 = (f32[4,64,128]{2,1,0:T(8,128)S(1)}, f32[4,64,128]{2,1,0:T(8,128)S(1)}, u32[]{:S(2)}, u32[]{:S(2)}) collective-permute-start(f32[4,64,128]{2,1,0:T(8,128)S(1)} %shard_map.86), channel_id=1, source_target_pairs={{0,416},{1,129},{32,448},{33,161},{64,480},{65,193},{96,0},{97,225... | collective-permute-start | bytes 393224 | tf_op jit(solution)/shard_map/ppermute | solution.py:387

commit v8 on v7

--- a/solution.py
+++ b/solution.py
@@ -21,6 +21,7 @@
 MEETINGS = (((0, 2), (0, 2)), ((0, 1), (0, 1)), ((1, 2), (1, 3)), ((2, 3), (2, 3)))
 EIGHT = 3
 EIGHT_CORE = 1
+SOON = 1
 
 
 def wave_parts(rows, columns):
@@ -85,12 +86,12 @@
 
 
 def pick(first, second):
-    return first if first is second else jnp.where(on_first(), first, second)
+    return first if first == second else jnp.where(on_first(), first, second)
 
 
 def places(unit):
     first, second = MEETINGS[unit]
-    return pick(first[0], second[0]), pick(first[1], second[1])
+    return (first[0], second[0]), (first[1], second[1])
 
 
 def turned(unit, half, value):
@@ -99,11 +100,19 @@
     return swap(value) if half else value
 
 
-def reader(own_blocks, blocks):
-    def read(place, plane):
-        if isinstance(place, int):
-            return blocks[4 * place - 4 + plane] if place else own_blocks[plane]
-        return blocks[4 * place - 4 + plane]
+def reader(own_blocks, shared_blocks, lone_blocks):
+    def read_one(place, plane):
+        if place == 0:
+            return own_blocks[plane]
+        if place == 2:
+            return lone_blocks[plane]
+        return shared_blocks[2 * place - 2 + plane]
+
+    def read(of_cores, plane):
+        first, second = of_cores
+        if first == second:
+            return read_one(first, plane)
+        return jnp.where(on_first(), read_one(first, plane), read_one(second, plane))
 
     return read
 
@@ -139,43 +148,54 @@
     return table_times(table_y, rows).reshape(PEERS, 16, rows.shape[1])
 
 
-def forward_kernel(own_blocks, shared, alone, table_z, table_y, out, blocks):
+def density(read, unit, half, plane):
+    left, right = places(unit)
+    left, right = read(left, plane), turned(unit, half, read(right, plane))
+    if unit == EIGHT and half:
+        own = read((0, 0), plane)
+        left, right = jnp.where(on_eight(), own, left), jnp.where(on_eight(), own, right)
+    return left * right
+
+
+def send_unit(read, unit, out, base, table_z, table_y):
+    rows = spectrum(
+        [
+            jnp.concatenate([density(read, unit, half, plane) for half in range(2)], axis=1)
+            for plane in range(4)
+        ],
+        table_z,
+        table_y,
+    )
+    for ky_high in range(2):
+        for high in range(2):
+            at = base + 16 * ky_high + 8 * high
+            out[:, at : at + 8, :] = rows[
+                :, 8 * ky_high : 8 * ky_high + 8, LANES * high : LANES * high + LANES
+            ]
+
+
+def early_kernel(own_blocks, shared, table_z, table_y, out, shared_blocks):
     core = lax.axis_index("pool")
-    unfold(shared, 256 * core, blocks, 0)
-    unfold(alone, 0, blocks, 1)
-    unfold(shared, 256 * (1 - core), blocks, 2)
-    read = reader(own_blocks, blocks)
-
-    def density(unit, half, plane):
-        left, right = places(unit)
-        left, right = read(left, plane), turned(unit, half, read(right, plane))
-        if unit == EIGHT and half:
-            own = read(0, plane)
-            left, right = jnp.where(on_eight(), own, left), jnp.where(on_eight(), own, right)
-        return left * right
-
-    for u in range(UNITS):
-        rows = spectrum(
-            [
-                jnp.concatenate([density(u, 0, plane), density(u, 1, plane)], axis=1)
-                for plane in range(4)
-            ],
-            table_z,
-            table_y,
-        )
-        for ky_high in range(2):
-            for high in range(2):
-                at = 32 * u + 16 * ky_high + 8 * high
-                out[:, at : at + 8, :] = rows[
-                    :, 8 * ky_high : 8 * ky_high + 8, LANES * high : LANES * high + LANES
-                ]
-
+    unfold(shared, 256 * core, shared_blocks, 0)
+    unfold(shared, 256 * (1 - core), shared_blocks, 1)
+    read = reader(own_blocks, shared_blocks, None)
+    send_unit(read, SOON, out, 0, table_z, table_y)
     last = []
     for at, behind in ((own_blocks[0], own_blocks[2]), (own_blocks[1], own_blocks[3])):
         pairs = jnp.where(low_lanes(N), at * swap(at), behind * swap(behind))
         last.append(jnp.concatenate([pairs, jnp.zeros((N, LANES), jnp.float32)], axis=1))
     rows = spectrum(last, table_z, table_y)
-    out[:, 32 * UNITS :, :] = jnp.where(on_first(), rows[:, :8], rows[:, 8:])
+    out[:, 32:, :] = jnp.where(on_first(), rows[:, :8], rows[:, 8:])
+
+
+def forward_kernel(own_blocks, shared_blocks, early, alone, table_z, table_y, out, lone_blocks):
+    out[:, 32 * SOON : 32 * SOON + 32, :] = early[:, :32, :]
+    out[:, 32 * UNITS :, :] = early[:, 32:, :]
+    unfold(alone, 0, lone_blocks, 0)
+    read = reader(own_blocks, shared_blocks, lone_blocks)
+    for u in range(UNITS):
+        if u != SOON:
+            send_unit(read, u, out, 32 * u, table_z, table_y)
 
 
 def middle_kernel(spectra, kernel, table_x, table_x_back, out):
@@ -217,7 +237,8 @@
 def backward_kernel(
     returned,
     own_blocks,
-    blocks,
+    shared_blocks,
+    lone_blocks,
     table_y_back,
     table_z_back,
     own_field,
@@ -227,7 +248,7 @@
     fields,
 ):
     fields[...] = jnp.zeros_like(fields)
-    read = reader(own_blocks, blocks)
+    read = reader(own_blocks, shared_blocks, lone_blocks)
 
     def collect(unit, half, plane, potential):
         left, right = places(unit)
@@ -237,9 +258,9 @@
             squares = jnp.where(on_eight(), potential, 0.0)
             potential = potential - squares
             given = jnp.where(on_eight(), 0.0, given)
-            fields[plane] += squares * read(0, plane)
-        fields[4 * left + plane] += potential * partner
-        fields[4 * right + plane] += given
+            fields[plane] += squares * own_blocks[plane]
+        fields[4 * pick(*left) + plane] += potential * partner
+        fields[4 * pick(*right) + plane] += given
 
     def potentials(pairs):
         rows = table_times(table_y_back, jnp.concatenate(pairs, axis=1))
@@ -326,14 +347,24 @@
     )(own)
 
 
-def forward(own_blocks, shared, alone, table_z, table_y):
+def early(own_blocks, shared, table_z, table_y):
+    return pl.pallas_call(
+        early_kernel,
+        out_shape=[jax.ShapeDtypeStruct((PEERS, 40, LANES), jnp.float32), planes(8)],
+        in_specs=[VMEM] * 4,
+        out_specs=[VMEM] * 2,
+        compiler_params=PARAMS,
+    )(own_blocks, shared, table_z, table_y)
+
+
+def forward(own_blocks, shared_blocks, rows, alone, table_z, table_y):
     return pl.pallas_call(
         forward_kernel,
-        out_shape=[CHUNKS, planes(12)],
-        in_specs=[VMEM] * 5,
+        out_shape=[CHUNKS, planes(4)],
+        in_specs=[VMEM] * 6,
         out_specs=[VMEM] * 2,
         compiler_params=PARAMS,
-    )(own_blocks, shared, alone, table_z, table_y)
+    )(own_blocks, shared_blocks, rows, alone, table_z, table_y)
 
 
 def middle(spectra, kernel, table_x, table_x_back):
@@ -346,15 +377,15 @@
     )(spectra, kernel, table_x, table_x_back)
 
 
-def backward(returned, own_blocks, blocks, table_y_back, table_z_back):
+def backward(returned, own_blocks, shared_blocks, lone_blocks, table_y_back, table_z_back):
     return pl.pallas_call(
         backward_kernel,
         out_shape=[planes(4)] * 4,
-        in_specs=[VMEM] * 5,
+        in_specs=[VMEM] * 6,
         out_specs=[VMEM] * 4,
         scratch_shapes=[pltpu.VMEM((16, N, LANES), jnp.float32)],
         compiler_params=PARAMS,
-    )(returned, own_blocks, blocks, table_y_back, table_z_back)
+    )(returned, own_blocks, shared_blocks, lone_blocks, table_y_back, table_z_back)
 
 
 def share(mine, others, relayed):
@@ -403,10 +434,11 @@
     shared = both_cores(along_band(own, [-s for s in SHARED]))
     own_blocks, own_again = first(own)
     alone = along_band(own_again, [-s for s in ALONE])
-    spectra, blocks = forward(own_blocks, shared, alone, table_z, table_y)
+    rows, shared_blocks = early(own_blocks, shared, table_z, table_y)
+    spectra, lone_blocks = forward(own_blocks, shared_blocks, rows, alone, table_z, table_y)
     returned = exchange(middle(exchange(spectra), kernel, table_x, table_x_back))
     own_field, shared_field, lone_field, other_field = backward(
-        returned, own_blocks, blocks, table_y_back, table_z_back
+        returned, own_blocks, shared_blocks, lone_blocks, table_y_back, table_z_back
     )
     relayed = along_band(lone_field, RELAY)
     shared_field = along_band(share(shared_field, both_cores(other_field), relayed), SHARED)

time: 95.9 us -> 96.9 us (1.010)
  the two profiles are of different devices: /device:TPU:33 before, /device:TPU:1 now
where the time goes in v8:
time: 96.9 us; the launch traced here: 96.6 us
  blocking collectives  40.4 us (42%)
  starting transfers between devices  29.8 us (31%)
  waiting for transfers between devices  18.6 us (19%)
  Pallas kernels  6.64 us (7%)
    all_to_all x2, blocking collectives, exchange(): return lax.all_to_all(value, 'fft', split_axis=0, concat_axis=0, tiled=True)  34.4 us
    ppermute x4, starting transfers between devices, along_band(): return lax.ppermute(value, ('band', 'pool'), pairs)  29.8 us
    ppermute x4, waiting for transfers between devices, along_band(): return lax.ppermute(value, ('band', 'pool'), pairs)  18.6 us
    all_gather x3, blocking collectives, both_cores(): return lax.all_gather(value, 'pool', tiled=True)  5.97 us
  transfers between devices with their start and end apart: 4, of which 4 were waited for; matrix products, arithmetic and copies ran while one was open for 0% of the time, Pallas kernels for 1%

profile of v8, /device:TPU:1, one launch (start us, length us, event | category | flops | bytes accessed | tf_op | source)
XLA Modules:
  0.0 96.6 jit_solution(16565650334463382012)
XLA Ops:
  0.0 13.4 %collective-permute-start = (f32[256,128]{1,0:T(8,128)}, f32[256,128]{1,0:T(8,128)S(1)}, u32[]{:S(2)}, u32[]{:S(2)}) collective-permute-start(f32[256,128]{1,0:T(8,128)} %bitcast.10), channel_id=1, source_target_pairs={{0,96},{1,385},{32,128},{33,417},{64,160},{65,449},{96,192},{97,48... | collective-permute-start | bytes 393224 | tf_op jit(solution)/shard_map/ppermute | solution.py:418
  13.4 0.0 copy-start.7
  13.4 0.9 copy-done.7
  14.3 0.1 shard_map.82
  14.4 4.7 %collective-permute-start.1 = (f32[256,128]{1,0:T(8,128)S(1)}, f32[256,128]{1,0:T(8,128)S(1)}, u32[]{:S(2)}, u32[]{:S(2)}) collective-permute-start(f32[256,128]{1,0:T(8,128)S(1)} %get-tuple-element.18), channel_id=1, source_target_pairs={{0,64},{1,353},{32,96},{33,385},{64,128},{65,417},{96,160},{97,449... | collective-permute-start | bytes 393224 | tf_op jit(solution)/shard_map/ppermute | solution.py:418
  19.2 0.7 collective-permute-done
  19.9 2.0 %all_gather.9.shared = f32[512,128]{1,0:T(8,128)S(1)} all-gather(f32[256,128]{1,0:T(8,128)S(1)} %collective-permute-done), channel_id=1, replica_groups=mesh['band'=16,'fft'=16,'pool'=2] {'pool'}, dimensions={0}, use_global_device_ids=true | all-gather | bytes 393216 | tf_op jit(solution)/shard_map/all_gather | solution.py:422
  21.9 0.0 copy-done
  21.9 0.0 copy-done.1
  21.9 1.2 %shard_map.83 = (f32[16,40,128]{2,1,0:T(8,128)S(1)}, f32[8,64,128]{2,1,0:T(8,128)S(1)}) custom-call(f32[4,64,128]{2,1,0:T(8,128)S(1)} %get-tuple-element.15.own_blocks, f32[512,128]{1,0:T(8,128)S(1)} %all_gather.9.shared, bf16[2,256,256]{2,1,0:T(8,128)(2,1)S(1)} %copy-done.1, bf16[2,256,256]{2,1,0:T(8,128)(2,1)S(1)} %copy-done), custom_call_target="tpu_custom_call" | custom-call | tf_op jit(solution)/shard_map/pallas_call | solution.py:351
  23.1 7.9 %collective-permute-done.1.alone = f32[256,128]{1,0:T(8,128)S(1)} collective-permute-done((f32[256,128]{1,0:T(8,128)S(1)}, f32[256,128]{1,0:T(8,128)S(1)}, u32[]{:S(2)}, u32[]{:S(2)}) %collective-permute-start.1) | collective-permute-done | bytes 131104 | tf_op jit(solution)/shard_map/ppermute | solution.py:418
  31.0 1.2 %shard_map.84 = (f32[16,136,128]{2,1,0:T(8,128)S(1)}, f32[4,64,128]{2,1,0:T(8,128)S(1)}) custom-call(f32[4,64,128]{2,1,0:T(8,128)S(1)} %get-tuple-element.15.own_blocks, f32[8,64,128]{2,1,0:T(8,128)S(1)} %get-tuple-element.16.shared_blocks, f32[16,40,128]{2,1,0:T(8,128)S(1)} %get-tuple-element.17.early, f32[256,128]{1,0:T(8,128)S(1)} %collective-permute-done.1.alone, ...), custom_call_target="tpu_custom_call" | custom-call | tf_op jit(solution)/shard_map/pallas_call | solution.py:361
  32.2 0.0 copy-start.4
  32.2 0.0 copy-start.5
  32.2 0.0 copy-start.6
  32.3 18.8 %all_to_all.10.spectra = f32[16,136,128]{2,1,0:T(8,128)S(1)} all-to-all(f32[16,136,128]{2,1,0:T(8,128)S(1)} %get-tuple-element.19), channel_id=1, replica_groups=mesh['band'=16,'fft'=16,'pool'=2] {'fft'}, dimensions={0} | all-to-all | bytes 2228224 | tf_op jit(solution)/shard_map/all_to_all | solution.py:426
  51.1 0.0 copy-done.4
  51.1 0.0 copy-done.5
  51.1 0.0 copy-done.6
  51.1 1.7 %shard_map.85 = f32[16,136,128]{2,1,0:T(8,128)S(1)} custom-call(f32[16,136,128]{2,1,0:T(8,128)S(1)} %all_to_all.10.spectra, f32[64,256]{1,0:T(8,128)S(1)} %copy-done.6, bf16[2,256,256]{2,1,0:T(8,128)(2,1)S(1)} %copy-done.5, bf16[2,256,256]{2,1,0:T(8,128)(2,1)S(1)} %copy-done.4), custom_call_target="tpu_custom_call" | custom-call | tf_op jit(solution)/shard_map/pallas_call | solution.py:371
  52.8 0.0 copy-start.3
  52.8 15.6 %all_to_all.11.returned = f32[16,136,128]{2,1,0:T(8,128)S(1)} all-to-all(f32[16,136,128]{2,1,0:T(8,128)S(1)} %shard_map.85), channel_id=1, replica_groups=mesh['band'=16,'fft'=16,'pool'=2] {'fft'}, dimensions={0} | all-to-all | bytes 2228224 | tf_op jit(solution)/shard_map/all_to_all | solution.py:426
  68.4 0.0 copy-done.2
  68.4 0.0 copy-done.3
  68.4 1.7 %shard_map.86 = (f32[4,64,128]{2,1,0:T(8,128)S(1)}, f32[4,64,128]{2,1,0:T(8,128)S(1)}, f32[4,64,128]{2,1,0:T(8,128)S(1)}, f32[4,64,128]{2,1,0:T(8,128)S(1)}) custom-call(f32[16,136,128]{2,1,0:T(8,128)S(1)} %all_to_all.11.returned, f32[4,64,128]{2,1,0:T(8,128)S(1)} %get-tuple-element.15.own_blocks, f32[8,64,128]{2,1,0:T(8,128)S(1)} %get-tuple-element.16.shared_blocks, ...), custom_call_target="tpu_custom_call" | custom-call | tf_op jit(solution)/shard_map/pallas_call | solution.py:381
  70.1 3.0 %collective-permute-start.2 = (f32[4,64,128]{2,1,0:T(8,128)S(1)}, f32[4,64,128]{2,1,0:T(8,128)S(1)}, u32[]{:S(2)}, u32[]{:S(2)}) collective-permute-start(f32[4,64,128]{2,1,0:T(8,128)S(1)} %get-tuple-element.23), channel_id=1, source_target_pairs={{0,32},{1,33},{32,64},{33,65},{64,96},{65,97},{96,128},{97,129},{1... | collective-permute-start | bytes 393224 | tf_op jit(solution)/shard_map/ppermute | solution.py:418
  73.1 2.0 %all_gather.10.others = f32[8,64,128]{2,1,0:T(8,128)S(1)} all-gather(f32[4,64,128]{2,1,0:T(8,128)S(1)} %get-tuple-element.22), channel_id=1, replica_groups=mesh['band'=16,'fft'=16,'pool'=2] {'pool'}, dimensions={0}, use_global_device_ids=true | all-gather | bytes 393216 | tf_op jit(solution)/shard_map/all_gather | solution.py:422
  75.1 1.9 %collective-permute-done.2.relayed = f32[4,64,128]{2,1,0:T(8,128)S(1)} collective-permute-done((f32[4,64,128]{2,1,0:T(8,128)S(1)}, f32[4,64,128]{2,1,0:T(8,128)S(1)}, u32[]{:S(2)}, u32[]{:S(2)}) %collective-permute-start.2) | collective-permute-done | bytes 131104 | tf_op jit(solution)/shard_map/ppermute | solution.py:418
  77.0 8.7 %collective-permute-start.3 = (f32[4,64,128]{2,1,0:T(8,128)S(1)}, f32[4,64,128]{2,1,0:T(8,128)S(1)}, u32[]{:S(2)}, u32[]{:S(2)}) collective-permute-start(f32[4,64,128]{2,1,0:T(8,128)S(1)} %shard_map.87), channel_id=1, source_target_pairs={{0,416},{1,129},{32,448},{33,161},{64,480},{65,193},{96,0},{97,225... | collective-permute-start | bytes 393224 | tf_op jit(solution)/shard_map/ppermute | solution.py:418
  85.7 8.1 %collective-permute-done.3 = f32[4,64,128]{2,1,0:T(8,128)S(1)} collective-permute-done((f32[4,64,128]{2,1,0:T(8,128)S(1)}, f32[4,64,128]{2,1,0:T(8,128)S(1)}, u32[]{:S(2)}, u32[]{:S(2)}) %collective-permute-start.3) | collective-permute-done | bytes 131104 | tf_op jit(solution)/shard_map/ppermute | solution.py:418
  93.8 2.0 %all_gather.11.both = f32[8,64,128]{2,1,0:T(8,128)S(1)} all-gather(f32[4,64,128]{2,1,0:T(8,128)S(1)} %add.3), channel_id=1, replica_groups=mesh['band'=16,'fft'=16,'pool'=2] {'pool'}, dimensions={0}, use_global_device_ids=true | all-gather | bytes 393216 | tf_op jit(solution)/shard_map/all_gather | solution.py:422
  95.8 0.8 shard_map.88
  (5 shorter events, 0.0 us)
Async XLA Ops:
  0.0 21.9 %copy-start = (bf16[2,256,256]{2,1,0:T(8,128)(2,1)S(1)}, bf16[2,256,256]{2,1,0:T(8,128)(2,1)}, u32[]{:S(2)}) copy-start(bf16[2,256,256]{2,1,0:T(8,128)(2,1)} %constant.13.clone.table_y) | copy-start | bytes 786436
  0.0 21.9 %copy-start.1 = (bf16[2,256,256]{2,1,0:T(8,128)(2,1)S(1)}, bf16[2,256,256]{2,1,0:T(8,128)(2,1)}, u32[]{:S(2)}) copy-start(bf16[2,256,256]{2,1,0:T(8,128)(2,1)} %constant.12.clone.table_z) | copy-start | bytes 786436
  0.0 19.9 %collective-permute-start = (f32[256,128]{1,0:T(8,128)}, f32[256,128]{1,0:T(8,128)S(1)}, u32[]{:S(2)}, u32[]{:S(2)}) collective-permute-start(f32[256,128]{1,0:T(8,128)} %bitcast.10), channel_id=1, source_target_pairs={{0,96},{1,385},{32,128},{33,417},{64,160},{65,449},{96,192},{97,48... | collective-permute-start | bytes 393224 | tf_op jit(solution)/shard_map/ppermute | solution.py:418
  13.4 0.9 copy-start.7
  14.4 16.5 %collective-permute-start.1 = (f32[256,128]{1,0:T(8,128)S(1)}, f32[256,128]{1,0:T(8,128)S(1)}, u32[]{:S(2)}, u32[]{:S(2)}) collective-permute-start(f32[256,128]{1,0:T(8,128)S(1)} %get-tuple-element.18), channel_id=1, source_target_pairs={{0,64},{1,353},{32,96},{33,385},{64,128},{65,417},{96,160},{97,449... | collective-permute-start | bytes 393224 | tf_op jit(solution)/shard_map/ppermute | solution.py:418
  32.2 18.9 %copy-start.4 = (bf16[2,256,256]{2,1,0:T(8,128)(2,1)S(1)}, bf16[2,256,256]{2,1,0:T(8,128)(2,1)}, u32[]{:S(2)}) copy-start(bf16[2,256,256]{2,1,0:T(8,128)(2,1)} %constant.15.clone.table_x_back) | copy-start | bytes 786436
  32.2 18.9 %copy-start.5 = (bf16[2,256,256]{2,1,0:T(8,128)(2,1)S(1)}, bf16[2,256,256]{2,1,0:T(8,128)(2,1)}, u32[]{:S(2)}) copy-start(bf16[2,256,256]{2,1,0:T(8,128)(2,1)} %constant.14.clone.table_x) | copy-start | bytes 786436
  32.2 18.8 %copy-start.6 = (f32[64,256]{1,0:T(8,128)S(1)}, f32[64,256]{1,0:T(8,128)}, u32[]{:S(2)}) copy-start(f32[64,256]{1,0:T(8,128)} %kernel.1) | copy-start | bytes 196612
  52.8 15.6 %copy-start.2 = (bf16[2,256,256]{2,1,0:T(8,128)(2,1)S(1)}, bf16[2,256,256]{2,1,0:T(8,128)(2,1)}, u32[]{:S(2)}) copy-start(bf16[2,256,256]{2,1,0:T(8,128)(2,1)} %constant.17.clone.table_z_back) | copy-start | bytes 786436
  52.8 15.6 %copy-start.3 = (bf16[2,256,256]{2,1,0:T(8,128)(2,1)S(1)}, bf16[2,256,256]{2,1,0:T(8,128)(2,1)}, u32[]{:S(2)}) copy-start(bf16[2,256,256]{2,1,0:T(8,128)(2,1)} %constant.16.clone.table_y_back) | copy-start | bytes 786436
  70.1 6.9 %collective-permute-start.2 = (f32[4,64,128]{2,1,0:T(8,128)S(1)}, f32[4,64,128]{2,1,0:T(8,128)S(1)}, u32[]{:S(2)}, u32[]{:S(2)}) collective-permute-start(f32[4,64,128]{2,1,0:T(8,128)S(1)} %get-tuple-element.23), channel_id=1, source_target_pairs={{0,32},{1,33},{32,64},{33,65},{64,96},{65,97},{96,128},{97,129},{1... | collective-permute-start | bytes 393224 | tf_op jit(solution)/shard_map/ppermute | solution.py:418
  77.0 16.7 %collective-permute-start.3 = (f32[4,64,128]{2,1,0:T(8,128)S(1)}, f32[4,64,128]{2,1,0:T(8,128)S(1)}, u32[]{:S(2)}, u32[]{:S(2)}) collective-permute-start(f32[4,64,128]{2,1,0:T(8,128)S(1)} %shard_map.87), channel_id=1, source_target_pairs={{0,416},{1,129},{32,448},{33,161},{64,480},{65,193},{96,0},{97,225... | collective-permute-start | bytes 393224 | tf_op jit(solution)/shard_map/ppermute | solution.py:418

commit v9 on v7

--- a/solution.py
+++ b/solution.py
@@ -16,11 +16,11 @@
 ROWS = 32 * UNITS + 8
 
 SHARED = (-3, 4)
-ALONE = (-2, 5)
-RELAY = tuple(lone - shared for lone, shared in zip(ALONE, SHARED))
-MEETINGS = (((0, 2), (0, 2)), ((0, 1), (0, 1)), ((1, 2), (1, 3)), ((2, 3), (2, 3)))
+ALONE = (5, -2)
+RELAY = (1, 1)
+MEETINGS = (((0, 2), (0, 2)), ((0, 1), (0, 1)), ((1, 3), (2, 3)), ((1, 2), (1, 2)))
 EIGHT = 3
-EIGHT_CORE = 1
+EIGHT_CORE = 0
 
 
 def wave_parts(rows, columns):
@@ -377,10 +377,10 @@
     )(both)
 
 
-def along_band(value, steps):
+def along_band(value, steps, crossed=False):
     count = lax.axis_size("band")
     pairs = [
-        (2 * source + core, 2 * ((source + steps[core]) % count) + core)
+        (2 * source + core, 2 * ((source + steps[core]) % count) + (core ^ crossed))
         for source in range(count)
         for core in range(2)
     ]
@@ -408,7 +408,7 @@
     own_field, shared_field, lone_field, other_field = backward(
         returned, own_blocks, blocks, table_y_back, table_z_back
     )
-    relayed = along_band(lone_field, RELAY)
+    relayed = along_band(lone_field, RELAY, True)
     shared_field = along_band(share(shared_field, both_cores(other_field), relayed), SHARED)
     field = final(both_cores(shared_field + own_field))
     return field.reshape(2, HALF, 4, LANES).transpose(0, 2, 1, 3).reshape(2, 4, N * N)

time: 95.9 us -> 92.4 us (0.964)
  the two profiles are of different devices: /device:TPU:33 before, /device:TPU:1 now
where the time goes in v9:
time: 92.4 us; the launch traced here: 91.1 us
  blocking collectives  41.9 us (45%)
  starting transfers between devices  34.6 us (37%)
  waiting for transfers between devices  7.49 us (8%)
  Pallas kernels  6.01 us (7%)
  local copies, waits for them, and re-layouts  0.95 us (1%)
    ppermute x4, starting transfers between devices, along_band(): return lax.ppermute(value, ('band', 'pool'), pairs)  34.6 us
    all_to_all x2, blocking collectives, exchange(): return lax.all_to_all(value, 'fft', split_axis=0, concat_axis=0, tiled=True)  34.3 us
    all_gather x3, blocking collectives, both_cores(): return lax.all_gather(value, 'pool', tiled=True)  7.6 us
    ppermute x4, waiting for transfers between devices, along_band(): return lax.ppermute(value, ('band', 'pool'), pairs)  7.49 us
  transfers between devices with their start and end apart: 4, of which 4 were waited for; matrix products, arithmetic and copies ran while one was open for 0% of the time, Pallas kernels for 0%

profile of v9, /device:TPU:1, one launch (start us, length us, event | category | flops | bytes accessed | tf_op | source)
XLA Modules:
  0.0 91.1 jit_solution(1325855716721252377)
XLA Ops:
  0.0 0.0 copy-start.2
  0.0 13.4 %collective-permute-start = (f32[256,128]{1,0:T(8,128)}, f32[256,128]{1,0:T(8,128)S(1)}, u32[]{:S(2)}, u32[]{:S(2)}) collective-permute-start(f32[256,128]{1,0:T(8,128)} %bitcast.10), channel_id=1, source_target_pairs={{0,96},{1,385},{32,128},{33,417},{64,160},{65,449},{96,192},{97,48... | collective-permute-start | bytes 393224 | tf_op jit(solution)/shard_map/ppermute | solution.py:387
  13.4 0.0 copy-start.7
  13.4 0.9 copy-done.7
  14.3 0.1 shard_map.82
  14.4 3.1 %collective-permute-start.1 = (f32[256,128]{1,0:T(8,128)S(1)}, f32[256,128]{1,0:T(8,128)S(1)}, u32[]{:S(2)}, u32[]{:S(2)}) collective-permute-start(f32[256,128]{1,0:T(8,128)S(1)} %get-tuple-element.14), channel_id=1, source_target_pairs={{0,352},{1,65},{32,384},{33,97},{64,416},{65,129},{96,448},{97,161... | collective-permute-start | bytes 393224 | tf_op jit(solution)/shard_map/ppermute | solution.py:387
  17.5 4.2 %collective-permute-done = f32[256,128]{1,0:T(8,128)S(1)} collective-permute-done((f32[256,128]{1,0:T(8,128)}, f32[256,128]{1,0:T(8,128)S(1)}, u32[]{:S(2)}, u32[]{:S(2)}) %collective-permute-start) | collective-permute-done | bytes 131104 | tf_op jit(solution)/shard_map/ppermute | solution.py:387
  21.7 2.0 %all_gather.9.shared = f32[512,128]{1,0:T(8,128)S(1)} all-gather(f32[256,128]{1,0:T(8,128)S(1)} %collective-permute-done), channel_id=1, replica_groups=mesh['band'=16,'fft'=16,'pool'=2] {'pool'}, dimensions={0}, use_global_device_ids=true | all-gather | bytes 393216 | tf_op jit(solution)/shard_map/all_gather | solution.py:391
  23.7 0.1 collective-permute-done.1.alone
  23.8 0.0 copy-done.2
  23.8 0.0 copy-done.3
  23.8 1.8 %shard_map.83 = (f32[16,136,128]{2,1,0:T(8,128)S(1)}, f32[12,64,128]{2,1,0:T(8,128)S(1)}) custom-call(f32[4,64,128]{2,1,0:T(8,128)S(1)} %get-tuple-element.13.own_blocks, f32[512,128]{1,0:T(8,128)S(1)} %all_gather.9.shared, f32[256,128]{1,0:T(8,128)S(1)} %collective-permute-done.1.alone, bf16[2,256,256]{2,1,0:T(8,128)(2,1)S(1)} %copy-done.3, ...), custom_call_target="tpu_custom_call" | custom-call | tf_op jit(solution)/shard_map/pallas_call | solution.py:330
  25.6 0.0 copy-start.4
  25.6 0.0 copy-start.5
  25.6 0.0 copy-start.6
  25.6 18.9 %all_to_all.10.spectra = f32[16,136,128]{2,1,0:T(8,128)S(1)} all-to-all(f32[16,136,128]{2,1,0:T(8,128)S(1)} %get-tuple-element.15), channel_id=1, replica_groups=mesh['band'=16,'fft'=16,'pool'=2] {'fft'}, dimensions={0} | all-to-all | bytes 2228224 | tf_op jit(solution)/shard_map/all_to_all | solution.py:395
  44.5 0.0 copy-done.4
  44.5 0.0 copy-done.5
  44.5 0.0 copy-done.6
  44.5 1.7 %shard_map.84 = f32[16,136,128]{2,1,0:T(8,128)S(1)} custom-call(f32[16,136,128]{2,1,0:T(8,128)S(1)} %all_to_all.10.spectra, f32[64,256]{1,0:T(8,128)S(1)} %copy-done.6, bf16[2,256,256]{2,1,0:T(8,128)(2,1)S(1)} %copy-done.5, bf16[2,256,256]{2,1,0:T(8,128)(2,1)S(1)} %copy-done.4), custom_call_target="tpu_custom_call" | custom-call | tf_op jit(solution)/shard_map/pallas_call | solution.py:340
  46.2 0.0 copy-start.1
  46.2 15.4 %all_to_all.11.returned = f32[16,136,128]{2,1,0:T(8,128)S(1)} all-to-all(f32[16,136,128]{2,1,0:T(8,128)S(1)} %shard_map.84), channel_id=1, replica_groups=mesh['band'=16,'fft'=16,'pool'=2] {'fft'}, dimensions={0} | all-to-all | bytes 2228224 | tf_op jit(solution)/shard_map/all_to_all | solution.py:395
  61.7 0.0 copy-done
  61.7 0.0 copy-done.1
  61.7 1.7 %shard_map.85 = (f32[4,64,128]{2,1,0:T(8,128)S(1)}, f32[4,64,128]{2,1,0:T(8,128)S(1)}, f32[4,64,128]{2,1,0:T(8,128)S(1)}, f32[4,64,128]{2,1,0:T(8,128)S(1)}) custom-call(f32[16,136,128]{2,1,0:T(8,128)S(1)} %all_to_all.11.returned, f32[4,64,128]{2,1,0:T(8,128)S(1)} %get-tuple-element.13.own_blocks, f32[12,64,128]{2,1,0:T(8,128)S(1)} %get-tuple-element.16.blocks, ...), custom_call_target="tpu_custom_call" | custom-call | tf_op jit(solution)/shard_map/pallas_call | solution.py:350
  63.3 10.6 %collective-permute-start.2 = (f32[4,64,128]{2,1,0:T(8,128)S(1)}, f32[4,64,128]{2,1,0:T(8,128)S(1)}, u32[]{:S(2)}, u32[]{:S(2)}) collective-permute-start(f32[4,64,128]{2,1,0:T(8,128)S(1)} %get-tuple-element.19), channel_id=1, source_target_pairs={{0,33},{1,32},{32,65},{33,64},{64,97},{65,96},{96,129},{97,128},{1... | collective-permute-start | bytes 393224 | tf_op jit(solution)/shard_map/ppermute | solution.py:387
  73.9 2.0 %all_gather.10.others = f32[8,64,128]{2,1,0:T(8,128)S(1)} all-gather(f32[4,64,128]{2,1,0:T(8,128)S(1)} %get-tuple-element.18), channel_id=1, replica_groups=mesh['band'=16,'fft'=16,'pool'=2] {'pool'}, dimensions={0}, use_global_device_ids=true | all-gather | bytes 393216 | tf_op jit(solution)/shard_map/all_gather | solution.py:391
  75.9 0.7 collective-permute-done.2.relayed
  76.7 7.5 %collective-permute-start.3 = (f32[4,64,128]{2,1,0:T(8,128)S(1)}, f32[4,64,128]{2,1,0:T(8,128)S(1)}, u32[]{:S(2)}, u32[]{:S(2)}) collective-permute-start(f32[4,64,128]{2,1,0:T(8,128)S(1)} %shard_map.86), channel_id=1, source_target_pairs={{0,416},{1,129},{32,448},{33,161},{64,480},{65,193},{96,0},{97,225... | collective-permute-start | bytes 393224 | tf_op jit(solution)/shard_map/ppermute | solution.py:387
  84.2 2.5 %collective-permute-done.3 = f32[4,64,128]{2,1,0:T(8,128)S(1)} collective-permute-done((f32[4,64,128]{2,1,0:T(8,128)S(1)}, f32[4,64,128]{2,1,0:T(8,128)S(1)}, u32[]{:S(2)}, u32[]{:S(2)}) %collective-permute-start.3) | collective-permute-done | bytes 131104 | tf_op jit(solution)/shard_map/ppermute | solution.py:387
  86.8 3.6 %all_gather.11.both = f32[8,64,128]{2,1,0:T(8,128)S(1)} all-gather(f32[4,64,128]{2,1,0:T(8,128)S(1)} %add.3), channel_id=1, replica_groups=mesh['band'=16,'fft'=16,'pool'=2] {'pool'}, dimensions={0}, use_global_device_ids=true | all-gather | bytes 393216 | tf_op jit(solution)/shard_map/all_gather | solution.py:391
  90.3 0.8 shard_map.87
  (4 shorter events, 0.0 us)
Async XLA Ops:
  0.0 23.8 %copy-start.2 = (bf16[2,256,256]{2,1,0:T(8,128)(2,1)S(1)}, bf16[2,256,256]{2,1,0:T(8,128)(2,1)}, u32[]{:S(2)}) copy-start(bf16[2,256,256]{2,1,0:T(8,128)(2,1)} %constant.13.clone.table_y) | copy-start | bytes 786436
  0.0 23.8 %copy-start.3 = (bf16[2,256,256]{2,1,0:T(8,128)(2,1)S(1)}, bf16[2,256,256]{2,1,0:T(8,128)(2,1)}, u32[]{:S(2)}) copy-start(bf16[2,256,256]{2,1,0:T(8,128)(2,1)} %constant.12.clone.table_z) | copy-start | bytes 786436
  0.0 21.7 %collective-permute-start = (f32[256,128]{1,0:T(8,128)}, f32[256,128]{1,0:T(8,128)S(1)}, u32[]{:S(2)}, u32[]{:S(2)}) collective-permute-start(f32[256,128]{1,0:T(8,128)} %bitcast.10), channel_id=1, source_target_pairs={{0,96},{1,385},{32,128},{33,417},{64,160},{65,449},{96,192},{97,48... | collective-permute-start | bytes 393224 | tf_op jit(solution)/shard_map/ppermute | solution.py:387
  13.4 0.9 %copy-start.7 = (f32[2,4,4096]{2,1,0:T(4,128)S(1)}, f32[2,4,4096]{2,1,0:T(4,128)}, u32[]{:S(2)}) copy-start(f32[2,4,4096]{2,1,0:T(4,128)} %param.8) | copy-start | bytes 393220
  14.4 9.3 %collective-permute-start.1 = (f32[256,128]{1,0:T(8,128)S(1)}, f32[256,128]{1,0:T(8,128)S(1)}, u32[]{:S(2)}, u32[]{:S(2)}) collective-permute-start(f32[256,128]{1,0:T(8,128)S(1)} %get-tuple-element.14), channel_id=1, source_target_pairs={{0,352},{1,65},{32,384},{33,97},{64,416},{65,129},{96,448},{97,161... | collective-permute-start | bytes 393224 | tf_op jit(solution)/shard_map/ppermute | solution.py:387
  25.6 18.9 %copy-start.4 = (bf16[2,256,256]{2,1,0:T(8,128)(2,1)S(1)}, bf16[2,256,256]{2,1,0:T(8,128)(2,1)}, u32[]{:S(2)}) copy-start(bf16[2,256,256]{2,1,0:T(8,128)(2,1)} %constant.15.clone.table_x_back) | copy-start | bytes 786436
  25.6 18.9 %copy-start.5 = (bf16[2,256,256]{2,1,0:T(8,128)(2,1)S(1)}, bf16[2,256,256]{2,1,0:T(8,128)(2,1)}, u32[]{:S(2)}) copy-start(bf16[2,256,256]{2,1,0:T(8,128)(2,1)} %constant.14.clone.table_x) | copy-start | bytes 786436
  25.6 18.9 %copy-start.6 = (f32[64,256]{1,0:T(8,128)S(1)}, f32[64,256]{1,0:T(8,128)}, u32[]{:S(2)}) copy-start(f32[64,256]{1,0:T(8,128)} %kernel.1) | copy-start | bytes 196612
  46.2 15.5 %copy-start = (bf16[2,256,256]{2,1,0:T(8,128)(2,1)S(1)}, bf16[2,256,256]{2,1,0:T(8,128)(2,1)}, u32[]{:S(2)}) copy-start(bf16[2,256,256]{2,1,0:T(8,128)(2,1)} %constant.17.clone.table_z_back) | copy-start | bytes 786436
  46.2 15.5 %copy-start.1 = (bf16[2,256,256]{2,1,0:T(8,128)(2,1)S(1)}, bf16[2,256,256]{2,1,0:T(8,128)(2,1)}, u32[]{:S(2)}) copy-start(bf16[2,256,256]{2,1,0:T(8,128)(2,1)} %constant.16.clone.table_y_back) | copy-start | bytes 786436
  63.3 13.3 %collective-permute-start.2 = (f32[4,64,128]{2,1,0:T(8,128)S(1)}, f32[4,64,128]{2,1,0:T(8,128)S(1)}, u32[]{:S(2)}, u32[]{:S(2)}) collective-permute-start(f32[4,64,128]{2,1,0:T(8,128)S(1)} %get-tuple-element.19), channel_id=1, source_target_pairs={{0,33},{1,32},{32,65},{33,64},{64,97},{65,96},{96,129},{97,128},{1... | collective-permute-start | bytes 393224 | tf_op jit(solution)/shard_map/ppermute | solution.py:387
  76.7 10.1 %collective-permute-start.3 = (f32[4,64,128]{2,1,0:T(8,128)S(1)}, f32[4,64,128]{2,1,0:T(8,128)S(1)}, u32[]{:S(2)}, u32[]{:S(2)}) collective-permute-start(f32[4,64,128]{2,1,0:T(8,128)S(1)} %shard_map.86), channel_id=1, source_target_pairs={{0,416},{1,129},{32,448},{33,161},{64,480},{65,193},{96,0},{97,225... | collective-permute-start | bytes 393224 | tf_op jit(solution)/shard_map/ppermute | solution.py:387

commit v10 on v9

--- a/solution.py
+++ b/solution.py
@@ -173,8 +173,8 @@
     last = []
     for at, behind in ((own_blocks[0], own_blocks[2]), (own_blocks[1], own_blocks[3])):
         pairs = jnp.where(low_lanes(N), at * swap(at), behind * swap(behind))
-        last.append(jnp.concatenate([pairs, jnp.zeros((N, LANES), jnp.float32)], axis=1))
-    rows = spectrum(last, table_z, table_y)
+        last.append(pairs)
+    rows = spectrum(last, table_z[:, :LANES], table_y)
     out[:, 32 * UNITS :, :] = jnp.where(on_first(), rows[:, :8], rows[:, 8:])
 
 
@@ -226,7 +226,15 @@
     other_field,
     fields,
 ):
-    fields[...] = jnp.zeros_like(fields)
+    started = set()
+
+    def add(place, plane, value):
+        if not isinstance(place, int) or (place, plane) in started:
+            fields[4 * place + plane] += value
+        else:
+            started.add((place, plane))
+            fields[4 * place + plane] = value
+
     read = reader(own_blocks, blocks)
 
     def collect(unit, half, plane, potential):
@@ -237,11 +245,11 @@
             squares = jnp.where(on_eight(), potential, 0.0)
             potential = potential - squares
             given = jnp.where(on_eight(), 0.0, given)
-            fields[plane] += squares * read(0, plane)
-        fields[4 * left + plane] += potential * partner
-        fields[4 * right + plane] += given
-
-    def potentials(pairs):
+            add(0, plane, squares * read(0, plane))
+        add(left, plane, potential * partner)
+        add(right, plane, given)
+
+    def potentials(pairs, table_z_back):
         rows = table_times(table_y_back, jnp.concatenate(pairs, axis=1))
         planes_of = [
             jnp.concatenate(
@@ -265,7 +273,7 @@
             at = 32 * u + 8 * high
             both = [returned[:, at : at + 8, :], returned[:, at + 16 : at + 24, :]]
             pairs.append(jnp.concatenate(both, axis=1).reshape(256, LANES))
-        rows = potentials(pairs)
+        rows = potentials(pairs, table_z_back)
         for plane in range(4):
             for half in range(2):
                 collect(
@@ -276,7 +284,8 @@
                 )
     last = returned[:, 32 * UNITS :, :]
     last = [jnp.where(on_first(), last, 0.0), jnp.where(on_first(), 0.0, last)]
-    rows = potentials([jnp.concatenate(last, axis=1).reshape(256, LANES)])
+    last = [jnp.concatenate(last, axis=1).reshape(256, LANES)]
+    rows = potentials(last, table_z_back[:, :, :LANES])
     low = low_lanes(N)
     for at in range(2):
         potential = rows[at * N : at * N + N, :LANES]

time: 92.4 us -> 92.4 us (level)
  no operation moved by 1% of the time
where the time goes in v10:
time: 92.4 us; the launch traced here: 91.1 us
  blocking collectives  41.9 us (45%)
  starting transfers between devices  34.6 us (37%)
  waiting for transfers between devices  7.48 us (8%)
  Pallas kernels  6.05 us (7%)
  local copies, waits for them, and re-layouts  0.95 us (1%)
    ppermute x4, starting transfers between devices, along_band(): return lax.ppermute(value, ('band', 'pool'), pairs)  34.6 us
    all_to_all x2, blocking collectives, exchange(): return lax.all_to_all(value, 'fft', split_axis=0, concat_axis=0, tiled=True)  34.3 us
    all_gather x3, blocking collectives, both_cores(): return lax.all_gather(value, 'pool', tiled=True)  7.61 us
    ppermute x4, waiting for transfers between devices, along_band(): return lax.ppermute(value, ('band', 'pool'), pairs)  7.48 us
  transfers between devices with their start and end apart: 4, of which 4 were waited for; matrix products, arithmetic and copies ran while one was open for 0% of the time, Pallas kernels for 0%

profile of v10, /device:TPU:1, one launch (start us, length us, event | category | flops | bytes accessed | tf_op | source)
XLA Modules:
  0.0 91.1 jit_solution(8603919697414097160)
XLA Ops:
  0.0 0.0 copy-start.2
  0.0 13.4 %collective-permute-start = (f32[256,128]{1,0:T(8,128)}, f32[256,128]{1,0:T(8,128)S(1)}, u32[]{:S(2)}, u32[]{:S(2)}) collective-permute-start(f32[256,128]{1,0:T(8,128)} %bitcast.10), channel_id=1, source_target_pairs={{0,96},{1,385},{32,128},{33,417},{64,160},{65,449},{96,192},{97,48... | collective-permute-start | bytes 393224 | tf_op jit(solution)/shard_map/ppermute | solution.py:396
  13.4 0.0 copy-start.7
  13.4 0.9 copy-done.7
  14.3 0.1 shard_map.82
  14.4 3.1 %collective-permute-start.1 = (f32[256,128]{1,0:T(8,128)S(1)}, f32[256,128]{1,0:T(8,128)S(1)}, u32[]{:S(2)}, u32[]{:S(2)}) collective-permute-start(f32[256,128]{1,0:T(8,128)S(1)} %get-tuple-element.14), channel_id=1, source_target_pairs={{0,352},{1,65},{32,384},{33,97},{64,416},{65,129},{96,448},{97,161... | collective-permute-start | bytes 393224 | tf_op jit(solution)/shard_map/ppermute | solution.py:396
  17.5 4.2 %collective-permute-done = f32[256,128]{1,0:T(8,128)S(1)} collective-permute-done((f32[256,128]{1,0:T(8,128)}, f32[256,128]{1,0:T(8,128)S(1)}, u32[]{:S(2)}, u32[]{:S(2)}) %collective-permute-start) | collective-permute-done | bytes 131104 | tf_op jit(solution)/shard_map/ppermute | solution.py:396
  21.7 2.0 %all_gather.9.shared = f32[512,128]{1,0:T(8,128)S(1)} all-gather(f32[256,128]{1,0:T(8,128)S(1)} %collective-permute-done), channel_id=1, replica_groups=mesh['band'=16,'fft'=16,'pool'=2] {'pool'}, dimensions={0}, use_global_device_ids=true | all-gather | bytes 393216 | tf_op jit(solution)/shard_map/all_gather | solution.py:400
  23.7 0.1 collective-permute-done.1.alone
  23.8 0.0 copy-done.2
  23.8 0.0 copy-done.3
  23.8 1.8 %shard_map.83 = (f32[16,136,128]{2,1,0:T(8,128)S(1)}, f32[12,64,128]{2,1,0:T(8,128)S(1)}) custom-call(f32[4,64,128]{2,1,0:T(8,128)S(1)} %get-tuple-element.13.own_blocks, f32[512,128]{1,0:T(8,128)S(1)} %all_gather.9.shared, f32[256,128]{1,0:T(8,128)S(1)} %collective-permute-done.1.alone, bf16[2,256,256]{2,1,0:T(8,128)(2,1)S(1)} %copy-done.3, ...), custom_call_target="tpu_custom_call" | custom-call | tf_op jit(solution)/shard_map/pallas_call | solution.py:339
  25.6 0.0 copy-start.4
  25.6 0.0 copy-start.5
  25.6 0.0 copy-start.6
  25.6 18.9 %all_to_all.10.spectra = f32[16,136,128]{2,1,0:T(8,128)S(1)} all-to-all(f32[16,136,128]{2,1,0:T(8,128)S(1)} %get-tuple-element.15), channel_id=1, replica_groups=mesh['band'=16,'fft'=16,'pool'=2] {'fft'}, dimensions={0} | all-to-all | bytes 2228224 | tf_op jit(solution)/shard_map/all_to_all | solution.py:404
  44.5 0.0 copy-done.4
  44.5 0.0 copy-done.5
  44.5 0.0 copy-done.6
  44.5 1.7 %shard_map.84 = f32[16,136,128]{2,1,0:T(8,128)S(1)} custom-call(f32[16,136,128]{2,1,0:T(8,128)S(1)} %all_to_all.10.spectra, f32[64,256]{1,0:T(8,128)S(1)} %copy-done.6, bf16[2,256,256]{2,1,0:T(8,128)(2,1)S(1)} %copy-done.5, bf16[2,256,256]{2,1,0:T(8,128)(2,1)S(1)} %copy-done.4), custom_call_target="tpu_custom_call" | custom-call | tf_op jit(solution)/shard_map/pallas_call | solution.py:349
  46.2 0.0 copy-start.1
  46.2 15.4 %all_to_all.11.returned = f32[16,136,128]{2,1,0:T(8,128)S(1)} all-to-all(f32[16,136,128]{2,1,0:T(8,128)S(1)} %shard_map.84), channel_id=1, replica_groups=mesh['band'=16,'fft'=16,'pool'=2] {'fft'}, dimensions={0} | all-to-all | bytes 2228224 | tf_op jit(solution)/shard_map/all_to_all | solution.py:404
  61.7 0.0 copy-done
  61.7 0.0 copy-done.1
  61.7 1.7 %shard_map.85 = (f32[4,64,128]{2,1,0:T(8,128)S(1)}, f32[4,64,128]{2,1,0:T(8,128)S(1)}, f32[4,64,128]{2,1,0:T(8,128)S(1)}, f32[4,64,128]{2,1,0:T(8,128)S(1)}) custom-call(f32[16,136,128]{2,1,0:T(8,128)S(1)} %all_to_all.11.returned, f32[4,64,128]{2,1,0:T(8,128)S(1)} %get-tuple-element.13.own_blocks, f32[12,64,128]{2,1,0:T(8,128)S(1)} %get-tuple-element.16.blocks, ...), custom_call_target="tpu_custom_call" | custom-call | tf_op jit(solution)/shard_map/pallas_call | solution.py:359
  63.4 10.5 %collective-permute-start.2 = (f32[4,64,128]{2,1,0:T(8,128)S(1)}, f32[4,64,128]{2,1,0:T(8,128)S(1)}, u32[]{:S(2)}, u32[]{:S(2)}) collective-permute-start(f32[4,64,128]{2,1,0:T(8,128)S(1)} %get-tuple-element.19), channel_id=1, source_target_pairs={{0,33},{1,32},{32,65},{33,64},{64,97},{65,96},{96,129},{97,128},{1... | collective-permute-start | bytes 393224 | tf_op jit(solution)/shard_map/ppermute | solution.py:396
  73.9 2.1 %all_gather.10.others = f32[8,64,128]{2,1,0:T(8,128)S(1)} all-gather(f32[4,64,128]{2,1,0:T(8,128)S(1)} %get-tuple-element.18), channel_id=1, replica_groups=mesh['band'=16,'fft'=16,'pool'=2] {'pool'}, dimensions={0}, use_global_device_ids=true | all-gather | bytes 393216 | tf_op jit(solution)/shard_map/all_gather | solution.py:400
  76.0 0.7 collective-permute-done.2.relayed
  76.7 7.5 %collective-permute-start.3 = (f32[4,64,128]{2,1,0:T(8,128)S(1)}, f32[4,64,128]{2,1,0:T(8,128)S(1)}, u32[]{:S(2)}, u32[]{:S(2)}) collective-permute-start(f32[4,64,128]{2,1,0:T(8,128)S(1)} %shard_map.86), channel_id=1, source_target_pairs={{0,416},{1,129},{32,448},{33,161},{64,480},{65,193},{96,0},{97,225... | collective-permute-start | bytes 393224 | tf_op jit(solution)/shard_map/ppermute | solution.py:396
  84.2 2.5 %collective-permute-done.3 = f32[4,64,128]{2,1,0:T(8,128)S(1)} collective-permute-done((f32[4,64,128]{2,1,0:T(8,128)S(1)}, f32[4,64,128]{2,1,0:T(8,128)S(1)}, u32[]{:S(2)}, u32[]{:S(2)}) %collective-permute-start.3) | collective-permute-done | bytes 131104 | tf_op jit(solution)/shard_map/ppermute | solution.py:396
  86.8 3.6 %all_gather.11.both = f32[8,64,128]{2,1,0:T(8,128)S(1)} all-gather(f32[4,64,128]{2,1,0:T(8,128)S(1)} %add.3), channel_id=1, replica_groups=mesh['band'=16,'fft'=16,'pool'=2] {'pool'}, dimensions={0}, use_global_device_ids=true | all-gather | bytes 393216 | tf_op jit(solution)/shard_map/all_gather | solution.py:400
  90.4 0.8 shard_map.87
  (4 shorter events, 0.0 us)
Async XLA Ops:
  0.0 23.8 %copy-start.2 = (bf16[2,256,256]{2,1,0:T(8,128)(2,1)S(1)}, bf16[2,256,256]{2,1,0:T(8,128)(2,1)}, u32[]{:S(2)}) copy-start(bf16[2,256,256]{2,1,0:T(8,128)(2,1)} %constant.13.clone.table_y) | copy-start | bytes 786436
  0.0 23.8 %copy-start.3 = (bf16[2,256,256]{2,1,0:T(8,128)(2,1)S(1)}, bf16[2,256,256]{2,1,0:T(8,128)(2,1)}, u32[]{:S(2)}) copy-start(bf16[2,256,256]{2,1,0:T(8,128)(2,1)} %constant.12.clone.table_z) | copy-start | bytes 786436
  0.0 21.7 %collective-permute-start = (f32[256,128]{1,0:T(8,128)}, f32[256,128]{1,0:T(8,128)S(1)}, u32[]{:S(2)}, u32[]{:S(2)}) collective-permute-start(f32[256,128]{1,0:T(8,128)} %bitcast.10), channel_id=1, source_target_pairs={{0,96},{1,385},{32,128},{33,417},{64,160},{65,449},{96,192},{97,48... | collective-permute-start | bytes 393224 | tf_op jit(solution)/shard_map/ppermute | solution.py:396
  13.4 0.9 %copy-start.7 = (f32[2,4,4096]{2,1,0:T(4,128)S(1)}, f32[2,4,4096]{2,1,0:T(4,128)}, u32[]{:S(2)}) copy-start(f32[2,4,4096]{2,1,0:T(4,128)} %param.8) | copy-start | bytes 393220
  14.4 9.3 %collective-permute-start.1 = (f32[256,128]{1,0:T(8,128)S(1)}, f32[256,128]{1,0:T(8,128)S(1)}, u32[]{:S(2)}, u32[]{:S(2)}) collective-permute-start(f32[256,128]{1,0:T(8,128)S(1)} %get-tuple-element.14), channel_id=1, source_target_pairs={{0,352},{1,65},{32,384},{33,97},{64,416},{65,129},{96,448},{97,161... | collective-permute-start | bytes 393224 | tf_op jit(solution)/shard_map/ppermute | solution.py:396
  25.6 18.9 %copy-start.4 = (bf16[2,256,256]{2,1,0:T(8,128)(2,1)S(1)}, bf16[2,256,256]{2,1,0:T(8,128)(2,1)}, u32[]{:S(2)}) copy-start(bf16[2,256,256]{2,1,0:T(8,128)(2,1)} %constant.15.clone.table_x_back) | copy-start | bytes 786436
  25.6 18.9 %copy-start.5 = (bf16[2,256,256]{2,1,0:T(8,128)(2,1)S(1)}, bf16[2,256,256]{2,1,0:T(8,128)(2,1)}, u32[]{:S(2)}) copy-start(bf16[2,256,256]{2,1,0:T(8,128)(2,1)} %constant.14.clone.table_x) | copy-start | bytes 786436
  25.6 18.9 %copy-start.6 = (f32[64,256]{1,0:T(8,128)S(1)}, f32[64,256]{1,0:T(8,128)}, u32[]{:S(2)}) copy-start(f32[64,256]{1,0:T(8,128)} %kernel.1) | copy-start | bytes 196612
  46.2 15.5 %copy-start = (bf16[2,256,256]{2,1,0:T(8,128)(2,1)S(1)}, bf16[2,256,256]{2,1,0:T(8,128)(2,1)}, u32[]{:S(2)}) copy-start(bf16[2,256,256]{2,1,0:T(8,128)(2,1)} %constant.17.clone.table_z_back) | copy-start | bytes 786436
  46.2 15.5 %copy-start.1 = (bf16[2,256,256]{2,1,0:T(8,128)(2,1)S(1)}, bf16[2,256,256]{2,1,0:T(8,128)(2,1)}, u32[]{:S(2)}) copy-start(bf16[2,256,256]{2,1,0:T(8,128)(2,1)} %constant.16.clone.table_y_back) | copy-start | bytes 786436
  63.4 13.3 %collective-permute-start.2 = (f32[4,64,128]{2,1,0:T(8,128)S(1)}, f32[4,64,128]{2,1,0:T(8,128)S(1)}, u32[]{:S(2)}, u32[]{:S(2)}) collective-permute-start(f32[4,64,128]{2,1,0:T(8,128)S(1)} %get-tuple-element.19), channel_id=1, source_target_pairs={{0,33},{1,32},{32,65},{33,64},{64,97},{65,96},{96,129},{97,128},{1... | collective-permute-start | bytes 393224 | tf_op jit(solution)/shard_map/ppermute | solution.py:396
  76.7 10.1 %collective-permute-start.3 = (f32[4,64,128]{2,1,0:T(8,128)S(1)}, f32[4,64,128]{2,1,0:T(8,128)S(1)}, u32[]{:S(2)}, u32[]{:S(2)}) collective-permute-start(f32[4,64,128]{2,1,0:T(8,128)S(1)} %shard_map.86), channel_id=1, source_target_pairs={{0,416},{1,129},{32,448},{33,161},{64,480},{65,193},{96,0},{97,225... | collective-permute-start | bytes 393224 | tf_op jit(solution)/shard_map/ppermute | solution.py:396

commit v11 on v10

--- a/solution.py
+++ b/solution.py
@@ -60,12 +60,16 @@
 
 def times_table(value, table):
     high, low = halves(value)
-    return dot(high, table[0]) + dot(low, table[0]) + dot(high, table[1])
+    rows = value.shape[0]
+    both = dot(jnp.concatenate([high, low], axis=0), table[0])
+    return both[:rows] + both[rows:] + dot(high, table[1])
 
 
 def table_times(table, value):
     high, low = halves(value)
-    return dot(table[0], high) + dot(table[0], low) + dot(table[1], high)
+    rows = table.shape[1]
+    both = dot(jnp.concatenate([table[0], table[1]], axis=0), high)
+    return both[:rows] + both[rows:] + dot(table[0], low)
 
 
 def swap(value):

time: 92.4 us -> 92.2 us (level)
  no operation moved by 1% of the time
where the time goes in v11:
time: 92.2 us; the launch traced here: 90.9 us
  blocking collectives  41.9 us (45%)
  starting transfers between devices  34.6 us (38%)
  waiting for transfers between devices  7.48 us (8%)
  Pallas kernels  5.83 us (6%)
  local copies, waits for them, and re-layouts  0.95 us (1%)
    ppermute x4, starting transfers between devices, along_band(): return lax.ppermute(value, ('band', 'pool'), pairs)  34.6 us
    all_to_all x2, blocking collectives, exchange(): return lax.all_to_all(value, 'fft', split_axis=0, concat_axis=0, tiled=True)  34.3 us
    all_gather x3, blocking collectives, both_cores(): return lax.all_gather(value, 'pool', tiled=True)  7.62 us
    ppermute x4, waiting for transfers between devices, along_band(): return lax.ppermute(value, ('band', 'pool'), pairs)  7.48 us
  transfers between devices with their start and end apart: 4, of which 4 were waited for; matrix products, arithmetic and copies ran while one was open for 0% of the time, Pallas kernels for 0%

profile of v11, /device:TPU:1, one launch (start us, length us, event | category | flops | bytes accessed | tf_op | source)
XLA Modules:
  0.0 90.9 jit_solution(12692809699370376422)
XLA Ops:
  0.0 0.0 copy-start.2
  0.0 13.4 %collective-permute-start = (f32[256,128]{1,0:T(8,128)}, f32[256,128]{1,0:T(8,128)S(1)}, u32[]{:S(2)}, u32[]{:S(2)}) collective-permute-start(f32[256,128]{1,0:T(8,128)} %bitcast.10), channel_id=1, source_target_pairs={{0,96},{1,385},{32,128},{33,417},{64,160},{65,449},{96,192},{97,48... | collective-permute-start | bytes 393224 | tf_op jit(solution)/shard_map/ppermute | solution.py:400
  13.4 0.0 copy-start.7
  13.4 0.9 copy-done.7
  14.3 0.1 shard_map.82
  14.4 3.1 %collective-permute-start.1 = (f32[256,128]{1,0:T(8,128)S(1)}, f32[256,128]{1,0:T(8,128)S(1)}, u32[]{:S(2)}, u32[]{:S(2)}) collective-permute-start(f32[256,128]{1,0:T(8,128)S(1)} %get-tuple-element.14), channel_id=1, source_target_pairs={{0,352},{1,65},{32,384},{33,97},{64,416},{65,129},{96,448},{97,161... | collective-permute-start | bytes 393224 | tf_op jit(solution)/shard_map/ppermute | solution.py:400
  17.5 4.2 %collective-permute-done = f32[256,128]{1,0:T(8,128)S(1)} collective-permute-done((f32[256,128]{1,0:T(8,128)}, f32[256,128]{1,0:T(8,128)S(1)}, u32[]{:S(2)}, u32[]{:S(2)}) %collective-permute-start) | collective-permute-done | bytes 131104 | tf_op jit(solution)/shard_map/ppermute | solution.py:400
  21.7 2.0 %all_gather.9.shared = f32[512,128]{1,0:T(8,128)S(1)} all-gather(f32[256,128]{1,0:T(8,128)S(1)} %collective-permute-done), channel_id=1, replica_groups=mesh['band'=16,'fft'=16,'pool'=2] {'pool'}, dimensions={0}, use_global_device_ids=true | all-gather | bytes 393216 | tf_op jit(solution)/shard_map/all_gather | solution.py:404
  23.7 0.1 collective-permute-done.1.alone
  23.8 0.0 copy-done.2
  23.8 0.0 copy-done.3
  23.8 1.6 %shard_map.83 = (f32[16,136,128]{2,1,0:T(8,128)S(1)}, f32[12,64,128]{2,1,0:T(8,128)S(1)}) custom-call(f32[4,64,128]{2,1,0:T(8,128)S(1)} %get-tuple-element.13.own_blocks, f32[512,128]{1,0:T(8,128)S(1)} %all_gather.9.shared, f32[256,128]{1,0:T(8,128)S(1)} %collective-permute-done.1.alone, bf16[2,256,256]{2,1,0:T(8,128)(2,1)S(1)} %copy-done.3, ...), custom_call_target="tpu_custom_call" | custom-call | tf_op jit(solution)/shard_map/pallas_call | solution.py:343
  25.4 0.0 copy-start.4
  25.4 0.0 copy-start.5
  25.5 0.0 copy-start.6
  25.5 18.9 %all_to_all.10.spectra = f32[16,136,128]{2,1,0:T(8,128)S(1)} all-to-all(f32[16,136,128]{2,1,0:T(8,128)S(1)} %get-tuple-element.15), channel_id=1, replica_groups=mesh['band'=16,'fft'=16,'pool'=2] {'fft'}, dimensions={0} | all-to-all | bytes 2228224 | tf_op jit(solution)/shard_map/all_to_all | solution.py:408
  44.3 0.0 copy-done.4
  44.4 0.0 copy-done.5
  44.4 0.0 copy-done.6
  44.4 1.7 %shard_map.84 = f32[16,136,128]{2,1,0:T(8,128)S(1)} custom-call(f32[16,136,128]{2,1,0:T(8,128)S(1)} %all_to_all.10.spectra, f32[64,256]{1,0:T(8,128)S(1)} %copy-done.6, bf16[2,256,256]{2,1,0:T(8,128)(2,1)S(1)} %copy-done.5, bf16[2,256,256]{2,1,0:T(8,128)(2,1)S(1)} %copy-done.4), custom_call_target="tpu_custom_call" | custom-call | tf_op jit(solution)/shard_map/pallas_call | solution.py:353
  46.1 0.0 copy-start.1
  46.1 15.4 %all_to_all.11.returned = f32[16,136,128]{2,1,0:T(8,128)S(1)} all-to-all(f32[16,136,128]{2,1,0:T(8,128)S(1)} %shard_map.84), channel_id=1, replica_groups=mesh['band'=16,'fft'=16,'pool'=2] {'fft'}, dimensions={0} | all-to-all | bytes 2228224 | tf_op jit(solution)/shard_map/all_to_all | solution.py:408
  61.5 0.0 copy-done
  61.5 0.0 copy-done.1
  61.5 1.6 %shard_map.85 = (f32[4,64,128]{2,1,0:T(8,128)S(1)}, f32[4,64,128]{2,1,0:T(8,128)S(1)}, f32[4,64,128]{2,1,0:T(8,128)S(1)}, f32[4,64,128]{2,1,0:T(8,128)S(1)}) custom-call(f32[16,136,128]{2,1,0:T(8,128)S(1)} %all_to_all.11.returned, f32[4,64,128]{2,1,0:T(8,128)S(1)} %get-tuple-element.13.own_blocks, f32[12,64,128]{2,1,0:T(8,128)S(1)} %get-tuple-element.16.blocks, ...), custom_call_target="tpu_custom_call" | custom-call | tf_op jit(solution)/shard_map/pallas_call | solution.py:363
  63.2 10.6 %collective-permute-start.2 = (f32[4,64,128]{2,1,0:T(8,128)S(1)}, f32[4,64,128]{2,1,0:T(8,128)S(1)}, u32[]{:S(2)}, u32[]{:S(2)}) collective-permute-start(f32[4,64,128]{2,1,0:T(8,128)S(1)} %get-tuple-element.19), channel_id=1, source_target_pairs={{0,33},{1,32},{32,65},{33,64},{64,97},{65,96},{96,129},{97,128},{1... | collective-permute-start | bytes 393224 | tf_op jit(solution)/shard_map/ppermute | solution.py:400
  73.7 2.1 %all_gather.10.others = f32[8,64,128]{2,1,0:T(8,128)S(1)} all-gather(f32[4,64,128]{2,1,0:T(8,128)S(1)} %get-tuple-element.18), channel_id=1, replica_groups=mesh['band'=16,'fft'=16,'pool'=2] {'pool'}, dimensions={0}, use_global_device_ids=true | all-gather | bytes 393216 | tf_op jit(solution)/shard_map/all_gather | solution.py:404
  75.8 0.7 collective-permute-done.2.relayed
  76.5 7.5 %collective-permute-start.3 = (f32[4,64,128]{2,1,0:T(8,128)S(1)}, f32[4,64,128]{2,1,0:T(8,128)S(1)}, u32[]{:S(2)}, u32[]{:S(2)}) collective-permute-start(f32[4,64,128]{2,1,0:T(8,128)S(1)} %shard_map.86), channel_id=1, source_target_pairs={{0,416},{1,129},{32,448},{33,161},{64,480},{65,193},{96,0},{97,225... | collective-permute-start | bytes 393224 | tf_op jit(solution)/shard_map/ppermute | solution.py:400
  84.0 2.5 %collective-permute-done.3 = f32[4,64,128]{2,1,0:T(8,128)S(1)} collective-permute-done((f32[4,64,128]{2,1,0:T(8,128)S(1)}, f32[4,64,128]{2,1,0:T(8,128)S(1)}, u32[]{:S(2)}, u32[]{:S(2)}) %collective-permute-start.3) | collective-permute-done | bytes 131104 | tf_op jit(solution)/shard_map/ppermute | solution.py:400
  86.6 3.6 %all_gather.11.both = f32[8,64,128]{2,1,0:T(8,128)S(1)} all-gather(f32[4,64,128]{2,1,0:T(8,128)S(1)} %add.3), channel_id=1, replica_groups=mesh['band'=16,'fft'=16,'pool'=2] {'pool'}, dimensions={0}, use_global_device_ids=true | all-gather | bytes 393216 | tf_op jit(solution)/shard_map/all_gather | solution.py:404
  90.2 0.8 shard_map.87
  (4 shorter events, 0.0 us)
Async XLA Ops:
  0.0 23.8 %copy-start.2 = (bf16[2,256,256]{2,1,0:T(8,128)(2,1)S(1)}, bf16[2,256,256]{2,1,0:T(8,128)(2,1)}, u32[]{:S(2)}) copy-start(bf16[2,256,256]{2,1,0:T(8,128)(2,1)} %constant.13.clone.table_y) | copy-start | bytes 786436
  0.0 23.8 %copy-start.3 = (bf16[2,256,256]{2,1,0:T(8,128)(2,1)S(1)}, bf16[2,256,256]{2,1,0:T(8,128)(2,1)}, u32[]{:S(2)}) copy-start(bf16[2,256,256]{2,1,0:T(8,128)(2,1)} %constant.12.clone.table_z) | copy-start | bytes 786436
  0.0 21.7 %collective-permute-start = (f32[256,128]{1,0:T(8,128)}, f32[256,128]{1,0:T(8,128)S(1)}, u32[]{:S(2)}, u32[]{:S(2)}) collective-permute-start(f32[256,128]{1,0:T(8,128)} %bitcast.10), channel_id=1, source_target_pairs={{0,96},{1,385},{32,128},{33,417},{64,160},{65,449},{96,192},{97,48... | collective-permute-start | bytes 393224 | tf_op jit(solution)/shard_map/ppermute | solution.py:400
  13.4 0.9 %copy-start.7 = (f32[2,4,4096]{2,1,0:T(4,128)S(1)}, f32[2,4,4096]{2,1,0:T(4,128)}, u32[]{:S(2)}) copy-start(f32[2,4,4096]{2,1,0:T(4,128)} %param.8) | copy-start | bytes 393220
  14.4 9.3 %collective-permute-start.1 = (f32[256,128]{1,0:T(8,128)S(1)}, f32[256,128]{1,0:T(8,128)S(1)}, u32[]{:S(2)}, u32[]{:S(2)}) collective-permute-start(f32[256,128]{1,0:T(8,128)S(1)} %get-tuple-element.14), channel_id=1, source_target_pairs={{0,352},{1,65},{32,384},{33,97},{64,416},{65,129},{96,448},{97,161... | collective-permute-start | bytes 393224 | tf_op jit(solution)/shard_map/ppermute | solution.py:400
  25.4 18.9 %copy-start.4 = (bf16[2,256,256]{2,1,0:T(8,128)(2,1)S(1)}, bf16[2,256,256]{2,1,0:T(8,128)(2,1)}, u32[]{:S(2)}) copy-start(bf16[2,256,256]{2,1,0:T(8,128)(2,1)} %constant.15.clone.table_x_back) | copy-start | bytes 786436
  25.4 18.9 %copy-start.5 = (bf16[2,256,256]{2,1,0:T(8,128)(2,1)S(1)}, bf16[2,256,256]{2,1,0:T(8,128)(2,1)}, u32[]{:S(2)}) copy-start(bf16[2,256,256]{2,1,0:T(8,128)(2,1)} %constant.14.clone.table_x) | copy-start | bytes 786436
  25.5 18.9 %copy-start.6 = (f32[64,256]{1,0:T(8,128)S(1)}, f32[64,256]{1,0:T(8,128)}, u32[]{:S(2)}) copy-start(f32[64,256]{1,0:T(8,128)} %kernel.1) | copy-start | bytes 196612
  46.0 15.5 %copy-start = (bf16[2,256,256]{2,1,0:T(8,128)(2,1)S(1)}, bf16[2,256,256]{2,1,0:T(8,128)(2,1)}, u32[]{:S(2)}) copy-start(bf16[2,256,256]{2,1,0:T(8,128)(2,1)} %constant.17.clone.table_z_back) | copy-start | bytes 786436
  46.1 15.5 %copy-start.1 = (bf16[2,256,256]{2,1,0:T(8,128)(2,1)S(1)}, bf16[2,256,256]{2,1,0:T(8,128)(2,1)}, u32[]{:S(2)}) copy-start(bf16[2,256,256]{2,1,0:T(8,128)(2,1)} %constant.16.clone.table_y_back) | copy-start | bytes 786436
  63.2 13.3 %collective-permute-start.2 = (f32[4,64,128]{2,1,0:T(8,128)S(1)}, f32[4,64,128]{2,1,0:T(8,128)S(1)}, u32[]{:S(2)}, u32[]{:S(2)}) collective-permute-start(f32[4,64,128]{2,1,0:T(8,128)S(1)} %get-tuple-element.19), channel_id=1, source_target_pairs={{0,33},{1,32},{32,65},{33,64},{64,97},{65,96},{96,129},{97,128},{1... | collective-permute-start | bytes 393224 | tf_op jit(solution)/shard_map/ppermute | solution.py:400
  76.5 10.1 %collective-permute-start.3 = (f32[4,64,128]{2,1,0:T(8,128)S(1)}, f32[4,64,128]{2,1,0:T(8,128)S(1)}, u32[]{:S(2)}, u32[]{:S(2)}) collective-permute-start(f32[4,64,128]{2,1,0:T(8,128)S(1)} %shard_map.86), channel_id=1, source_target_pairs={{0,416},{1,129},{32,448},{33,161},{64,480},{65,193},{96,0},{97,225... | collective-permute-start | bytes 393224 | tf_op jit(solution)/shard_map/ppermute | solution.py:400
